TPU v7x, 512 devices: a whole 4x8x8 slice. The times are simulated.
512 devices in a mesh: dp: 32 (over z, y_lo, core), tensor: 16 (over y_hi, x).
Axes of the slice: x: 4, y: 8 (y_hi: 4, y_lo: 2; y = y_hi * 2 + y_lo), z: 8, core: 2. Of those that a mesh axis runs over, the one named last changes fastest.
Arguments:
- activations: bfloat16 [512, 8192], P('tensor', 'dp'), may hold values from -6 to 6
- gate_weight: bfloat16 [8192, 28672], P('dp', 'tensor'), may hold values from -0.0625 to 0.0625
- up_weight: bfloat16 [8192, 28672], P('dp', 'tensor'), may hold values from -0.0625 to 0.0625
- hidden_grad: bfloat16 [512, 28672], P('dp', 'tensor'), may hold values from -1.5 to 1.5
Outputs:
- hidden: bfloat16 [512, 28672], P('dp', 'tensor')
- input_grad: bfloat16 [512, 8192], P('tensor', 'dp')
- gate_grad: bfloat16 [8192, 28672], P('dp', 'tensor')
- up_grad: bfloat16 [8192, 28672], P('dp', 'tensor')
All inputs are finite; a program needn't handle non-finite values.
Results may differ from a plain program's by a relative error of at most 0.0049.
Values may be sent and summed in bfloat16 or wider, within the bound.
No kernel may reach another device: no remote copies, remote signals or barrier semaphores. Data moves between devices by JAX's collectives and lax.ppermute only.
A program may use at most 64 MiB of HBM per device.

v0:
```python
import jax
import jax.numpy as jnp
from jax import lax
from jax.sharding import PartitionSpec as P


def swiglu_back(gate_pre, up_pre, cotangent):
    sigmoid_gate = jax.nn.sigmoid(gate_pre)
    back_gate = (
        cotangent * up_pre * sigmoid_gate * (1.0 + gate_pre * (1.0 - sigmoid_gate))
    ).astype(jnp.bfloat16)
    back_up = (cotangent * gate_pre * sigmoid_gate).astype(jnp.bfloat16)
    return (back_gate, back_up)


def swiglu_forward(gate_pre, up_pre):
    return (gate_pre * jax.nn.sigmoid(gate_pre) * up_pre).astype(jnp.bfloat16)


def term_maker(tokens_all, weight):
    return jnp.dot(tokens_all, weight, preferred_element_type=jnp.float32)


def per_device(activations, gate_weight, up_weight, hidden_grad):
    tokens_all = lax.all_gather(activations, "tensor", axis=0, tiled=True)
    gate_pre = lax.psum_scatter(
        term_maker(tokens_all, gate_weight), "dp", scatter_dimension=0, tiled=True
    )
    up_pre = lax.psum_scatter(
        term_maker(tokens_all, up_weight), "dp", scatter_dimension=0, tiled=True
    )
    hidden = swiglu_forward(gate_pre, up_pre)
    back_gate, back_up = swiglu_back(gate_pre, up_pre, hidden_grad.astype(jnp.float32))
    gate_full, up_full = (
        lax.all_gather(back_gate, "dp", axis=0, tiled=True),
        lax.all_gather(back_up, "dp", axis=0, tiled=True),
    )
    input_grad = lax.psum_scatter(
        jnp.einsum("tf,df->td", gate_full, gate_weight, preferred_element_type=jnp.float32)
        + jnp.einsum("tf,df->td", up_full, up_weight, preferred_element_type=jnp.float32),
        "tensor",
        scatter_dimension=0,
        tiled=True,
    ).astype(jnp.bfloat16)
    gate_grad = jnp.einsum(
        "td,tf->df", tokens_all, gate_full, preferred_element_type=jnp.float32
    ).astype(jnp.bfloat16)
    up_grad = jnp.einsum(
        "td,tf->df", tokens_all, up_full, preferred_element_type=jnp.float32
    ).astype(jnp.bfloat16)
    return (hidden, input_grad, gate_grad, up_grad)


def solution(mesh):
    placed = (P("tensor", "dp"), P("dp", "tensor"), P("dp", "tensor"), P("dp", "tensor"))
    return jax.shard_map(
        per_device,
        mesh=mesh,
        in_specs=placed,
        out_specs=(P("dp", "tensor"), P("tensor", "dp"), P("dp", "tensor"), P("dp", "tensor")),
        check_vma=False,
    )
```

profile of v0, /device:TPU:1, one launch (start us, length us, event | category | flops | bytes accessed | tf_op | source)
XLA Modules:
  0.0 547.6 jit_solution(13080774918352903089)
XLA Ops:
  7.2 0.0 copy-start
  7.2 0.0 reduce-scatter.6.cloned.1.call-start
  7.2 40.3 %all_gather.9 = bf16[512,256]{1,0:T(8,128)(2,1)S(1)} all-gather(bf16[32,256]{1,0:T(8,128)(2,1)} %param.4), channel_id=1, replica_groups=mesh['dp'=32,'tensor'=16] {'tensor'}, dimensions={0}, use_global_device_ids=true | all-gather | bytes 278528 | tf_op jit(solution)/shard_map/all_gather | solution.py:25
  47.6 3.6 fusion.8
  51.2 0.0 reduce-scatter.6.cloned.1.call-update
  51.2 0.0 reduce-scatter.4.cloned.1.call-start
  51.3 0.0 copy-done
  51.3 2.5 fusion.7
  53.7 0.0 copy-start.3
  53.7 0.0 reduce-scatter.4.cloned.1.call-update
  53.8 0.0 all-gather.3.cloned.1.call-start
  53.8 125.0 %reduce-scatter.6.cloned.1.call-done = f32[16,1792]{1,0:T(8,128)} async-done(((f32[512,1792]{1,0:T(8,128)}), f32[16,1792]{1,0:T(8,128)}) %reduce-scatter.6.cloned.1.call-update) | async-done | bytes 114704 | tf_op jit(solution)/shard_map/reduce_scatter | solution.py:29
  178.8 126.6 %reduce-scatter.4.cloned.1.call-done = f32[16,1792]{1,0:T(8,128)} async-done(((f32[512,1792]{1,0:T(8,128)}), f32[16,1792]{1,0:T(8,128)}) %reduce-scatter.4.cloned.1.call-update) | async-done | bytes 114704 | tf_op jit(solution)/shard_map/reduce_scatter | solution.py:26
  305.4 0.0 copy-done.3
  305.4 1.7 fusion.4
  307.1 0.0 copy-start.1
  307.1 0.0 all-gather.3.cloned.1.call-update
  307.1 0.0 all-gather.5.cloned.1.call-start
  307.2 0.5 all-gather.5.cloned.1.call-update
  307.7 0.0 reduce-scatter.8.cloned.1.call-start
  307.7 70.2 %all-gather.3.cloned.1.call-done = bf16[512,1792]{1,0:T(8,128)(2,1)} async-done(((bf16[16,1792]{1,0:T(8,128)(2,1)}), bf16[512,1792]{1,0:T(8,128)(2,1)}) %all-gather.3.cloned.1.call-update) | async-done | bytes 1835024 | tf_op jit(solution)/shard_map/all_gather | solution.py:35
  377.9 2.2 fusion.9
  380.1 67.5 %all-gather.5.cloned.1.call-done = bf16[512,1792]{1,0:T(8,128)(2,1)} async-done(((bf16[16,1792]{1,0:T(8,128)(2,1)}), bf16[512,1792]{1,0:T(8,128)(2,1)}) %all-gather.5.cloned.1.call-update) | async-done | bytes 1835024 | tf_op jit(solution)/shard_map/all_gather | solution.py:36
  447.6 0.0 copy-done.1
  447.6 3.0 convolution_add_fusion
  450.5 0.0 reduce-scatter.8.cloned.1.call-update
  450.6 3.1 fusion
  453.7 0.0 copy-start.2
  453.7 2.3 copy.8
  456.0 0.0 copy-done.2
  456.0 1.6 fusion.1
  457.7 2.2 copy.9
  459.9 79.8 %reduce-scatter.8.cloned.1.call-done = f32[32,256]{1,0:T(8,128)} async-done(((f32[512,256]{1,0:T(8,128)}), f32[32,256]{1,0:T(8,128)}) %reduce-scatter.8.cloned.1.call-update) | async-done | bytes 32784 | tf_op jit(solution)/shard_map/reduce_scatter | solution.py:38
  539.7 1.4 convert_element_type.31
Async XLA Ops:
  7.2 44.1 %copy-start = (bf16[256,1792]{1,0:T(8,128)(2,1)S(1)}, bf16[256,1792]{1,0:T(8,128)(2,1)}, u32[]{:S(2)}) copy-start(bf16[256,1792]{1,0:T(8,128)(2,1)} %param.5) | copy-start | bytes 2752516
  7.2 171.6 %reduce-scatter.6.cloned.1.call-start = ((), (), s32[]{:S(2)}) async-start(), calls=%async_computation.4 | async-start | bytes 3784704 | tf_op jit(solution)/shard_map/reduce_scatter | solution.py:29
  51.2 254.2 %reduce-scatter.4.cloned.1.call-start = ((), (), s32[]{:S(2)}) async-start(), calls=%async_computation.3 | async-start | bytes 3784704 | tf_op jit(solution)/shard_map/reduce_scatter | solution.py:26
  53.7 251.7 %copy-start.3 = (bf16[16,1792]{1,0:T(8,128)(2,1)S(1)}, bf16[16,1792]{1,0:T(8,128)(2,1)}, u32[]{:S(2)}) copy-start(bf16[16,1792]{1,0:T(8,128)(2,1)} %param.7) | copy-start | bytes 172036
  53.8 324.1 %all-gather.3.cloned.1.call-start = ((), (), s32[]{:S(2)}) async-start(), calls=%async_computation.5 | async-start | bytes 1892352 | tf_op jit(solution)/shard_map/all_gather | solution.py:35
  307.1 140.5 %copy-start.1 = (bf16[256,1792]{1,0:T(8,128)(2,1)S(1)}, bf16[256,1792]{1,0:T(8,128)(2,1)}, u32[]{:S(2)}) copy-start(bf16[256,1792]{1,0:T(8,128)(2,1)} %param.6) | copy-start | bytes 2752516
  307.1 140.5 %all-gather.5.cloned.1.call-start = ((), (), s32[]{:S(2)}) async-start(), calls=%async_computation.6 | async-start | bytes 1892352 | tf_op jit(solution)/shard_map/all_gather | solution.py:36
  307.7 232.0 %reduce-scatter.8.cloned.1.call-start = ((), (), s32[]{:S(2)}) async-start(), calls=%async_computation.7 | async-start | bytes 557056 | tf_op jit(solution)/shard_map/reduce_scatter | solution.py:38
  453.7 2.3 copy-start.2
Sparse Core Ops, SparseCore 0:
  51.3 127.4 reduce-scatter.5
  181.9 123.4 reduce-scatter.3
  308.1 69.7 all-gather.2
  380.5 67.0 all-gather.4
  451.5 88.1 reduce-scatter.7
where the time goes:
time: 548 us
  waiting for transfers between devices  470 us (86%)
  blocking collectives  40.3 us (7%)
  matrix products  16 us (3%)
  between operations  13.8 us (3%)
    reduce_scatter x1, waiting for transfers between devices, per_device(): lax.psum_scatter(term_maker(tokens_all, gate_weight), 'dp', scatter_dimen...  127 us
    reduce_scatter x1, waiting for transfers between devices, per_device(): lax.psum_scatter(term_maker(tokens_all, up_weight), 'dp', scatter_dimensi...  125 us
    reduce_scatter x1, waiting for transfers between devices, per_device(): lax.psum_scatter(jnp.einsum('tf,df->td', gate_full, gate_weight, preferre...  79.8 us
    all_gather x1, waiting for transfers between devices, per_device(): lax.all_gather(back_gate, 'dp', axis=0, tiled=True)  70.2 us
    all_gather x1, waiting for transfers between devices, per_device(): lax.all_gather(back_up, 'dp', axis=0, tiled=True)  67.5 us
    all_gather x1, blocking collectives, per_device(): tokens_all = lax.all_gather(activations, 'tensor', axis=0, tiled=True)  40.3 us
  transfers between devices with their start and end apart: 5, of which 5 were waited for; matrix products, arithmetic and copies ran while one was open for 3% of the time, Pallas kernels for 0%

commit v1 on v0

v1 whole, which is shorter than its diff:
```python
import jax
import jax.numpy as jnp
from jax import lax
from jax.sharding import PartitionSpec as P

F32, BF16 = jnp.float32, jnp.bfloat16

Y_SWAP = [(i, i ^ 2) for i in range(32)]
CORE_SWAP = [(i, i ^ 1) for i in range(32)]
Z_GROUPS = [[z * 4 + r for z in range(8)] for r in range(4)]


def dot(a, b):
    return jnp.dot(a, b, preferred_element_type=F32)


def dot_nt(a, b):
    return lax.dot_general(a, b, (((1,), (1,)), ((), ())), preferred_element_type=F32)


def dot_tn(a, b):
    return lax.dot_general(a, b, (((0,), (0,)), ((), ())), preferred_element_type=F32)


def swap_y(x):
    return lax.ppermute(x, "dp", Y_SWAP)


def swap_core(x):
    return lax.ppermute(x, "dp", CORE_SWAP)


def ordered(first, mine, other, axis):
    return jnp.where(
        first,
        jnp.concatenate([mine, other], axis),
        jnp.concatenate([other, mine], axis),
    )


def per_device(activations, gate_weight, up_weight, hidden_grad):
    index = lax.axis_index("dp")
    y0 = (index // 2) % 2 == 0
    c0 = index % 2 == 0
    tensor = lax.axis_size("tensor")
    rows, width = activations.shape
    half = gate_weight.shape[1] // 2
    block = hidden_grad.shape[0]

    def pick(cond, a, b):
        return jnp.where(cond, a, b)

    lo = jnp.concatenate([gate_weight[:, :half], up_weight[:, :half]], 1)
    hi = jnp.concatenate([gate_weight[:, half:], up_weight[:, half:]], 1)
    weight_own = pick(y0, lo, hi)
    weight_peer = swap_y(pick(y0, hi, lo))

    tokens = lax.all_to_all(
        jnp.broadcast_to(activations[None], (tensor, rows, width)), "tensor", 0, 0
    )
    tokens = tokens.reshape(-1, 2, block, width)
    even = tokens[:, 0].reshape(-1, width)
    odd = tokens[:, 1].reshape(-1, width)
    keep_own, send_own = pick(c0, even, odd), pick(c0, odd, even)
    peer = swap_y(jnp.concatenate([keep_own, send_own], 0))
    count = keep_own.shape[0]
    keep_peer, send_peer = peer[:count], peer[count:]

    sent = (dot(send_own, weight_own) + dot(send_peer, weight_peer)).astype(BF16)
    got = swap_core(sent)
    kept = dot(keep_own, weight_own) + dot(keep_peer, weight_peer)
    part = (kept + got.astype(F32)).astype(BF16)
    part = part.reshape(8, 2 * block, 2 * half)
    part = lax.all_to_all(part, "dp", 0, 0, axis_index_groups=Z_GROUPS)
    pre = jnp.sum(part.astype(F32), 0)
    gate_pre, up_pre = pre[:, :half], pre[:, half:]

    grad_lo, grad_hi = hidden_grad[:, :half], hidden_grad[:, half:]
    grad = ordered(
        y0, pick(y0, grad_lo, grad_hi), swap_y(pick(y0, grad_hi, grad_lo)), 0
    ).astype(F32)

    sig = jax.nn.sigmoid(gate_pre)
    hidden = (gate_pre * sig * up_pre).astype(BF16)
    gate_back = (grad * up_pre * sig * (1.0 + gate_pre * (1.0 - sig))).astype(BF16)
    up_back = (grad * gate_pre * sig).astype(BF16)
    back = jnp.concatenate([gate_back, up_back], 1)

    back_own = lax.all_gather(back, "dp", axis=0, tiled=True, axis_index_groups=Z_GROUPS)
    back_other = swap_core(back_own)

    h_lo, h_hi = hidden[:block], hidden[block:]
    hidden = ordered(y0, pick(y0, h_lo, h_hi), swap_y(pick(y0, h_hi, h_lo)), 1)

    def input_part(weight):
        own, other = dot_nt(back_own, weight), dot_nt(back_other, weight)
        shape = (-1, 1, block, width)
        return ordered(c0, own.reshape(shape), other.reshape(shape), 1)

    peer_part = swap_y(input_part(weight_peer).astype(BF16))
    total = (input_part(weight_own) + peer_part.astype(F32)).astype(BF16)
    total = lax.all_to_all(total.reshape(tensor, rows, width), "tensor", 0, 0)
    input_grad = jnp.sum(total.astype(F32), 0).astype(BF16)

    def weight_part(keep, send):
        return (dot_tn(keep, back_own) + dot_tn(send, back_other)).astype(BF16)

    from_peer = swap_y(weight_part(keep_peer, send_peer))
    mine = weight_part(keep_own, send_own)
    gate_grad = ordered(y0, mine[:, :half], from_peer[:, :half], 1)
    up_grad = ordered(y0, mine[:, half:], from_peer[:, half:], 1)
    return (hidden, input_grad, gate_grad, up_grad)


def solution(mesh):
    placed = (P("tensor", "dp"), P("dp", "tensor"), P("dp", "tensor"), P("dp", "tensor"))
    return jax.shard_map(
        per_device,
        mesh=mesh,
        in_specs=placed,
        out_specs=(P("dp", "tensor"), P("tensor", "dp"), P("dp", "tensor"), P("dp", "tensor")),
        check_vma=False,
    )
```

time: 548 us -> 167 us (0.30)
  waiting for transfers between devices: 470 us -> 71 us
  starting transfers between devices: 0.2 us -> 54.5 us
  blocking collectives: 40.3 us -> 20.7 us
  between operations: 13.8 us -> 0.93 us
  matrix products: 16 us -> 9.8 us
    reduce_scatter x3 -> x0, waiting for transfers between devices: 331 us -> none  [the longest x1 127 us: per_device(): lax.psum_scatter(term_maker(tokens_all, gate_weight), 'dp', scatter_dimen...]
    all_gather x2 -> x0, waiting for transfers between devices: 138 us -> none  [the longest x1 70.2 us: per_device(): lax.all_gather(back_gate, 'dp', axis=0, tiled=True)]
    all_to_all x0 -> x3, waiting for transfers between devices: none -> 48.1 us  [the longest x1 23.7 us: per_device(): part = lax.all_to_all(part, 'dp', 0, 0, axis_index_groups=Z_GROUPS)]
    all_to_all x0 -> x3, starting transfers between devices: none -> 28.3 us  [the longest x1 10.2 us: per_device(): lax.all_to_all(jnp.broadcast_to(activations[None], (tensor, rows, width))...]
    ppermute x0 -> x8, starting transfers between devices: none -> 26.2 us  [the longest x6 15 us: swap_y(): return lax.ppermute(x, 'dp', Y_SWAP)]
    ppermute x0 -> x8, waiting for transfers between devices: none -> 22.9 us  [the longest x6 21.2 us: swap_y(): return lax.ppermute(x, 'dp', Y_SWAP)]
    all_gather x1, blocking collectives: 40.3 us -> 20.7 us  [per_device(): lax.all_gather(back, 'dp', axis=0, tiled=True, axis_index_groups=Z_GROUPS)]
    dot_general x6 -> x12, matrix products: 16 us -> 9.8 us  [the longest x4 5.47 us: dot_tn(): lax.dot_general(a, b, (((0,), (0,)), ((), ())), preferred_element_type=F32)]
  transfers between devices with their start and end apart: 5 -> 11, of which waited for: 5 -> 6; matrix products, arithmetic and copies ran while one was open for 3% -> 7% of each run, Pallas kernels for 0% -> 0%
where the time goes in v1:
time: 167 us; the launch traced here: 166 us
  waiting for transfers between devices  71 us (43%)
  starting transfers between devices  54.5 us (33%)
  blocking collectives  20.7 us (12%)
  matrix products  9.8 us (6%)
  other arithmetic  5.28 us (3%)
  local copies, waits for them, and re-layouts  4.15 us (2%)
    all_to_all x1, waiting for transfers between devices, per_device(): part = lax.all_to_all(part, 'dp', 0, 0, axis_index_groups=Z_GROUPS)  23.7 us
    ppermute x6, waiting for transfers between devices, swap_y(): return lax.ppermute(x, 'dp', Y_SWAP)  21.2 us
    all_gather x1, blocking collectives, per_device(): lax.all_gather(back, 'dp', axis=0, tiled=True, axis_index_groups=Z_GROUPS)  20.7 us
    all_to_all x1, waiting for transfers between devices, per_device(): total = lax.all_to_all(total.reshape(tensor, rows, width), 'tensor', 0, 0)  19.1 us
    ppermute x6, starting transfers between devices, swap_y(): return lax.ppermute(x, 'dp', Y_SWAP)  15 us
    ppermute x2, starting transfers between devices, swap_core(): return lax.ppermute(x, 'dp', CORE_SWAP)  11.2 us
    all_to_all x1, starting transfers between devices, per_device(): lax.all_to_all(jnp.broadcast_to(activations[None], (tensor, rows, width))...  10.2 us
    all_to_all x1, starting transfers between devices, per_device(): part = lax.all_to_all(part, 'dp', 0, 0, axis_index_groups=Z_GROUPS)  10.2 us
  transfers between devices with their start and end apart: 11, of which 6 were waited for; matrix products, arithmetic and copies ran while one was open for 7% of the time, Pallas kernels for 0%

profile of v1, /device:TPU:1, one launch (start us, length us, event | category | flops | bytes accessed | tf_op | source)
XLA Modules:
  0.0 166.3 jit_solution(11826271873727042457)
XLA Ops:
  0.6 0.0 copy-start
  0.6 1.5 broadcast_in_dim.2
  2.2 10.2 %all-to-all-start = ((bf16[16,32,256]{2,1,0:T(8,128)(2,1)}), bf16[16,32,256]{2,1,0:T(8,128)(2,1)S(1)}, u32[]{:S(2)}, u32[]{:S(2)}) async-start(bf16[16,32,256]{2,1,0:T(8,128)(2,1)} %broadcast_in_dim.2), calls=%async_computation | async-start | bytes 524288 | tf_op jit(solution)/shard_map/all_to_all | solution.py:58
  12.4 1.2 fusion.20
  13.7 0.0 copy-done
  13.7 0.1 fusion.21
  13.7 1.2 broadcast_select_fusion
  15.0 2.3 %collective-permute-start.1 = (bf16[256,1792]{1,0:T(8,128)(2,1)}, bf16[256,1792]{1,0:T(8,128)(2,1)S(1)}, u32[]{:S(2)}, u32[]{:S(2)}) collective-permute-start(bf16[256,1792]{1,0:T(8,128)(2,1)} %get-tuple-element.4), channel_id=1, source_target_pairs={{0,32},{16,48},{32,0},{48,16},{64,96},{80,112},{96,64},{112,80},{1... | collective-permute-start | bytes 2752520 | tf_op jit(solution)/shard_map/ppermute | solution.py:26
  17.3 5.2 %all-to-all-done = bf16[16,32,256]{2,1,0:T(8,128)(2,1)S(1)} async-done(((bf16[16,32,256]{2,1,0:T(8,128)(2,1)}), bf16[16,32,256]{2,1,0:T(8,128)(2,1)S(1)}, u32[]{:S(2)}, u32[]{:S(2)}) %all-to-all-start) | async-done | bytes 262176 | tf_op jit(solution)/shard_map/all_to_all | solution.py:58
  22.6 2.2 %collective-permute-start = (bf16[512,256]{1,0:T(8,128)(2,1)S(1)}, bf16[512,256]{1,0:T(8,128)(2,1)S(1)}, u32[]{:S(2)}, u32[]{:S(2)}) collective-permute-start(bf16[512,256]{1,0:T(8,128)(2,1)S(1)} %pad_maximum_fusion.2), channel_id=1, source_target_pairs={{0,32},{16,48},{32,0},{48,16},{64,96},{80,112},{96,64},{112,80},{1... | collective-permute-start | bytes 786440 | tf_op jit(solution)/shard_map/ppermute | solution.py:26
  24.7 0.4 fusion.23
  25.1 20.1 %collective-permute-done = bf16[512,256]{1,0:T(8,128)(2,1)S(1)} collective-permute-done((bf16[512,256]{1,0:T(8,128)(2,1)S(1)}, bf16[512,256]{1,0:T(8,128)(2,1)S(1)}, u32[]{:S(2)}, u32[]{:S(2)}) %collective-permute-start) | collective-permute-done | bytes 262176 | tf_op jit(solution)/shard_map/ppermute | solution.py:26
  45.2 0.0 collective-permute-done.1
  45.2 0.4 fusion.2
  45.6 3.0 %collective-permute-start.2 = (bf16[256,1792]{1,0:T(8,128)(2,1)S(1)}, bf16[256,1792]{1,0:T(8,128)(2,1)S(1)}, u32[]{:S(2)}, u32[]{:S(2)}) collective-permute-start(bf16[256,1792]{1,0:T(8,128)(2,1)S(1)} %fusion.2), channel_id=1, source_target_pairs={{0,16},{16,0},{32,48},{48,32},{64,80},{80,64},{96,112},{112,96},{1... | collective-permute-start | bytes 2752520 | tf_op jit(solution)/shard_map/ppermute | solution.py:30
  48.6 0.4 fusion.22
  49.0 1.7 collective-permute-done.2
  50.7 1.4 fusion.1
  52.1 0.0 copy-start.1
  52.1 10.2 %all-to-all-start.1 = ((bf16[8,32,1792]{2,1,0:T(8,128)(2,1)}), bf16[8,32,1792]{2,1,0:T(8,128)(2,1)S(1)}, u32[]{:S(2)}, u32[]{:S(2)}) async-start(bf16[8,32,1792]{2,1,0:T(8,128)(2,1)} %bitcast.3), calls=%async_computation.1 | async-start | bytes 1835008 | tf_op jit(solution)/shard_map/all_to_all | solution.py:74
  62.2 0.0 copy-done.1
  62.3 2.6 %collective-permute-start.4 = (bf16[16,896]{1,0:T(8,128)(2,1)S(1)}, bf16[16,896]{1,0:T(8,128)(2,1)S(1)}, u32[]{:S(2)}, u32[]{:S(2)}) collective-permute-start(bf16[16,896]{1,0:T(8,128)(2,1)S(1)} %get-tuple-element.19), channel_id=1, source_target_pairs={{0,32},{16,48},{32,0},{48,16},{64,96},{80,112},{96,64},{112,80},{1... | collective-permute-start | bytes 86024 | tf_op jit(solution)/shard_map/ppermute | solution.py:26
  64.9 23.7 %all-to-all-done.1 = bf16[8,32,1792]{2,1,0:T(8,128)(2,1)S(1)} async-done(((bf16[8,32,1792]{2,1,0:T(8,128)(2,1)}), bf16[8,32,1792]{2,1,0:T(8,128)(2,1)S(1)}, u32[]{:S(2)}, u32[]{:S(2)}) %all-to-all-start.1) | async-done | bytes 917536 | tf_op jit(solution)/shard_map/all_to_all | solution.py:74
  88.6 0.1 convert_reduce_fusion
  88.7 0.0 collective-permute-done.4
  88.8 0.1 fusion.15
  88.9 20.7 %all_gather.3 = bf16[256,1792]{1,0:T(8,128)(2,1)S(1)} all-gather(bf16[32,1792]{1,0:T(8,128)(2,1)S(1)} %pad_maximum_fusion.3), channel_id=1, replica_groups={{0,64,128,192,256,320,384,448},{16,80,144,208,272,336,400,464},{32,96,1..., dimensions={0}, use_global_device_ids=true | all-gather | bytes 1032192 | tf_op jit(solution)/shard_map/all_gather | solution.py:89
  109.6 0.4 fusion.24
  110.0 8.3 %collective-permute-start.5 = (bf16[256,1792]{1,0:T(8,128)(2,1)S(1)}, bf16[256,1792]{1,0:T(8,128)(2,1)S(1)}, u32[]{:S(2)}, u32[]{:S(2)}) collective-permute-start(bf16[256,1792]{1,0:T(8,128)(2,1)S(1)} %all_gather.3), channel_id=1, source_target_pairs={{0,16},{16,0},{32,48},{48,32},{64,80},{80,64},{96,112},{112,96},{1... | collective-permute-start | bytes 2752520 | tf_op jit(solution)/shard_map/ppermute | solution.py:30
  118.3 2.6 %collective-permute-start.3 = (bf16[16,896]{1,0:T(8,128)(2,1)S(1)}, bf16[16,896]{1,0:T(8,128)(2,1)S(1)}, u32[]{:S(2)}, u32[]{:S(2)}) collective-permute-start(bf16[16,896]{1,0:T(8,128)(2,1)S(1)} %get-tuple-element.22), channel_id=1, source_target_pairs={{0,32},{16,48},{32,0},{48,16},{64,96},{80,112},{96,64},{112,80},{1... | collective-permute-start | bytes 86024 | tf_op jit(solution)/shard_map/ppermute | solution.py:26
  120.9 1.7 %fusion.28 = f32[256,1792]{1,0:T(8,128)} fusion(bf16[256,256]{1,0:T(8,128)(2,1)S(1)} %bitcast.43, bf16[256,1792]{1,0:T(8,128)(2,1)S(1)} %all_gather.3), kind=kOutput, calls=%fused_computation.55 | convolution fusion | flops 234881024 | bytes 2883584 | tf_op jit(solution)/shard_map/dot_general | solution.py:22
  122.6 0.4 fusion.26
  123.1 0.0 collective-permute-done.3
  123.1 0.6 maximum_select_fusion.4
  123.7 0.0 collective-permute-done.5
  123.7 0.4 fusion.27
  124.2 2.7 %collective-permute-start.6 = (bf16[16,2,16,256]{3,2,1,0:T(8,128)(2,1)S(1)}, bf16[16,2,16,256]{3,2,1,0:T(8,128)(2,1)S(1)}, u32[]{:S(2)}, u32[]{:S(2)}) collective-permute-start(bf16[16,2,16,256]{3,2,1,0:T(8,128)(2,1)S(1)} %fusion.7), channel_id=1, source_target_pairs={{0,32},{16,48},{32,0},{48,16},{64,96},{80,112},{96,64},{112,80},{1... | collective-permute-start | bytes 786440 | tf_op jit(solution)/shard_map/ppermute | solution.py:26
  126.9 0.4 fusion.8
  127.3 1.4 fusion.4
  128.7 2.6 %collective-permute-start.7 = (bf16[256,1792]{1,0:T(8,128)(2,1)}, bf16[256,1792]{1,0:T(8,128)(2,1)}, u32[]{:S(2)}, u32[]{:S(2)}) collective-permute-start(bf16[256,1792]{1,0:T(8,128)(2,1)} %fusion.4), channel_id=1, source_target_pairs={{0,32},{16,48},{32,0},{48,16},{64,96},{80,112},{96,64},{112,80},{1... | collective-permute-start | bytes 2752520 | tf_op jit(solution)/shard_map/ppermute | solution.py:26
  131.3 0.4 fusion.25
  131.7 1.1 collective-permute-done.6
  132.9 0.8 fusion.6
  133.7 7.9 %all-to-all-start.2 = ((bf16[16,32,256]{2,1,0:T(8,128)(2,1)}), bf16[16,32,256]{2,1,0:T(8,128)(2,1)S(1)}, u32[]{:S(2)}, u32[]{:S(2)}) async-start(bf16[16,32,256]{2,1,0:T(8,128)(2,1)} %bitcast.16), calls=%async_computation.2 | async-start | bytes 524288 | tf_op jit(solution)/shard_map/all_to_all | solution.py:102
  141.6 1.9 %fusion.3 = bf16[256,1792]{1,0:T(8,128)(2,1)S(1)} fusion(f32[256,1792]{1,0:T(8,128)} %fusion.28, bf16[256,256]{1,0:T(8,128)(2,1)S(1)} %bitcast.46, bf16[256,1792]{1,0:T(8,128)(2,1)S(1)} %collective-permute-done.5), kind=kOutput, calls=%fused_computation.7 | convolution fusion | flops 235798528 | bytes 3801088 | tf_op jit(solution)/shard_map/dot_general | solution.py:22
  143.5 0.1 fusion.18
  143.6 19.1 %all-to-all-done.2 = bf16[16,32,256]{2,1,0:T(8,128)(2,1)S(1)} async-done(((bf16[16,32,256]{2,1,0:T(8,128)(2,1)}), bf16[16,32,256]{2,1,0:T(8,128)(2,1)S(1)}, u32[]{:S(2)}, u32[]{:S(2)}) %all-to-all-start.2) | async-done | bytes 262176 | tf_op jit(solution)/shard_map/all_to_all | solution.py:102
  162.7 0.6 reduce_sum.22
  163.4 0.0 collective-permute-done.7
  163.4 1.2 fusion.19
  164.6 1.6 maximum_select_fusion
  (6 shorter events, 0.1 us)
Async XLA Ops:
  0.6 13.0 %copy-start = (bf16[256,1792]{1,0:T(8,128)(2,1)S(1)}, bf16[256,1792]{1,0:T(8,128)(2,1)}, u32[]{:S(2)}) copy-start(bf16[256,1792]{1,0:T(8,128)(2,1)} %param.6) | copy-start | bytes 2752516
  2.2 20.3 %all-to-all-start = ((bf16[16,32,256]{2,1,0:T(8,128)(2,1)}), bf16[16,32,256]{2,1,0:T(8,128)(2,1)S(1)}, u32[]{:S(2)}, u32[]{:S(2)}) async-start(bf16[16,32,256]{2,1,0:T(8,128)(2,1)} %broadcast_in_dim.2), calls=%async_computation | async-start | bytes 524288 | tf_op jit(solution)/shard_map/all_to_all | solution.py:58
  15.0 30.2 %collective-permute-start.1 = (bf16[256,1792]{1,0:T(8,128)(2,1)}, bf16[256,1792]{1,0:T(8,128)(2,1)S(1)}, u32[]{:S(2)}, u32[]{:S(2)}) collective-permute-start(bf16[256,1792]{1,0:T(8,128)(2,1)} %get-tuple-element.4), channel_id=1, source_target_pairs={{0,32},{16,48},{32,0},{48,16},{64,96},{80,112},{96,64},{112,80},{1... | collective-permute-start | bytes 2752520 | tf_op jit(solution)/shard_map/ppermute | solution.py:26
  22.6 22.7 %collective-permute-start = (bf16[512,256]{1,0:T(8,128)(2,1)S(1)}, bf16[512,256]{1,0:T(8,128)(2,1)S(1)}, u32[]{:S(2)}, u32[]{:S(2)}) collective-permute-start(bf16[512,256]{1,0:T(8,128)(2,1)S(1)} %pad_maximum_fusion.2), channel_id=1, source_target_pairs={{0,32},{16,48},{32,0},{48,16},{64,96},{80,112},{96,64},{112,80},{1... | collective-permute-start | bytes 786440 | tf_op jit(solution)/shard_map/ppermute | solution.py:26
  45.6 5.1 %collective-permute-start.2 = (bf16[256,1792]{1,0:T(8,128)(2,1)S(1)}, bf16[256,1792]{1,0:T(8,128)(2,1)S(1)}, u32[]{:S(2)}, u32[]{:S(2)}) collective-permute-start(bf16[256,1792]{1,0:T(8,128)(2,1)S(1)} %fusion.2), channel_id=1, source_target_pairs={{0,16},{16,0},{32,48},{48,32},{64,80},{80,64},{96,112},{112,96},{1... | collective-permute-start | bytes 2752520 | tf_op jit(solution)/shard_map/ppermute | solution.py:30
  52.1 10.2 %copy-start.1 = (bf16[16,1792]{1,0:T(8,128)(2,1)S(1)}, bf16[16,1792]{1,0:T(8,128)(2,1)}, u32[]{:S(2)}) copy-start(bf16[16,1792]{1,0:T(8,128)(2,1)} %param.7) | copy-start | bytes 172036
  52.1 36.6 %all-to-all-start.1 = ((bf16[8,32,1792]{2,1,0:T(8,128)(2,1)}), bf16[8,32,1792]{2,1,0:T(8,128)(2,1)S(1)}, u32[]{:S(2)}, u32[]{:S(2)}) async-start(bf16[8,32,1792]{2,1,0:T(8,128)(2,1)} %bitcast.3), calls=%async_computation.1 | async-start | bytes 1835008 | tf_op jit(solution)/shard_map/all_to_all | solution.py:74
  62.3 26.5 %collective-permute-start.4 = (bf16[16,896]{1,0:T(8,128)(2,1)S(1)}, bf16[16,896]{1,0:T(8,128)(2,1)S(1)}, u32[]{:S(2)}, u32[]{:S(2)}) collective-permute-start(bf16[16,896]{1,0:T(8,128)(2,1)S(1)} %get-tuple-element.19), channel_id=1, source_target_pairs={{0,32},{16,48},{32,0},{48,16},{64,96},{80,112},{96,64},{112,80},{1... | collective-permute-start | bytes 86024 | tf_op jit(solution)/shard_map/ppermute | solution.py:26
  110.0 13.7 %collective-permute-start.5 = (bf16[256,1792]{1,0:T(8,128)(2,1)S(1)}, bf16[256,1792]{1,0:T(8,128)(2,1)S(1)}, u32[]{:S(2)}, u32[]{:S(2)}) collective-permute-start(bf16[256,1792]{1,0:T(8,128)(2,1)S(1)} %all_gather.3), channel_id=1, source_target_pairs={{0,16},{16,0},{32,48},{48,32},{64,80},{80,64},{96,112},{112,96},{1... | collective-permute-start | bytes 2752520 | tf_op jit(solution)/shard_map/ppermute | solution.py:30
  118.3 4.8 %collective-permute-start.3 = (bf16[16,896]{1,0:T(8,128)(2,1)S(1)}, bf16[16,896]{1,0:T(8,128)(2,1)S(1)}, u32[]{:S(2)}, u32[]{:S(2)}) collective-permute-start(bf16[16,896]{1,0:T(8,128)(2,1)S(1)} %get-tuple-element.22), channel_id=1, source_target_pairs={{0,32},{16,48},{32,0},{48,16},{64,96},{80,112},{96,64},{112,80},{1... | collective-permute-start | bytes 86024 | tf_op jit(solution)/shard_map/ppermute | solution.py:26
  124.2 8.7 %collective-permute-start.6 = (bf16[16,2,16,256]{3,2,1,0:T(8,128)(2,1)S(1)}, bf16[16,2,16,256]{3,2,1,0:T(8,128)(2,1)S(1)}, u32[]{:S(2)}, u32[]{:S(2)}) collective-permute-start(bf16[16,2,16,256]{3,2,1,0:T(8,128)(2,1)S(1)} %fusion.7), channel_id=1, source_target_pairs={{0,32},{16,48},{32,0},{48,16},{64,96},{80,112},{96,64},{112,80},{1... | collective-permute-start | bytes 786440 | tf_op jit(solution)/shard_map/ppermute | solution.py:26
  128.7 34.7 %collective-permute-start.7 = (bf16[256,1792]{1,0:T(8,128)(2,1)}, bf16[256,1792]{1,0:T(8,128)(2,1)}, u32[]{:S(2)}, u32[]{:S(2)}) collective-permute-start(bf16[256,1792]{1,0:T(8,128)(2,1)} %fusion.4), channel_id=1, source_target_pairs={{0,32},{16,48},{32,0},{48,16},{64,96},{80,112},{96,64},{112,80},{1... | collective-permute-start | bytes 2752520 | tf_op jit(solution)/shard_map/ppermute | solution.py:26
  133.7 29.1 %all-to-all-start.2 = ((bf16[16,32,256]{2,1,0:T(8,128)(2,1)}), bf16[16,32,256]{2,1,0:T(8,128)(2,1)S(1)}, u32[]{:S(2)}, u32[]{:S(2)}) async-start(bf16[16,32,256]{2,1,0:T(8,128)(2,1)} %bitcast.16), calls=%async_computation.2 | async-start | bytes 524288 | tf_op jit(solution)/shard_map/all_to_all | solution.py:102

commit v2 on v0

v2 whole, which is shorter than its diff:
```python
import jax
import jax.numpy as jnp
from jax import lax
from jax.experimental import pallas as pl
from jax.experimental.pallas import tpu as pltpu
from jax.sharding import PartitionSpec as P

F32, BF16 = jnp.float32, jnp.bfloat16

CORE_SWAP = [(i, i ^ 1) for i in range(32)]
Y_SWAP = [(i, i ^ 2) for i in range(32)]
QUAD_SWAP = [None, Y_SWAP, [(i, i ^ 4) for i in range(32)], [(i, i ^ 6) for i in range(32)]]
Z_GROUPS = [[z * 4 + r for z in range(8)] for r in range(4)]
X_GROUPS = [[4 * h + x for x in range(4)] for h in range(4)]
QUAD_YHI_GROUPS = [
    [((2 * q + b) * 4 + 2 * y + c) * 16 + 4 * h + x for b in range(2) for y in range(2) for h in range(4)]
    for q in range(4) for c in range(2) for x in range(4)
]

PARAMS = pltpu.CompilerParams(vmem_limit_bytes=32 * 1024 * 1024)
VMEM = pl.BlockSpec(memory_space=pltpu.VMEM)
SMEM = pl.BlockSpec(memory_space=pltpu.SMEM)


def struct(shape, dtype=BF16):
    return jax.ShapeDtypeStruct(shape, dtype)


def call(kernel, n_in, out_shape, flops):
    many = isinstance(out_shape, list)
    return pl.pallas_call(
        kernel,
        out_shape=out_shape,
        in_specs=[SMEM] + [VMEM] * n_in,
        out_specs=[VMEM] * len(out_shape) if many else VMEM,
        compiler_params=PARAMS,
        cost_estimate=pl.CostEstimate(flops=flops, bytes_accessed=4 << 20, transcendentals=0),
    )


def spans(n, step=256):
    return [slice(i, min(i + step, n)) for i in range(0, n, step)]


def arrange_and_send(place, raw, w0, w1, w2, w3, tokens, sent):
    width = raw.shape[-1]
    half, block = tokens.shape[0] // 2, raw.shape[-2]
    for part in range(2):
        core = place[1] ^ part
        for k in range(4):
            member = place[0] ^ k
            for h in range(4):
                for x in range(4):
                    row = part * half + (h * 4 + x) * block
                    tokens[row : row + block, k * width : (k + 1) * width] = raw[x, member, h, core]
    for s in spans(sent.shape[1]):
        total = None
        for k, w in enumerate((w0, w1, w2, w3)):
            term = jnp.dot(
                tokens[half:, k * width : (k + 1) * width], w[:, s], preferred_element_type=F32
            )
            total = term if total is None else total + term
        sent[:, s] = total


def keep_sums(place, tokens, w0, w1, w2, w3, got, out):
    width = w0.shape[0]
    half = out.shape[0]
    for s in spans(out.shape[1]):
        total = got[:, s]
        for k, w in enumerate((w0, w1, w2, w3)):
            total = total + jnp.dot(
                tokens[:half, k * width : (k + 1) * width], w[:, s], preferred_element_type=F32
            )
        out[:, s] = total.astype(BF16)


def input_parts(place, own, other, w0, w1, w2, w3, out):
    block = out.shape[-2]
    for part, back in enumerate((own, other)):
        core = place[1] ^ part
        for k, w in enumerate((w0, w1, w2, w3)):
            member = place[0] ^ k
            term = lax.dot_general(
                back[...], w[...], (((1,), (1,)), ((), ())), preferred_element_type=F32
            ).astype(BF16)
            for h in range(4):
                for x in range(4):
                    row = (h * 4 + x) * block
                    out[x, member, h, core] = term[row : row + block]


def weight_parts(place, tokens, own, other, *outs):
    width, n = outs[0].shape
    half = own.shape[0]
    dims = (((0,), (0,)), ((), ()))
    for k, out in enumerate(outs):
        for s in spans(n):
            cols = slice(k * width, (k + 1) * width)
            term = lax.dot_general(tokens[:half, cols], own[:, s], dims, preferred_element_type=F32)
            term += lax.dot_general(tokens[half:, cols], other[:, s], dims, preferred_element_type=F32)
            out[:, s] = term.astype(BF16)


def after(x, *others):
    return lax.optimization_barrier((x, *others))[0]


def per_device(activations, gate_weight, up_weight, hidden_grad):
    index = lax.axis_index("dp")
    core, y, z_bit = index & 1, (index >> 1) & 1, (index >> 2) & 1
    y0, z0 = y == 0, z_bit == 0
    place = jnp.stack([z_bit * 2 + y, core]).astype(jnp.int32)
    rows, width = activations.shape
    half = gate_weight.shape[1] // 2
    block = hidden_grad.shape[0]
    count = 16 * block
    flops = 2 * count * 4 * width * half

    def pick(cond, a, b):
        return jnp.where(cond, a, b)

    def by_member(parts):
        a = [pick(y0, parts[i], parts[i ^ 1]) for i in range(4)]
        return [pick(z0, a[i], a[i ^ 2]) for i in range(4)]

    def pair(mine, other):
        return pick(y0, mine, other), pick(y0, other, mine)

    pieces = by_member(
        [gate_weight[:, :half], gate_weight[:, half:], up_weight[:, :half], up_weight[:, half:]]
    )
    weights = [pieces[0]] + [lax.ppermute(pieces[k], "dp", QUAD_SWAP[k]) for k in (1, 2, 3)]

    raw = lax.all_to_all(
        jnp.broadcast_to(activations[None], (16, rows, width)), ("dp", "tensor"), 0, 0,
        axis_index_groups=QUAD_YHI_GROUPS,
    )
    raw = after(raw, weights[1])
    raw = lax.all_to_all(
        jnp.broadcast_to(raw[None], (4, 16, rows, width)), "tensor", 0, 0, axis_index_groups=X_GROUPS
    )
    raw = raw.reshape(4, 4, 4, 2, block, width)

    tokens, sent = call(
        arrange_and_send, 5, [struct((2 * count, 4 * width)), struct((count, half), F32)], flops
    )(place, raw, *weights)
    got = lax.ppermute(sent, "dp", CORE_SWAP)
    part = call(keep_sums, 6, struct((count, half)), flops)(place, tokens, *weights, got)
    part = lax.all_to_all(part.reshape(8, 2 * block, half), "dp", 0, 0, axis_index_groups=Z_GROUPS)
    gate_pre = jnp.sum(part[0::2].astype(F32), 0)
    up_pre = jnp.sum(part[1::2].astype(F32), 0)

    lo, hi = hidden_grad[:, :half], hidden_grad[:, half:]
    mine, other = pair(lo, hi)
    grad = jnp.concatenate(pair(mine, lax.ppermute(other, "dp", Y_SWAP)), 0).astype(F32)

    sig = jax.nn.sigmoid(gate_pre)
    hidden = (gate_pre * sig * up_pre).astype(BF16)
    gate_back = (grad * up_pre * sig * (1.0 + gate_pre * (1.0 - sig))).astype(BF16)
    up_back = (grad * gate_pre * sig).astype(BF16)

    own = lax.all_to_all(
        jnp.stack([gate_back, up_back] * 4), "dp", 0, 0, axis_index_groups=Z_GROUPS
    ).reshape(count, half)
    mine, other = pair(hidden[:block], hidden[block:])
    other = lax.ppermute(other, "dp", Y_SWAP)
    own = after(own, other)
    hidden = jnp.concatenate(pair(mine, other), 1)
    other = lax.ppermute(own, "dp", CORE_SWAP)

    total = call(input_parts, 6, struct((4, 4, 4, 2, block, width)), 2 * flops)(
        place, own, other, *weights
    )
    total = lax.all_to_all(
        total.reshape(4, 16, rows, width), "tensor", 0, 0, axis_index_groups=X_GROUPS
    )
    total = jnp.sum(total.astype(F32), 0).astype(BF16)

    grads = call(weight_parts, 3, [struct((width, half))] * 4, 2 * flops)(place, tokens, own, other)
    grads = [grads[0]] + [lax.ppermute(grads[k], "dp", QUAD_SWAP[k]) for k in (1, 2, 3)]

    total = after(total, grads[1])
    total = lax.all_to_all(total, ("dp", "tensor"), 0, 0, axis_index_groups=QUAD_YHI_GROUPS)
    input_grad = jnp.sum(total.astype(F32), 0).astype(BF16)

    grads = by_member(grads)
    gate_grad = jnp.concatenate(grads[:2], 1)
    up_grad = jnp.concatenate(grads[2:], 1)
    return (hidden, input_grad, gate_grad, up_grad)


def solution(mesh):
    placed = (P("tensor", "dp"), P("dp", "tensor"), P("dp", "tensor"), P("dp", "tensor"))
    return jax.shard_map(
        per_device,
        mesh=mesh,
        in_specs=placed,
        out_specs=(P("dp", "tensor"), P("tensor", "dp"), P("dp", "tensor"), P("dp", "tensor")),
        check_vma=False,
    )
```

time: 548 us -> 164 us (0.30)
  waiting for transfers between devices: 470 us -> 71.4 us
  starting transfers between devices: 0.2 us -> 65.3 us
  blocking collectives: 40.3 us -> 0 us
  matrix products: 16 us -> 0 us
  between operations: 13.8 us -> 0.85 us
  Pallas kernels: 0 us -> 8.21 us
  other arithmetic: 3.03 us -> 9.07 us
    reduce_scatter x3 -> x0, waiting for transfers between devices: 331 us -> none  [the longest x1 127 us: per_device(): lax.psum_scatter(term_maker(tokens_all, gate_weight), 'dp', scatter_dimen...]
    all_gather x2 -> x0, waiting for transfers between devices: 138 us -> none  [the longest x1 70.2 us: per_device(): lax.all_gather(back_gate, 'dp', axis=0, tiled=True)]
    ppermute x0 -> x10, waiting for transfers between devices: none -> 42.5 us  [the longest x3 28.7 us: per_device(): lax.ppermute(pieces[k], 'dp', QUAD_SWAP[k])]
    all_gather x1 -> x0, blocking collectives: 40.3 us -> none  [per_device(): tokens_all = lax.all_gather(activations, 'tensor', axis=0, tiled=True)]
    all_to_all x0 -> x6, starting transfers between devices: none -> 36.2 us  [the longest x1 9.56 us: per_device(): lax.all_to_all(jnp.broadcast_to(activations[None], (16, rows, width)), ('...]
    ppermute x0 -> x10, starting transfers between devices: none -> 29.1 us  [the longest x3 9.02 us: per_device(): lax.ppermute(pieces[k], 'dp', QUAD_SWAP[k])]
    all_to_all x0 -> x6, waiting for transfers between devices: none -> 28.9 us  [the longest x1 11.6 us: per_device(): lax.all_to_all(part.reshape(8, 2 * block, half), 'dp', 0, 0, axis_index_g...]
    dot_general x6 -> x0, matrix products: 16 us -> none  [the longest x2 6.1 us: term_maker(): return jnp.dot(tokens_all, weight, preferred_element_type=jnp.float32)]
  transfers between devices with their start and end apart: 5 -> 16, of which waited for: 5 -> 11; matrix products, arithmetic and copies ran while one was open for 3% -> 4% of each run, Pallas kernels for 0% -> 1%
where the time goes in v2:
time: 164 us; the launch traced here: 161 us
  waiting for transfers between devices  71.4 us (44%)
  starting transfers between devices  65.3 us (40%)
  other arithmetic  9.07 us (6%)
  Pallas kernels  8.21 us (5%)
  local copies, waits for them, and re-layouts  6.34 us (4%)
    ppermute x3, waiting for transfers between devices, per_device(): lax.ppermute(pieces[k], 'dp', QUAD_SWAP[k])  28.7 us
    all_to_all x1, waiting for transfers between devices, per_device(): lax.all_to_all(part.reshape(8, 2 * block, half), 'dp', 0, 0, axis_index_g...  11.6 us
    all_to_all x1, waiting for transfers between devices, per_device(): lax.all_to_all(jnp.stack([gate_back, up_back] * 4), 'dp', 0, 0, axis_inde...  11.5 us
    all_to_all x1, starting transfers between devices, per_device(): lax.all_to_all(jnp.broadcast_to(activations[None], (16, rows, width)), ('...  9.56 us
    all_to_all x1, starting transfers between devices, per_device(): lax.all_to_all(part.reshape(8, 2 * block, half), 'dp', 0, 0, axis_index_g...  9.21 us
    ppermute x3, starting transfers between devices, per_device(): lax.ppermute(pieces[k], 'dp', QUAD_SWAP[k])  9.02 us
    ppermute x3, starting transfers between devices, per_device(): lax.ppermute(grads[k], 'dp', QUAD_SWAP[k])  8.36 us
    ppermute x3, waiting for transfers between devices, per_device(): lax.ppermute(grads[k], 'dp', QUAD_SWAP[k])  5.68 us
  transfers between devices with their start and end apart: 16, of which 11 were waited for; matrix products, arithmetic and copies ran while one was open for 4% of the time, Pallas kernels for 1%

profile of v2, /device:TPU:1, one launch (start us, length us, event | category | flops | bytes accessed | tf_op | source)
XLA Modules:
  0.0 161.2 jit_solution(12928385736064065422)
XLA Ops:
  0.6 1.4 broadcast_in_dim.4
  2.1 9.6 %all-to-all-start = ((bf16[16,32,256]{2,1,0:T(8,128)(2,1)}), bf16[16,32,256]{2,1,0:T(8,128)(2,1)S(1)}, u32[]{:S(2)}, u32[]{:S(2)}) async-start(bf16[16,32,256]{2,1,0:T(8,128)(2,1)} %broadcast_in_dim.4), calls=%async_computation | async-start | bytes 524288 | tf_op jit(solution)/shard_map/all_to_all | solution.py:135
  11.7 2.4 %broadcast_select_fusion.12 = (bf16[256,896]{1,0:T(8,128)(2,1)S(1)}, bf16[256,896]{1,0:T(8,128)(2,1)S(1)}, bf16[256,896]{1,0:T(8,128)(2,1)}, bf16[256,896]{1,0:T(8,128)(2,1)S(1)}) fusion(pred[]{:T(512)S(6)} %eq.7, bf16[256,1792]{1,0:T(8,128)(2,1)} %param.5, pred[]{:T(512)S(6)} %eq.6, bf16[256,1792]{1,0:T(8,128)(2,1)} %param.6), kind=kLoop, calls=%fused_computation.16 | loop fusion | flops 1835008 | bytes 3670018 | tf_op jit(solution)/shard_map/jit(_where)/select_n | solution.py:121
  14.1 3.2 %collective-permute-start = (bf16[256,896]{1,0:T(8,128)(2,1)S(1)}, bf16[256,896]{1,0:T(8,128)(2,1)S(1)}, u32[]{:S(2)}, u32[]{:S(2)}) collective-permute-start(bf16[256,896]{1,0:T(8,128)(2,1)S(1)} %get-tuple-element.35), channel_id=1, source_target_pairs={{0,32},{16,48},{32,0},{48,16},{64,96},{80,112},{96,64},{112,80},{1... | collective-permute-start | bytes 1376264 | tf_op jit(solution)/shard_map/ppermute | solution.py:133
  17.4 11.9 %collective-permute-done.w1 = bf16[256,896]{1,0:T(8,128)(2,1)S(1)} collective-permute-done((bf16[256,896]{1,0:T(8,128)(2,1)S(1)}, bf16[256,896]{1,0:T(8,128)(2,1)S(1)}, u32[]{:S(2)}, u32[]{:S(2)}) %collective-permute-start) | collective-permute-done | bytes 458784 | tf_op jit(solution)/shard_map/ppermute | solution.py:133
  29.3 0.0 all-to-all-done
  29.3 1.1 broadcast_in_dim.5
  30.4 4.0 %all-to-all-start.1 = ((bf16[4,16,32,256]{3,2,1,0:T(8,128)(2,1)}), bf16[4,16,32,256]{3,2,1,0:T(8,128)(2,1)S(1)}, u32[]{:S(2)}, u32[]{:S(2)}) async-start(bf16[4,16,32,256]{3,2,1,0:T(8,128)(2,1)} %broadcast_in_dim.5), calls=%async_computation.1 | async-start | bytes 2097152 | tf_op jit(solution)/shard_map/all_to_all | solution.py:140
  34.4 3.2 %collective-permute-start.1 = (bf16[256,896]{1,0:T(8,128)(2,1)}, bf16[256,896]{1,0:T(8,128)(2,1)S(1)}, u32[]{:S(2)}, u32[]{:S(2)}) collective-permute-start(bf16[256,896]{1,0:T(8,128)(2,1)} %get-tuple-element.34), channel_id=1, source_target_pairs={{0,64},{16,80},{32,96},{48,112},{64,0},{80,16},{96,32},{112,48},{1... | collective-permute-start | bytes 1376264 | tf_op jit(solution)/shard_map/ppermute | solution.py:133
  37.6 2.6 %collective-permute-start.2 = (bf16[256,896]{1,0:T(8,128)(2,1)S(1)}, bf16[256,896]{1,0:T(8,128)(2,1)S(1)}, u32[]{:S(2)}, u32[]{:S(2)}) collective-permute-start(bf16[256,896]{1,0:T(8,128)(2,1)S(1)} %get-tuple-element.32), channel_id=1, source_target_pairs={{0,96},{16,112},{32,64},{48,80},{64,32},{80,48},{96,0},{112,16},{1... | collective-permute-start | bytes 1376264 | tf_op jit(solution)/shard_map/ppermute | solution.py:133
  40.2 0.1 pad_add_fusion.place
  40.3 16.8 %collective-permute-done.1.w2 = bf16[256,896]{1,0:T(8,128)(2,1)S(1)} collective-permute-done((bf16[256,896]{1,0:T(8,128)(2,1)}, bf16[256,896]{1,0:T(8,128)(2,1)S(1)}, u32[]{:S(2)}, u32[]{:S(2)}) %collective-permute-start.1) | collective-permute-done | bytes 458784 | tf_op jit(solution)/shard_map/ppermute | solution.py:133
  57.1 0.0 collective-permute-done.2.w3
  57.1 0.0 all-to-all-done.1
  57.1 1.3 shard_map.75
  58.4 0.0 copy-start
  58.4 4.1 %collective-permute-start.3 = (f32[256,896]{1,0:T(8,128)S(1)}, f32[256,896]{1,0:T(8,128)S(1)}, u32[]{:S(2)}, u32[]{:S(2)}) collective-permute-start(f32[256,896]{1,0:T(8,128)S(1)} %get-tuple-element.15), channel_id=1, source_target_pairs={{0,16},{16,0},{32,48},{48,32},{64,80},{80,64},{96,112},{112,96},{1... | collective-permute-start | bytes 2752520 | tf_op jit(solution)/shard_map/ppermute | solution.py:148
  62.6 2.1 %collective-permute-done.3.got = f32[256,896]{1,0:T(8,128)S(1)} collective-permute-done((f32[256,896]{1,0:T(8,128)S(1)}, f32[256,896]{1,0:T(8,128)S(1)}, u32[]{:S(2)}, u32[]{:S(2)}) %collective-permute-start.3) | collective-permute-done | bytes 917536 | tf_op jit(solution)/shard_map/ppermute | solution.py:148
  64.6 0.0 copy-start.2
  64.6 2.0 %shard_map.76 = bf16[256,896]{1,0:T(8,128)(2,1)} custom-call(s32[2]{0:T(128)S(1)} %pad_add_fusion.place, bf16[512,1024]{1,0:T(8,128)(2,1)S(1)} %get-tuple-element.14.tokens, bf16[256,896]{1,0:T(8,128)(2,1)S(1)} %get-tuple-element.33.w0, bf16[256,896]{1,0:T(8,128)(2,1)S(1)} %collective-permute-done.w1, bf16[256,896]{1,0:T(8,128)(2,1)S(1)} %collective-permute-done.1.w2, ...), custom_call_target="tpu_custom_call" | custom-call | flops 469762048 | bytes 4194304 | tf_op jit(solution)/shard_map/pallas_call | solution.py:149
  66.7 0.0 copy-done
  66.7 9.2 %all-to-all-start.2 = ((bf16[8,32,896]{2,1,0:T(8,128)(2,1)}), bf16[8,32,896]{2,1,0:T(8,128)(2,1)S(1)}, u32[]{:S(2)}, u32[]{:S(2)}) async-start(bf16[8,32,896]{2,1,0:T(8,128)(2,1)} %bitcast.3), calls=%async_computation.2 | async-start | bytes 917504 | tf_op jit(solution)/shard_map/all_to_all | solution.py:150
  75.9 0.0 copy-done.2
  75.9 2.6 %collective-permute-start.5 = (bf16[16,896]{1,0:T(8,128)(2,1)S(1)}, bf16[16,896]{1,0:T(8,128)(2,1)S(1)}, u32[]{:S(2)}, u32[]{:S(2)}) collective-permute-start(bf16[16,896]{1,0:T(8,128)(2,1)S(1)} %broadcast_select_fusion.16), channel_id=1, source_target_pairs={{0,32},{16,48},{32,0},{48,16},{64,96},{80,112},{96,64},{112,80},{1... | collective-permute-start | bytes 86024 | tf_op jit(solution)/shard_map/ppermute | solution.py:156
  78.5 2.3 %collective-permute-done.5 = bf16[16,896]{1,0:T(8,128)(2,1)S(1)} collective-permute-done((bf16[16,896]{1,0:T(8,128)(2,1)S(1)}, bf16[16,896]{1,0:T(8,128)(2,1)S(1)}, u32[]{:S(2)}, u32[]{:S(2)}) %collective-permute-start.5) | collective-permute-done | bytes 28704 | tf_op jit(solution)/shard_map/ppermute | solution.py:156
  80.8 11.6 %all-to-all-done.2 = bf16[8,32,896]{2,1,0:T(8,128)(2,1)S(1)} async-done(((bf16[8,32,896]{2,1,0:T(8,128)(2,1)}), bf16[8,32,896]{2,1,0:T(8,128)(2,1)S(1)}, u32[]{:S(2)}, u32[]{:S(2)}) %all-to-all-start.2) | async-done | bytes 458784 | tf_op jit(solution)/shard_map/all_to_all | solution.py:150
  92.4 0.1 convert_reduce_fusion.1
  92.5 0.7 constant_dynamic-update-slice_fusion.7
  93.2 0.7 constant_dynamic-update-slice_fusion.6
  93.8 0.6 constant_dynamic-update-slice_fusion.5
  94.5 0.6 constant_dynamic-update-slice_fusion.4
  95.1 0.6 constant_dynamic-update-slice_fusion.3
  95.7 0.6 constant_dynamic-update-slice_fusion.2
  96.3 0.6 constant_dynamic-update-slice_fusion.1
  97.0 0.6 constant_dynamic-update-slice_fusion
  97.6 3.5 %all-to-all-start.3 = ((bf16[8,32,896]{2,1,0:T(8,128)(2,1)}), bf16[8,32,896]{2,1,0:T(8,128)(2,1)S(1)}, u32[]{:S(2)}, u32[]{:S(2)}) async-start(bf16[8,32,896]{2,1,0:T(8,128)(2,1)} %constant_dynamic-update-slice_fusion), calls=%async_computation.3 | async-start | bytes 917504 | tf_op jit(solution)/shard_map/all_to_all | solution.py:163
  101.2 2.6 %collective-permute-start.4 = (bf16[16,896]{1,0:T(8,128)(2,1)S(1)}, bf16[16,896]{1,0:T(8,128)(2,1)S(1)}, u32[]{:S(2)}, u32[]{:S(2)}) collective-permute-start(bf16[16,896]{1,0:T(8,128)(2,1)S(1)} %broadcast_select_fusion.20), channel_id=1, source_target_pairs={{0,32},{16,48},{32,0},{48,16},{64,96},{80,112},{96,64},{112,80},{1... | collective-permute-start | bytes 86024 | tf_op jit(solution)/shard_map/ppermute | solution.py:167
  103.8 2.3 %collective-permute-done.4 = bf16[16,896]{1,0:T(8,128)(2,1)S(1)} collective-permute-done((bf16[16,896]{1,0:T(8,128)(2,1)S(1)}, bf16[16,896]{1,0:T(8,128)(2,1)S(1)}, u32[]{:S(2)}, u32[]{:S(2)}) %collective-permute-start.4) | collective-permute-done | bytes 28704 | tf_op jit(solution)/shard_map/ppermute | solution.py:167
  106.1 11.5 %all-to-all-done.3 = bf16[8,32,896]{2,1,0:T(8,128)(2,1)S(1)} async-done(((bf16[8,32,896]{2,1,0:T(8,128)(2,1)}), bf16[8,32,896]{2,1,0:T(8,128)(2,1)S(1)}, u32[]{:S(2)}, u32[]{:S(2)}) %all-to-all-start.3) | async-done | bytes 458784 | tf_op jit(solution)/shard_map/all_to_all | solution.py:163
  117.6 2.4 %collective-permute-start.6 = (bf16[256,896]{1,0:T(8,128)(2,1)S(1)}, bf16[256,896]{1,0:T(8,128)(2,1)S(1)}, u32[]{:S(2)}, u32[]{:S(2)}) collective-permute-start(bf16[256,896]{1,0:T(8,128)(2,1)S(1)} %bitcast.34), channel_id=1, source_target_pairs={{0,16},{16,0},{32,48},{48,32},{64,80},{80,64},{96,112},{112,96},{1... | collective-permute-start | bytes 1376264 | tf_op jit(solution)/shard_map/ppermute | solution.py:170
  119.9 1.4 collective-permute-done.6.other
  121.4 2.8 %shard_map.77 = bf16[4,4,4,2,16,256]{5,4,3,2,1,0:T(8,128)(2,1)} custom-call(s32[2]{0:T(128)S(1)} %pad_add_fusion.place, bf16[256,896]{1,0:T(8,128)(2,1)S(1)} %bitcast.35, bf16[256,896]{1,0:T(8,128)(2,1)S(1)} %collective-permute-done.6.other, bf16[256,896]{1,0:T(8,128)(2,1)S(1)} %get-tuple-element.33.w0, bf16[256,896]{1,0:T(8,128)(2,1)S(1)} %collective-permute-done.w1, ...), custom_call_target="tpu_custom_call" | custom-call | flops 939524096 | bytes 4194304 | tf_op jit(solution)/shard_map/pallas_call | solution.py:172
  124.2 0.0 copy-start.1
  124.2 4.4 %all-to-all-start.4 = ((bf16[4,16,32,256]{3,2,1,0:T(8,128)(2,1)}), bf16[4,16,32,256]{3,2,1,0:T(8,128)(2,1)}, u32[]{:S(2)}, u32[]{:S(2)}) async-start(bf16[4,16,32,256]{3,2,1,0:T(8,128)(2,1)} %bitcast.9), calls=%async_computation.4 | async-start | bytes 2097152 | tf_op jit(solution)/shard_map/all_to_all | solution.py:175
  128.5 0.0 copy-done.1
  128.6 2.1 %shard_map.78 = (bf16[256,896]{1,0:T(8,128)(2,1)S(1)}, bf16[256,896]{1,0:T(8,128)(2,1)}, bf16[256,896]{1,0:T(8,128)(2,1)S(1)}, bf16[256,896]{1,0:T(8,128)(2,1)S(1)}) custom-call(s32[2]{0:T(128)S(1)} %pad_add_fusion.place, bf16[512,1024]{1,0:T(8,128)(2,1)S(1)} %copy-done.1, bf16[256,896]{1,0:T(8,128)(2,1)S(1)} %bitcast.36, ...), custom_call_target="tpu_custom_call" | custom-call | flops 939524096 | bytes 4194304 | tf_op jit(solution)/shard_map/pallas_call | solution.py:180
  130.6 2.6 %collective-permute-start.7 = (bf16[256,896]{1,0:T(8,128)(2,1)}, bf16[256,896]{1,0:T(8,128)(2,1)S(1)}, u32[]{:S(2)}, u32[]{:S(2)}) collective-permute-start(bf16[256,896]{1,0:T(8,128)(2,1)} %get-tuple-element.17), channel_id=1, source_target_pairs={{0,32},{16,48},{32,0},{48,16},{64,96},{80,112},{96,64},{112,80},{1... | collective-permute-start | bytes 1376264 | tf_op jit(solution)/shard_map/ppermute | solution.py:181
  133.2 2.2 %collective-permute-start.8 = (bf16[256,896]{1,0:T(8,128)(2,1)S(1)}, bf16[256,896]{1,0:T(8,128)(2,1)S(1)}, u32[]{:S(2)}, u32[]{:S(2)}) collective-permute-start(bf16[256,896]{1,0:T(8,128)(2,1)S(1)} %get-tuple-element.20), channel_id=1, source_target_pairs={{0,64},{16,80},{32,96},{48,112},{64,0},{80,16},{96,32},{112,48},{1... | collective-permute-start | bytes 1376264 | tf_op jit(solution)/shard_map/ppermute | solution.py:181
  135.4 3.6 %collective-permute-start.9 = (bf16[256,896]{1,0:T(8,128)(2,1)S(1)}, bf16[256,896]{1,0:T(8,128)(2,1)S(1)}, u32[]{:S(2)}, u32[]{:S(2)}) collective-permute-start(bf16[256,896]{1,0:T(8,128)(2,1)S(1)} %get-tuple-element.21), channel_id=1, source_target_pairs={{0,96},{16,112},{32,64},{48,80},{64,32},{80,48},{96,0},{112,16},{1... | collective-permute-start | bytes 1376264 | tf_op jit(solution)/shard_map/ppermute | solution.py:181
  139.0 0.6 pad_maximum_fusion.2
  139.7 3.5 %all-to-all-done.4 = bf16[4,16,32,256]{3,2,1,0:T(8,128)(2,1)} async-done(((bf16[4,16,32,256]{3,2,1,0:T(8,128)(2,1)}), bf16[4,16,32,256]{3,2,1,0:T(8,128)(2,1)}, u32[]{:S(2)}, u32[]{:S(2)}) %all-to-all-start.4) | async-done | bytes 1048608 | tf_op jit(solution)/shard_map/all_to_all | solution.py:175
  143.2 2.2 %reduce_sum.50 = bf16[16,32,256]{2,1,0:T(8,128)(2,1)} reduce(bf16[4,16,32,256]{3,2,1,0:T(8,128)(2,1)} %all-to-all-done.4, bf16[]{:T(256)} %constant.18.clone.1), dimensions={0}, to_apply=%region_2.3 | reduce | flops 393216 | bytes 1310722 | tf_op jit(solution)/shard_map/reduce_sum | solution.py:178
  145.3 0.0 collective-permute-done.7
  145.3 5.6 %all-to-all-start.5 = ((bf16[16,32,256]{2,1,0:T(8,128)(2,1)}), bf16[16,32,256]{2,1,0:T(8,128)(2,1)S(1)}, u32[]{:S(2)}, u32[]{:S(2)}) async-start(bf16[16,32,256]{2,1,0:T(8,128)(2,1)} %reduce_sum.50), calls=%async_computation.5 | async-start | bytes 524288 | tf_op jit(solution)/shard_map/all_to_all | solution.py:184
  150.9 5.7 %collective-permute-done.8 = bf16[256,896]{1,0:T(8,128)(2,1)S(1)} collective-permute-done((bf16[256,896]{1,0:T(8,128)(2,1)S(1)}, bf16[256,896]{1,0:T(8,128)(2,1)S(1)}, u32[]{:S(2)}, u32[]{:S(2)}) %collective-permute-start.8) | collective-permute-done | bytes 458784 | tf_op jit(solution)/shard_map/ppermute | solution.py:181
  156.6 0.0 collective-permute-done.9
  156.6 0.2 broadcast_select_fusion.9
  156.8 1.4 pad_maximum_fusion
  158.2 2.3 %all-to-all-done.5 = bf16[16,32,256]{2,1,0:T(8,128)(2,1)S(1)} async-done(((bf16[16,32,256]{2,1,0:T(8,128)(2,1)}), bf16[16,32,256]{2,1,0:T(8,128)(2,1)S(1)}, u32[]{:S(2)}, u32[]{:S(2)}) %all-to-all-start.5) | async-done | bytes 262176 | tf_op jit(solution)/shard_map/all_to_all | solution.py:184
  160.5 0.6 reduce_sum.51
  (5 shorter events, 0.1 us)
Async XLA Ops:
  2.1 27.2 %all-to-all-start = ((bf16[16,32,256]{2,1,0:T(8,128)(2,1)}), bf16[16,32,256]{2,1,0:T(8,128)(2,1)S(1)}, u32[]{:S(2)}, u32[]{:S(2)}) async-start(bf16[16,32,256]{2,1,0:T(8,128)(2,1)} %broadcast_in_dim.4), calls=%async_computation | async-start | bytes 524288 | tf_op jit(solution)/shard_map/all_to_all | solution.py:135
  14.1 15.2 %collective-permute-start = (bf16[256,896]{1,0:T(8,128)(2,1)S(1)}, bf16[256,896]{1,0:T(8,128)(2,1)S(1)}, u32[]{:S(2)}, u32[]{:S(2)}) collective-permute-start(bf16[256,896]{1,0:T(8,128)(2,1)S(1)} %get-tuple-element.35), channel_id=1, source_target_pairs={{0,32},{16,48},{32,0},{48,16},{64,96},{80,112},{96,64},{112,80},{1... | collective-permute-start | bytes 1376264 | tf_op jit(solution)/shard_map/ppermute | solution.py:133
  30.4 26.7 %all-to-all-start.1 = ((bf16[4,16,32,256]{3,2,1,0:T(8,128)(2,1)}), bf16[4,16,32,256]{3,2,1,0:T(8,128)(2,1)S(1)}, u32[]{:S(2)}, u32[]{:S(2)}) async-start(bf16[4,16,32,256]{3,2,1,0:T(8,128)(2,1)} %broadcast_in_dim.5), calls=%async_computation.1 | async-start | bytes 2097152 | tf_op jit(solution)/shard_map/all_to_all | solution.py:140
  34.4 22.6 %collective-permute-start.1 = (bf16[256,896]{1,0:T(8,128)(2,1)}, bf16[256,896]{1,0:T(8,128)(2,1)S(1)}, u32[]{:S(2)}, u32[]{:S(2)}) collective-permute-start(bf16[256,896]{1,0:T(8,128)(2,1)} %get-tuple-element.34), channel_id=1, source_target_pairs={{0,64},{16,80},{32,96},{48,112},{64,0},{80,16},{96,32},{112,48},{1... | collective-permute-start | bytes 1376264 | tf_op jit(solution)/shard_map/ppermute | solution.py:133
  37.6 19.5 %collective-permute-start.2 = (bf16[256,896]{1,0:T(8,128)(2,1)S(1)}, bf16[256,896]{1,0:T(8,128)(2,1)S(1)}, u32[]{:S(2)}, u32[]{:S(2)}) collective-permute-start(bf16[256,896]{1,0:T(8,128)(2,1)S(1)} %get-tuple-element.32), channel_id=1, source_target_pairs={{0,96},{16,112},{32,64},{48,80},{64,32},{80,48},{96,0},{112,16},{1... | collective-permute-start | bytes 1376264 | tf_op jit(solution)/shard_map/ppermute | solution.py:133
  58.4 8.3 %copy-start = (bf16[512,1024]{1,0:T(8,128)(2,1)}, bf16[512,1024]{1,0:T(8,128)(2,1)S(1)}, u32[]{:S(2)}) copy-start(bf16[512,1024]{1,0:T(8,128)(2,1)S(1)} %get-tuple-element.14.tokens) | copy-start | bytes 3145732
  58.4 6.2 %collective-permute-start.3 = (f32[256,896]{1,0:T(8,128)S(1)}, f32[256,896]{1,0:T(8,128)S(1)}, u32[]{:S(2)}, u32[]{:S(2)}) collective-permute-start(f32[256,896]{1,0:T(8,128)S(1)} %get-tuple-element.15), channel_id=1, source_target_pairs={{0,16},{16,0},{32,48},{48,32},{64,80},{80,64},{96,112},{112,96},{1... | collective-permute-start | bytes 2752520 | tf_op jit(solution)/shard_map/ppermute | solution.py:148
  64.6 11.2 %copy-start.2 = (bf16[16,1792]{1,0:T(8,128)(2,1)S(1)}, bf16[16,1792]{1,0:T(8,128)(2,1)}, u32[]{:S(2)}) copy-start(bf16[16,1792]{1,0:T(8,128)(2,1)} %param.7) | copy-start | bytes 172036
  66.7 25.8 %all-to-all-start.2 = ((bf16[8,32,896]{2,1,0:T(8,128)(2,1)}), bf16[8,32,896]{2,1,0:T(8,128)(2,1)S(1)}, u32[]{:S(2)}, u32[]{:S(2)}) async-start(bf16[8,32,896]{2,1,0:T(8,128)(2,1)} %bitcast.3), calls=%async_computation.2 | async-start | bytes 917504 | tf_op jit(solution)/shard_map/all_to_all | solution.py:150
  75.9 4.9 %collective-permute-start.5 = (bf16[16,896]{1,0:T(8,128)(2,1)S(1)}, bf16[16,896]{1,0:T(8,128)(2,1)S(1)}, u32[]{:S(2)}, u32[]{:S(2)}) collective-permute-start(bf16[16,896]{1,0:T(8,128)(2,1)S(1)} %broadcast_select_fusion.16), channel_id=1, source_target_pairs={{0,32},{16,48},{32,0},{48,16},{64,96},{80,112},{96,64},{112,80},{1... | collective-permute-start | bytes 86024 | tf_op jit(solution)/shard_map/ppermute | solution.py:156
  97.6 20.0 %all-to-all-start.3 = ((bf16[8,32,896]{2,1,0:T(8,128)(2,1)}), bf16[8,32,896]{2,1,0:T(8,128)(2,1)S(1)}, u32[]{:S(2)}, u32[]{:S(2)}) async-start(bf16[8,32,896]{2,1,0:T(8,128)(2,1)} %constant_dynamic-update-slice_fusion), calls=%async_computation.3 | async-start | bytes 917504 | tf_op jit(solution)/shard_map/all_to_all | solution.py:163
  101.2 4.9 %collective-permute-start.4 = (bf16[16,896]{1,0:T(8,128)(2,1)S(1)}, bf16[16,896]{1,0:T(8,128)(2,1)S(1)}, u32[]{:S(2)}, u32[]{:S(2)}) collective-permute-start(bf16[16,896]{1,0:T(8,128)(2,1)S(1)} %broadcast_select_fusion.20), channel_id=1, source_target_pairs={{0,32},{16,48},{32,0},{48,16},{64,96},{80,112},{96,64},{112,80},{1... | collective-permute-start | bytes 86024 | tf_op jit(solution)/shard_map/ppermute | solution.py:167
  117.6 3.8 %collective-permute-start.6 = (bf16[256,896]{1,0:T(8,128)(2,1)S(1)}, bf16[256,896]{1,0:T(8,128)(2,1)S(1)}, u32[]{:S(2)}, u32[]{:S(2)}) collective-permute-start(bf16[256,896]{1,0:T(8,128)(2,1)S(1)} %bitcast.34), channel_id=1, source_target_pairs={{0,16},{16,0},{32,48},{48,32},{64,80},{80,64},{96,112},{112,96},{1... | collective-permute-start | bytes 1376264 | tf_op jit(solution)/shard_map/ppermute | solution.py:170
  124.2 4.4 %copy-start.1 = (bf16[512,1024]{1,0:T(8,128)(2,1)S(1)}, bf16[512,1024]{1,0:T(8,128)(2,1)}, u32[]{:S(2)}) copy-start(bf16[512,1024]{1,0:T(8,128)(2,1)} %copy-done) | copy-start | bytes 3145732
  124.2 19.0 %all-to-all-start.4 = ((bf16[4,16,32,256]{3,2,1,0:T(8,128)(2,1)}), bf16[4,16,32,256]{3,2,1,0:T(8,128)(2,1)}, u32[]{:S(2)}, u32[]{:S(2)}) async-start(bf16[4,16,32,256]{3,2,1,0:T(8,128)(2,1)} %bitcast.9), calls=%async_computation.4 | async-start | bytes 2097152 | tf_op jit(solution)/shard_map/all_to_all | solution.py:175
  130.6 14.7 %collective-permute-start.7 = (bf16[256,896]{1,0:T(8,128)(2,1)}, bf16[256,896]{1,0:T(8,128)(2,1)S(1)}, u32[]{:S(2)}, u32[]{:S(2)}) collective-permute-start(bf16[256,896]{1,0:T(8,128)(2,1)} %get-tuple-element.17), channel_id=1, source_target_pairs={{0,32},{16,48},{32,0},{48,16},{64,96},{80,112},{96,64},{112,80},{1... | collective-permute-start | bytes 1376264 | tf_op jit(solution)/shard_map/ppermute | solution.py:181
  133.2 23.4 %collective-permute-start.8 = (bf16[256,896]{1,0:T(8,128)(2,1)S(1)}, bf16[256,896]{1,0:T(8,128)(2,1)S(1)}, u32[]{:S(2)}, u32[]{:S(2)}) collective-permute-start(bf16[256,896]{1,0:T(8,128)(2,1)S(1)} %get-tuple-element.20), channel_id=1, source_target_pairs={{0,64},{16,80},{32,96},{48,112},{64,0},{80,16},{96,32},{112,48},{1... | collective-permute-start | bytes 1376264 | tf_op jit(solution)/shard_map/ppermute | solution.py:181
  135.4 21.2 %collective-permute-start.9 = (bf16[256,896]{1,0:T(8,128)(2,1)S(1)}, bf16[256,896]{1,0:T(8,128)(2,1)S(1)}, u32[]{:S(2)}, u32[]{:S(2)}) collective-permute-start(bf16[256,896]{1,0:T(8,128)(2,1)S(1)} %get-tuple-element.21), channel_id=1, source_target_pairs={{0,96},{16,112},{32,64},{48,80},{64,32},{80,48},{96,0},{112,16},{1... | collective-permute-start | bytes 1376264 | tf_op jit(solution)/shard_map/ppermute | solution.py:181
  145.3 15.2 %all-to-all-start.5 = ((bf16[16,32,256]{2,1,0:T(8,128)(2,1)}), bf16[16,32,256]{2,1,0:T(8,128)(2,1)S(1)}, u32[]{:S(2)}, u32[]{:S(2)}) async-start(bf16[16,32,256]{2,1,0:T(8,128)(2,1)} %reduce_sum.50), calls=%async_computation.5 | async-start | bytes 524288 | tf_op jit(solution)/shard_map/all_to_all | solution.py:184

commit v3 on v2

--- a/solution.py
+++ b/solution.py
@@ -63,16 +63,17 @@
         sent[:, s] = total
 
 
-def keep_sums(place, tokens, w0, w1, w2, w3, got, out):
+def keep_sums(place, tokens, w0, w1, w2, w3, out):
     width = w0.shape[0]
     half = out.shape[0]
     for s in spans(out.shape[1]):
-        total = got[:, s]
+        total = None
         for k, w in enumerate((w0, w1, w2, w3)):
-            total = total + jnp.dot(
+            term = jnp.dot(
                 tokens[:half, k * width : (k + 1) * width], w[:, s], preferred_element_type=F32
             )
-        out[:, s] = total.astype(BF16)
+            total = term if total is None else total + term
+        out[:, s] = total
 
 
 def input_parts(place, own, other, w0, w1, w2, w3, out):
@@ -136,7 +137,7 @@
         jnp.broadcast_to(activations[None], (16, rows, width)), ("dp", "tensor"), 0, 0,
         axis_index_groups=QUAD_YHI_GROUPS,
     )
-    raw = after(raw, weights[1])
+    raw = after(raw, weights[1], weights[2])
     raw = lax.all_to_all(
         jnp.broadcast_to(raw[None], (4, 16, rows, width)), "tensor", 0, 0, axis_index_groups=X_GROUPS
     )
@@ -146,7 +147,8 @@
         arrange_and_send, 5, [struct((2 * count, 4 * width)), struct((count, half), F32)], flops
     )(place, raw, *weights)
     got = lax.ppermute(sent, "dp", CORE_SWAP)
-    part = call(keep_sums, 6, struct((count, half)), flops)(place, tokens, *weights, got)
+    kept = call(keep_sums, 5, struct((count, half), F32), flops)(place, tokens, *weights)
+    part = (kept + got).astype(BF16)
     part = lax.all_to_all(part.reshape(8, 2 * block, half), "dp", 0, 0, axis_index_groups=Z_GROUPS)
     gate_pre = jnp.sum(part[0::2].astype(F32), 0)
     up_pre = jnp.sum(part[1::2].astype(F32), 0)
@@ -161,7 +163,10 @@
     up_back = (grad * gate_pre * sig).astype(BF16)
 
     own = lax.all_to_all(
-        jnp.stack([gate_back, up_back] * 4), "dp", 0, 0, axis_index_groups=Z_GROUPS
+        jnp.broadcast_to(jnp.stack([gate_back, up_back])[None], (4, 2, 2 * block, half)).reshape(
+            8, 2 * block, half
+        ),
+        "dp", 0, 0, axis_index_groups=Z_GROUPS,
     ).reshape(count, half)
     mine, other = pair(hidden[:block], hidden[block:])
     other = lax.ppermute(other, "dp", Y_SWAP)

time: 164 us -> 149 us (0.909)
  waiting for transfers between devices: 71.4 us -> 63.4 us
  local copies, waits for them, and re-layouts: 6.34 us -> 3.4 us
    ppermute x3, waiting for transfers between devices: 28.7 us -> 20 us  [per_device(): lax.ppermute(pieces[k], 'dp', QUAD_SWAP[k])]
    unnamed x11 -> x6, local copies, waits for them, and re-layouts: 3.15 us -> 0.01 us
  transfers between devices with their start and end apart: 16 -> 16, of which waited for: 11 -> 13; matrix products, arithmetic and copies ran while one was open for 4% -> 4% of each run, Pallas kernels for 1% -> 2%
where the time goes in v3:
time: 149 us; the launch traced here: 147 us
  starting transfers between devices  64.5 us (43%)
  waiting for transfers between devices  63.4 us (43%)
  other arithmetic  7.91 us (5%)
  Pallas kernels  7.44 us (5%)
  local copies, waits for them, and re-layouts  3.4 us (2%)
    ppermute x3, waiting for transfers between devices, per_device(): lax.ppermute(pieces[k], 'dp', QUAD_SWAP[k])  20 us
    all_to_all x1, waiting for transfers between devices, per_device(): lax.all_to_all(part.reshape(8, 2 * block, half), 'dp', 0, 0, axis_index_g...  11.6 us
    all_to_all x1, waiting for transfers between devices, per_device(): lax.all_to_all(jnp.broadcast_to(jnp.stack([gate_back, up_back])[None], (4...  11.5 us
    all_to_all x1, starting transfers between devices, per_device(): lax.all_to_all(jnp.broadcast_to(activations[None], (16, rows, width)), ('...  9.56 us
    all_to_all x1, starting transfers between devices, per_device(): lax.all_to_all(part.reshape(8, 2 * block, half), 'dp', 0, 0, axis_index_g...  9.13 us
    ppermute x3, starting transfers between devices, per_device(): lax.ppermute(pieces[k], 'dp', QUAD_SWAP[k])  9.12 us
    ppermute x3, starting transfers between devices, per_device(): lax.ppermute(grads[k], 'dp', QUAD_SWAP[k])  8.36 us
    ppermute x3, waiting for transfers between devices, per_device(): lax.ppermute(grads[k], 'dp', QUAD_SWAP[k])  5.68 us
  transfers between devices with their start and end apart: 16, of which 13 were waited for; matrix products, arithmetic and copies ran while one was open for 4% of the time, Pallas kernels for 2%

profile of v3, /device:TPU:1, one launch (start us, length us, event | category | flops | bytes accessed | tf_op | source)
XLA Modules:
  0.0 147.5 jit_solution(16448892495194869699)
XLA Ops:
  0.6 1.4 broadcast_in_dim.6
  2.1 9.6 %all-to-all-start = ((bf16[16,32,256]{2,1,0:T(8,128)(2,1)}), bf16[16,32,256]{2,1,0:T(8,128)(2,1)S(1)}, u32[]{:S(2)}, u32[]{:S(2)}) async-start(bf16[16,32,256]{2,1,0:T(8,128)(2,1)} %broadcast_in_dim.6), calls=%async_computation | async-start | bytes 524288 | tf_op jit(solution)/shard_map/all_to_all | solution.py:136
  11.7 1.7 %broadcast_select_fusion.12 = (bf16[256,896]{1,0:T(8,128)(2,1)S(1)}, bf16[256,896]{1,0:T(8,128)(2,1)S(1)}, bf16[256,896]{1,0:T(8,128)(2,1)S(1)}, bf16[256,896]{1,0:T(8,128)(2,1)S(1)}) fusion(pred[]{:T(512)S(6)} %eq.7, bf16[256,1792]{1,0:T(8,128)(2,1)} %param.5, pred[]{:T(512)S(6)} %eq.6, bf16[256,1792]{1,0:T(8,128)(2,1)} %param.6), kind=kLoop, calls=%fused_computation.17 | loop fusion | flops 1835008 | bytes 3670018 | tf_op jit(solution)/shard_map/jit(_where)/select_n | solution.py:122
  13.3 3.3 %collective-permute-start = (bf16[256,896]{1,0:T(8,128)(2,1)S(1)}, bf16[256,896]{1,0:T(8,128)(2,1)S(1)}, u32[]{:S(2)}, u32[]{:S(2)}) collective-permute-start(bf16[256,896]{1,0:T(8,128)(2,1)S(1)} %get-tuple-element.31), channel_id=1, source_target_pairs={{0,32},{16,48},{32,0},{48,16},{64,96},{80,112},{96,64},{112,80},{1... | collective-permute-start | bytes 1376264 | tf_op jit(solution)/shard_map/ppermute | solution.py:134
  16.6 3.1 %collective-permute-start.1 = (bf16[256,896]{1,0:T(8,128)(2,1)S(1)}, bf16[256,896]{1,0:T(8,128)(2,1)S(1)}, u32[]{:S(2)}, u32[]{:S(2)}) collective-permute-start(bf16[256,896]{1,0:T(8,128)(2,1)S(1)} %get-tuple-element.29), channel_id=1, source_target_pairs={{0,64},{16,80},{32,96},{48,112},{64,0},{80,16},{96,32},{112,48},{1... | collective-permute-start | bytes 1376264 | tf_op jit(solution)/shard_map/ppermute | solution.py:134
  19.7 9.3 %collective-permute-done.w1 = bf16[256,896]{1,0:T(8,128)(2,1)S(1)} collective-permute-done((bf16[256,896]{1,0:T(8,128)(2,1)S(1)}, bf16[256,896]{1,0:T(8,128)(2,1)S(1)}, u32[]{:S(2)}, u32[]{:S(2)}) %collective-permute-start) | collective-permute-done | bytes 458784 | tf_op jit(solution)/shard_map/ppermute | solution.py:134
  29.0 1.0 collective-permute-done.1.w2
  30.0 0.0 all-to-all-done
  30.0 1.1 broadcast_in_dim.7
  31.1 4.0 %all-to-all-start.1 = ((bf16[4,16,32,256]{3,2,1,0:T(8,128)(2,1)}), bf16[4,16,32,256]{3,2,1,0:T(8,128)(2,1)S(1)}, u32[]{:S(2)}, u32[]{:S(2)}) async-start(bf16[4,16,32,256]{3,2,1,0:T(8,128)(2,1)} %broadcast_in_dim.7), calls=%async_computation.1 | async-start | bytes 2097152 | tf_op jit(solution)/shard_map/all_to_all | solution.py:141
  35.2 2.8 %collective-permute-start.2 = (bf16[256,896]{1,0:T(8,128)(2,1)S(1)}, bf16[256,896]{1,0:T(8,128)(2,1)S(1)}, u32[]{:S(2)}, u32[]{:S(2)}) collective-permute-start(bf16[256,896]{1,0:T(8,128)(2,1)S(1)} %get-tuple-element.28), channel_id=1, source_target_pairs={{0,96},{16,112},{32,64},{48,80},{64,32},{80,48},{96,0},{112,16},{1... | collective-permute-start | bytes 1376264 | tf_op jit(solution)/shard_map/ppermute | solution.py:134
  37.9 0.1 pad_add_fusion.place
  38.0 9.7 %collective-permute-done.2.w3 = bf16[256,896]{1,0:T(8,128)(2,1)S(1)} collective-permute-done((bf16[256,896]{1,0:T(8,128)(2,1)S(1)}, bf16[256,896]{1,0:T(8,128)(2,1)S(1)}, u32[]{:S(2)}, u32[]{:S(2)}) %collective-permute-start.2) | collective-permute-done | bytes 458784 | tf_op jit(solution)/shard_map/ppermute | solution.py:134
  47.7 0.3 all-to-all-done.1
  48.1 1.3 shard_map.75
  49.4 0.0 copy-start
  49.4 5.0 %collective-permute-start.3 = (f32[256,896]{1,0:T(8,128)S(1)}, f32[256,896]{1,0:T(8,128)S(1)}, u32[]{:S(2)}, u32[]{:S(2)}) collective-permute-start(f32[256,896]{1,0:T(8,128)S(1)} %get-tuple-element.15), channel_id=1, source_target_pairs={{0,16},{16,0},{32,48},{48,32},{64,80},{80,64},{96,112},{112,96},{1... | collective-permute-start | bytes 2752520 | tf_op jit(solution)/shard_map/ppermute | solution.py:149
  54.5 1.3 shard_map.76
  55.7 0.0 copy-done
  55.7 0.0 copy-start.2
  55.8 0.8 collective-permute-done.3
  56.5 0.9 add_convert_fusion
  57.4 9.1 %all-to-all-start.2 = ((bf16[8,32,896]{2,1,0:T(8,128)(2,1)}), bf16[8,32,896]{2,1,0:T(8,128)(2,1)S(1)}, u32[]{:S(2)}, u32[]{:S(2)}) async-start(bf16[8,32,896]{2,1,0:T(8,128)(2,1)} %bitcast.35), calls=%async_computation.2 | async-start | bytes 917504 | tf_op jit(solution)/shard_map/all_to_all | solution.py:152
  66.5 0.0 copy-done.2
  66.6 2.1 %collective-permute-start.5 = (bf16[16,896]{1,0:T(8,128)(2,1)S(1)}, bf16[16,896]{1,0:T(8,128)(2,1)S(1)}, u32[]{:S(2)}, u32[]{:S(2)}) collective-permute-start(bf16[16,896]{1,0:T(8,128)(2,1)S(1)} %broadcast_select_fusion.16), channel_id=1, source_target_pairs={{0,32},{16,48},{32,0},{48,16},{64,96},{80,112},{96,64},{112,80},{1... | collective-permute-start | bytes 86024 | tf_op jit(solution)/shard_map/ppermute | solution.py:158
  68.7 2.8 %collective-permute-done.5 = bf16[16,896]{1,0:T(8,128)(2,1)S(1)} collective-permute-done((bf16[16,896]{1,0:T(8,128)(2,1)S(1)}, bf16[16,896]{1,0:T(8,128)(2,1)S(1)}, u32[]{:S(2)}, u32[]{:S(2)}) %collective-permute-start.5) | collective-permute-done | bytes 28704 | tf_op jit(solution)/shard_map/ppermute | solution.py:158
  71.5 11.6 %all-to-all-done.2 = bf16[8,32,896]{2,1,0:T(8,128)(2,1)S(1)} async-done(((bf16[8,32,896]{2,1,0:T(8,128)(2,1)}), bf16[8,32,896]{2,1,0:T(8,128)(2,1)S(1)}, u32[]{:S(2)}, u32[]{:S(2)}) %all-to-all-start.2) | async-done | bytes 458784 | tf_op jit(solution)/shard_map/all_to_all | solution.py:152
  83.1 0.1 convert_reduce_fusion.1
  83.2 0.1 fusion.2
  83.3 0.8 broadcast_in_dim.8
  84.1 3.5 %all-to-all-start.3 = ((bf16[8,32,896]{2,1,0:T(8,128)(2,1)}), bf16[8,32,896]{2,1,0:T(8,128)(2,1)S(1)}, u32[]{:S(2)}, u32[]{:S(2)}) async-start(bf16[8,32,896]{2,1,0:T(8,128)(2,1)} %bitcast.8), calls=%async_computation.3 | async-start | bytes 917504 | tf_op jit(solution)/shard_map/all_to_all | solution.py:165
  87.6 2.1 %collective-permute-start.4 = (bf16[16,896]{1,0:T(8,128)(2,1)S(1)}, bf16[16,896]{1,0:T(8,128)(2,1)S(1)}, u32[]{:S(2)}, u32[]{:S(2)}) collective-permute-start(bf16[16,896]{1,0:T(8,128)(2,1)S(1)} %broadcast_select_fusion.20), channel_id=1, source_target_pairs={{0,32},{16,48},{32,0},{48,16},{64,96},{80,112},{96,64},{112,80},{1... | collective-permute-start | bytes 86024 | tf_op jit(solution)/shard_map/ppermute | solution.py:172
  89.7 2.8 %collective-permute-done.4 = bf16[16,896]{1,0:T(8,128)(2,1)S(1)} collective-permute-done((bf16[16,896]{1,0:T(8,128)(2,1)S(1)}, bf16[16,896]{1,0:T(8,128)(2,1)S(1)}, u32[]{:S(2)}, u32[]{:S(2)}) %collective-permute-start.4) | collective-permute-done | bytes 28704 | tf_op jit(solution)/shard_map/ppermute | solution.py:172
  92.5 11.5 %all-to-all-done.3 = bf16[8,32,896]{2,1,0:T(8,128)(2,1)S(1)} async-done(((bf16[8,32,896]{2,1,0:T(8,128)(2,1)}), bf16[8,32,896]{2,1,0:T(8,128)(2,1)S(1)}, u32[]{:S(2)}, u32[]{:S(2)}) %all-to-all-start.3) | async-done | bytes 458784 | tf_op jit(solution)/shard_map/all_to_all | solution.py:165
  104.0 2.4 %collective-permute-start.6 = (bf16[256,896]{1,0:T(8,128)(2,1)S(1)}, bf16[256,896]{1,0:T(8,128)(2,1)S(1)}, u32[]{:S(2)}, u32[]{:S(2)}) collective-permute-start(bf16[256,896]{1,0:T(8,128)(2,1)S(1)} %bitcast.32), channel_id=1, source_target_pairs={{0,16},{16,0},{32,48},{48,32},{64,80},{80,64},{96,112},{112,96},{1... | collective-permute-start | bytes 1376264 | tf_op jit(solution)/shard_map/ppermute | solution.py:175
  106.4 1.4 collective-permute-done.6.other
  107.8 2.8 %shard_map.77 = bf16[4,4,4,2,16,256]{5,4,3,2,1,0:T(8,128)(2,1)} custom-call(s32[2]{0:T(128)S(1)} %pad_add_fusion.place, bf16[256,896]{1,0:T(8,128)(2,1)S(1)} %bitcast.33, bf16[256,896]{1,0:T(8,128)(2,1)S(1)} %collective-permute-done.6.other, bf16[256,896]{1,0:T(8,128)(2,1)S(1)} %get-tuple-element.30.w0, bf16[256,896]{1,0:T(8,128)(2,1)S(1)} %collective-permute-done.w1, ...), custom_call_target="tpu_custom_call" | custom-call | flops 939524096 | bytes 4194304 | tf_op jit(solution)/shard_map/pallas_call | solution.py:177
  110.6 0.0 copy-start.1
  110.6 4.4 %all-to-all-start.4 = ((bf16[4,16,32,256]{3,2,1,0:T(8,128)(2,1)}), bf16[4,16,32,256]{3,2,1,0:T(8,128)(2,1)}, u32[]{:S(2)}, u32[]{:S(2)}) async-start(bf16[4,16,32,256]{3,2,1,0:T(8,128)(2,1)} %bitcast.10), calls=%async_computation.4 | async-start | bytes 2097152 | tf_op jit(solution)/shard_map/all_to_all | solution.py:180
  115.0 0.0 copy-done.1
  115.0 2.1 %shard_map.78 = (bf16[256,896]{1,0:T(8,128)(2,1)S(1)}, bf16[256,896]{1,0:T(8,128)(2,1)}, bf16[256,896]{1,0:T(8,128)(2,1)S(1)}, bf16[256,896]{1,0:T(8,128)(2,1)S(1)}) custom-call(s32[2]{0:T(128)S(1)} %pad_add_fusion.place, bf16[512,1024]{1,0:T(8,128)(2,1)S(1)} %copy-done.1, bf16[256,896]{1,0:T(8,128)(2,1)S(1)} %bitcast.34, ...), custom_call_target="tpu_custom_call" | custom-call | flops 939524096 | bytes 4194304 | tf_op jit(solution)/shard_map/pallas_call | solution.py:185
  117.1 2.1 %collective-permute-start.7 = (bf16[256,896]{1,0:T(8,128)(2,1)}, bf16[256,896]{1,0:T(8,128)(2,1)S(1)}, u32[]{:S(2)}, u32[]{:S(2)}) collective-permute-start(bf16[256,896]{1,0:T(8,128)(2,1)} %get-tuple-element.17), channel_id=1, source_target_pairs={{0,32},{16,48},{32,0},{48,16},{64,96},{80,112},{96,64},{112,80},{1... | collective-permute-start | bytes 1376264 | tf_op jit(solution)/shard_map/ppermute | solution.py:186
  119.2 2.2 %collective-permute-start.8 = (bf16[256,896]{1,0:T(8,128)(2,1)S(1)}, bf16[256,896]{1,0:T(8,128)(2,1)S(1)}, u32[]{:S(2)}, u32[]{:S(2)}) collective-permute-start(bf16[256,896]{1,0:T(8,128)(2,1)S(1)} %get-tuple-element.20), channel_id=1, source_target_pairs={{0,64},{16,80},{32,96},{48,112},{64,0},{80,16},{96,32},{112,48},{1... | collective-permute-start | bytes 1376264 | tf_op jit(solution)/shard_map/ppermute | solution.py:186
  121.4 4.1 %collective-permute-start.9 = (bf16[256,896]{1,0:T(8,128)(2,1)S(1)}, bf16[256,896]{1,0:T(8,128)(2,1)S(1)}, u32[]{:S(2)}, u32[]{:S(2)}) collective-permute-start(bf16[256,896]{1,0:T(8,128)(2,1)S(1)} %get-tuple-element.21), channel_id=1, source_target_pairs={{0,96},{16,112},{32,64},{48,80},{64,32},{80,48},{96,0},{112,16},{1... | collective-permute-start | bytes 1376264 | tf_op jit(solution)/shard_map/ppermute | solution.py:186
  125.5 0.6 pad_maximum_fusion.3
  126.1 3.8 %all-to-all-done.4 = bf16[4,16,32,256]{3,2,1,0:T(8,128)(2,1)} async-done(((bf16[4,16,32,256]{3,2,1,0:T(8,128)(2,1)}), bf16[4,16,32,256]{3,2,1,0:T(8,128)(2,1)}, u32[]{:S(2)}, u32[]{:S(2)}) %all-to-all-start.4) | async-done | bytes 1048608 | tf_op jit(solution)/shard_map/all_to_all | solution.py:180
  129.9 2.2 %reduce_sum.50 = bf16[16,32,256]{2,1,0:T(8,128)(2,1)} reduce(bf16[4,16,32,256]{3,2,1,0:T(8,128)(2,1)} %all-to-all-done.4, bf16[]{:T(256)} %constant.18.clone.1), dimensions={0}, to_apply=%region_2.3 | reduce | flops 393216 | bytes 1310722 | tf_op jit(solution)/shard_map/reduce_sum | solution.py:183
  132.1 0.0 collective-permute-done.7
  132.1 4.8 %all-to-all-start.5 = ((bf16[16,32,256]{2,1,0:T(8,128)(2,1)}), bf16[16,32,256]{2,1,0:T(8,128)(2,1)S(1)}, u32[]{:S(2)}, u32[]{:S(2)}) async-start(bf16[16,32,256]{2,1,0:T(8,128)(2,1)} %reduce_sum.50), calls=%async_computation.5 | async-start | bytes 524288 | tf_op jit(solution)/shard_map/all_to_all | solution.py:189
  136.9 5.7 %collective-permute-done.8 = bf16[256,896]{1,0:T(8,128)(2,1)S(1)} collective-permute-done((bf16[256,896]{1,0:T(8,128)(2,1)S(1)}, bf16[256,896]{1,0:T(8,128)(2,1)S(1)}, u32[]{:S(2)}, u32[]{:S(2)}) %collective-permute-start.8) | collective-permute-done | bytes 458784 | tf_op jit(solution)/shard_map/ppermute | solution.py:186
  142.6 0.0 collective-permute-done.9
  142.6 0.2 broadcast_select_fusion.9
  142.8 1.4 pad_maximum_fusion
  144.2 2.7 %all-to-all-done.5 = bf16[16,32,256]{2,1,0:T(8,128)(2,1)S(1)} async-done(((bf16[16,32,256]{2,1,0:T(8,128)(2,1)}), bf16[16,32,256]{2,1,0:T(8,128)(2,1)S(1)}, u32[]{:S(2)}, u32[]{:S(2)}) %all-to-all-start.5) | async-done | bytes 262176 | tf_op jit(solution)/shard_map/all_to_all | solution.py:189
  146.8 0.6 reduce_sum.51
  (6 shorter events, 0.1 us)
Async XLA Ops:
  2.1 27.9 %all-to-all-start = ((bf16[16,32,256]{2,1,0:T(8,128)(2,1)}), bf16[16,32,256]{2,1,0:T(8,128)(2,1)S(1)}, u32[]{:S(2)}, u32[]{:S(2)}) async-start(bf16[16,32,256]{2,1,0:T(8,128)(2,1)} %broadcast_in_dim.6), calls=%async_computation | async-start | bytes 524288 | tf_op jit(solution)/shard_map/all_to_all | solution.py:136
  13.3 15.6 %collective-permute-start = (bf16[256,896]{1,0:T(8,128)(2,1)S(1)}, bf16[256,896]{1,0:T(8,128)(2,1)S(1)}, u32[]{:S(2)}, u32[]{:S(2)}) collective-permute-start(bf16[256,896]{1,0:T(8,128)(2,1)S(1)} %get-tuple-element.31), channel_id=1, source_target_pairs={{0,32},{16,48},{32,0},{48,16},{64,96},{80,112},{96,64},{112,80},{1... | collective-permute-start | bytes 1376264 | tf_op jit(solution)/shard_map/ppermute | solution.py:134
  16.6 13.4 %collective-permute-start.1 = (bf16[256,896]{1,0:T(8,128)(2,1)S(1)}, bf16[256,896]{1,0:T(8,128)(2,1)S(1)}, u32[]{:S(2)}, u32[]{:S(2)}) collective-permute-start(bf16[256,896]{1,0:T(8,128)(2,1)S(1)} %get-tuple-element.29), channel_id=1, source_target_pairs={{0,64},{16,80},{32,96},{48,112},{64,0},{80,16},{96,32},{112,48},{1... | collective-permute-start | bytes 1376264 | tf_op jit(solution)/shard_map/ppermute | solution.py:134
  31.1 16.9 %all-to-all-start.1 = ((bf16[4,16,32,256]{3,2,1,0:T(8,128)(2,1)}), bf16[4,16,32,256]{3,2,1,0:T(8,128)(2,1)S(1)}, u32[]{:S(2)}, u32[]{:S(2)}) async-start(bf16[4,16,32,256]{3,2,1,0:T(8,128)(2,1)} %broadcast_in_dim.7), calls=%async_computation.1 | async-start | bytes 2097152 | tf_op jit(solution)/shard_map/all_to_all | solution.py:141
  35.2 12.6 %collective-permute-start.2 = (bf16[256,896]{1,0:T(8,128)(2,1)S(1)}, bf16[256,896]{1,0:T(8,128)(2,1)S(1)}, u32[]{:S(2)}, u32[]{:S(2)}) collective-permute-start(bf16[256,896]{1,0:T(8,128)(2,1)S(1)} %get-tuple-element.28), channel_id=1, source_target_pairs={{0,96},{16,112},{32,64},{48,80},{64,32},{80,48},{96,0},{112,16},{1... | collective-permute-start | bytes 1376264 | tf_op jit(solution)/shard_map/ppermute | solution.py:134
  49.4 6.3 %copy-start = (bf16[512,1024]{1,0:T(8,128)(2,1)}, bf16[512,1024]{1,0:T(8,128)(2,1)S(1)}, u32[]{:S(2)}) copy-start(bf16[512,1024]{1,0:T(8,128)(2,1)S(1)} %get-tuple-element.14.tokens) | copy-start | bytes 3145732
  49.4 7.1 %collective-permute-start.3 = (f32[256,896]{1,0:T(8,128)S(1)}, f32[256,896]{1,0:T(8,128)S(1)}, u32[]{:S(2)}, u32[]{:S(2)}) collective-permute-start(f32[256,896]{1,0:T(8,128)S(1)} %get-tuple-element.15), channel_id=1, source_target_pairs={{0,16},{16,0},{32,48},{48,32},{64,80},{80,64},{96,112},{112,96},{1... | collective-permute-start | bytes 2752520 | tf_op jit(solution)/shard_map/ppermute | solution.py:149
  55.7 10.8 %copy-start.2 = (bf16[16,1792]{1,0:T(8,128)(2,1)S(1)}, bf16[16,1792]{1,0:T(8,128)(2,1)}, u32[]{:S(2)}) copy-start(bf16[16,1792]{1,0:T(8,128)(2,1)} %param.7) | copy-start | bytes 172036
  57.4 25.7 %all-to-all-start.2 = ((bf16[8,32,896]{2,1,0:T(8,128)(2,1)}), bf16[8,32,896]{2,1,0:T(8,128)(2,1)S(1)}, u32[]{:S(2)}, u32[]{:S(2)}) async-start(bf16[8,32,896]{2,1,0:T(8,128)(2,1)} %bitcast.35), calls=%async_computation.2 | async-start | bytes 917504 | tf_op jit(solution)/shard_map/all_to_all | solution.py:152
  66.6 4.9 %collective-permute-start.5 = (bf16[16,896]{1,0:T(8,128)(2,1)S(1)}, bf16[16,896]{1,0:T(8,128)(2,1)S(1)}, u32[]{:S(2)}, u32[]{:S(2)}) collective-permute-start(bf16[16,896]{1,0:T(8,128)(2,1)S(1)} %broadcast_select_fusion.16), channel_id=1, source_target_pairs={{0,32},{16,48},{32,0},{48,16},{64,96},{80,112},{96,64},{112,80},{1... | collective-permute-start | bytes 86024 | tf_op jit(solution)/shard_map/ppermute | solution.py:158
  84.1 20.0 %all-to-all-start.3 = ((bf16[8,32,896]{2,1,0:T(8,128)(2,1)}), bf16[8,32,896]{2,1,0:T(8,128)(2,1)S(1)}, u32[]{:S(2)}, u32[]{:S(2)}) async-start(bf16[8,32,896]{2,1,0:T(8,128)(2,1)} %bitcast.8), calls=%async_computation.3 | async-start | bytes 917504 | tf_op jit(solution)/shard_map/all_to_all | solution.py:165
  87.6 4.9 %collective-permute-start.4 = (bf16[16,896]{1,0:T(8,128)(2,1)S(1)}, bf16[16,896]{1,0:T(8,128)(2,1)S(1)}, u32[]{:S(2)}, u32[]{:S(2)}) collective-permute-start(bf16[16,896]{1,0:T(8,128)(2,1)S(1)} %broadcast_select_fusion.20), channel_id=1, source_target_pairs={{0,32},{16,48},{32,0},{48,16},{64,96},{80,112},{96,64},{112,80},{1... | collective-permute-start | bytes 86024 | tf_op jit(solution)/shard_map/ppermute | solution.py:172
  104.0 3.8 %collective-permute-start.6 = (bf16[256,896]{1,0:T(8,128)(2,1)S(1)}, bf16[256,896]{1,0:T(8,128)(2,1)S(1)}, u32[]{:S(2)}, u32[]{:S(2)}) collective-permute-start(bf16[256,896]{1,0:T(8,128)(2,1)S(1)} %bitcast.32), channel_id=1, source_target_pairs={{0,16},{16,0},{32,48},{48,32},{64,80},{80,64},{96,112},{112,96},{1... | collective-permute-start | bytes 1376264 | tf_op jit(solution)/shard_map/ppermute | solution.py:175
  110.6 4.4 %copy-start.1 = (bf16[512,1024]{1,0:T(8,128)(2,1)S(1)}, bf16[512,1024]{1,0:T(8,128)(2,1)}, u32[]{:S(2)}) copy-start(bf16[512,1024]{1,0:T(8,128)(2,1)} %copy-done) | copy-start | bytes 3145732
  110.6 19.3 %all-to-all-start.4 = ((bf16[4,16,32,256]{3,2,1,0:T(8,128)(2,1)}), bf16[4,16,32,256]{3,2,1,0:T(8,128)(2,1)}, u32[]{:S(2)}, u32[]{:S(2)}) async-start(bf16[4,16,32,256]{3,2,1,0:T(8,128)(2,1)} %bitcast.10), calls=%async_computation.4 | async-start | bytes 2097152 | tf_op jit(solution)/shard_map/all_to_all | solution.py:180
  117.1 15.0 %collective-permute-start.7 = (bf16[256,896]{1,0:T(8,128)(2,1)}, bf16[256,896]{1,0:T(8,128)(2,1)S(1)}, u32[]{:S(2)}, u32[]{:S(2)}) collective-permute-start(bf16[256,896]{1,0:T(8,128)(2,1)} %get-tuple-element.17), channel_id=1, source_target_pairs={{0,32},{16,48},{32,0},{48,16},{64,96},{80,112},{96,64},{112,80},{1... | collective-permute-start | bytes 1376264 | tf_op jit(solution)/shard_map/ppermute | solution.py:186
  119.2 23.4 %collective-permute-start.8 = (bf16[256,896]{1,0:T(8,128)(2,1)S(1)}, bf16[256,896]{1,0:T(8,128)(2,1)S(1)}, u32[]{:S(2)}, u32[]{:S(2)}) collective-permute-start(bf16[256,896]{1,0:T(8,128)(2,1)S(1)} %get-tuple-element.20), channel_id=1, source_target_pairs={{0,64},{16,80},{32,96},{48,112},{64,0},{80,16},{96,32},{112,48},{1... | collective-permute-start | bytes 1376264 | tf_op jit(solution)/shard_map/ppermute | solution.py:186
  121.4 21.2 %collective-permute-start.9 = (bf16[256,896]{1,0:T(8,128)(2,1)S(1)}, bf16[256,896]{1,0:T(8,128)(2,1)S(1)}, u32[]{:S(2)}, u32[]{:S(2)}) collective-permute-start(bf16[256,896]{1,0:T(8,128)(2,1)S(1)} %get-tuple-element.21), channel_id=1, source_target_pairs={{0,96},{16,112},{32,64},{48,80},{64,32},{80,48},{96,0},{112,16},{1... | collective-permute-start | bytes 1376264 | tf_op jit(solution)/shard_map/ppermute | solution.py:186
  132.1 14.7 %all-to-all-start.5 = ((bf16[16,32,256]{2,1,0:T(8,128)(2,1)}), bf16[16,32,256]{2,1,0:T(8,128)(2,1)S(1)}, u32[]{:S(2)}, u32[]{:S(2)}) async-start(bf16[16,32,256]{2,1,0:T(8,128)(2,1)} %reduce_sum.50), calls=%async_computation.5 | async-start | bytes 524288 | tf_op jit(solution)/shard_map/all_to_all | solution.py:189

commit v4 on v3

--- a/solution.py
+++ b/solution.py
@@ -18,6 +18,7 @@
 ]
 
 PARAMS = pltpu.CompilerParams(vmem_limit_bytes=32 * 1024 * 1024)
+MARK_FLOPS = 30_000_000_000
 VMEM = pl.BlockSpec(memory_space=pltpu.VMEM)
 SMEM = pl.BlockSpec(memory_space=pltpu.SMEM)
 
@@ -42,7 +43,11 @@
     return [slice(i, min(i + step, n)) for i in range(0, n, step)]
 
 
-def arrange_and_send(place, raw, w0, w1, w2, w3, tokens, sent):
+def arrived(w1, w2, w3, out):
+    out[...] = jnp.zeros_like(out)
+
+
+def arrange_and_send(place, mark, raw, w0, w1, w2, w3, tokens, sent):
     width = raw.shape[-1]
     half, block = tokens.shape[0] // 2, raw.shape[-2]
     for part in range(2):
@@ -131,21 +136,29 @@
     pieces = by_member(
         [gate_weight[:, :half], gate_weight[:, half:], up_weight[:, :half], up_weight[:, half:]]
     )
-    weights = [pieces[0]] + [lax.ppermute(pieces[k], "dp", QUAD_SWAP[k]) for k in (1, 2, 3)]
+    weights = [lax.ppermute(pieces[k], "dp", QUAD_SWAP[k]) for k in (1, 2, 3)]
+    mark = pl.pallas_call(
+        arrived,
+        out_shape=struct((8, 128), F32),
+        in_specs=[pl.BlockSpec(memory_space=pl.ANY)] * 3,
+        out_specs=VMEM,
+        compiler_params=PARAMS,
+        cost_estimate=pl.CostEstimate(flops=MARK_FLOPS, bytes_accessed=4096, transcendentals=0),
+    )(*weights)
+    weights = [pieces[0], *weights]
 
     raw = lax.all_to_all(
         jnp.broadcast_to(activations[None], (16, rows, width)), ("dp", "tensor"), 0, 0,
         axis_index_groups=QUAD_YHI_GROUPS,
     )
-    raw = after(raw, weights[1], weights[2])
     raw = lax.all_to_all(
         jnp.broadcast_to(raw[None], (4, 16, rows, width)), "tensor", 0, 0, axis_index_groups=X_GROUPS
     )
     raw = raw.reshape(4, 4, 4, 2, block, width)
 
     tokens, sent = call(
-        arrange_and_send, 5, [struct((2 * count, 4 * width)), struct((count, half), F32)], flops
-    )(place, raw, *weights)
+        arrange_and_send, 6, [struct((2 * count, 4 * width)), struct((count, half), F32)], flops
+    )(place, mark, raw, *weights)
     got = lax.ppermute(sent, "dp", CORE_SWAP)
     kept = call(keep_sums, 5, struct((count, half), F32), flops)(place, tokens, *weights)
     part = (kept + got).astype(BF16)

time: 149 us -> 144 us (0.966)
  the two profiles are of different devices: /device:TPU:1 before, /device:TPU:2 now
where the time goes in v4:
time: 144 us; the launch traced here: 143 us
  starting transfers between devices  68.4 us (48%)
  waiting for transfers between devices  53.6 us (37%)
  other arithmetic  8.99 us (6%)
  Pallas kernels  7.44 us (5%)
  local copies, waits for them, and re-layouts  3.39 us (2%)
    ppermute x3, waiting for transfers between devices, per_device(): weights = [lax.ppermute(pieces[k], 'dp', QUAD_SWAP[k]) for k in (1, 2, 3)]  12.1 us
    all_to_all x1, waiting for transfers between devices, per_device(): lax.all_to_all(jnp.broadcast_to(jnp.stack([gate_back, up_back])[None], (4...  10.6 us
    all_to_all x1, waiting for transfers between devices, per_device(): lax.all_to_all(part.reshape(8, 2 * block, half), 'dp', 0, 0, axis_index_g...  10.6 us
    all_to_all x1, starting transfers between devices, per_device(): lax.all_to_all(part.reshape(8, 2 * block, half), 'dp', 0, 0, axis_index_g...  9.57 us
    ppermute x3, starting transfers between devices, per_device(): lax.ppermute(grads[k], 'dp', QUAD_SWAP[k])  9.2 us
    ppermute x3, starting transfers between devices, per_device(): weights = [lax.ppermute(pieces[k], 'dp', QUAD_SWAP[k]) for k in (1, 2, 3)]  9.2 us
    all_to_all x1, starting transfers between devices, per_device(): lax.all_to_all(jnp.broadcast_to(activations[None], (16, rows, width)), ('...  9.01 us
    ppermute x3, waiting for transfers between devices, per_device(): lax.ppermute(grads[k], 'dp', QUAD_SWAP[k])  7.67 us
  transfers between devices with their start and end apart: 16, of which 13 were waited for; matrix products, arithmetic and copies ran while one was open for 6% of the time, Pallas kernels for 2%

profile of v4, /device:TPU:2, one launch (start us, length us, event | category | flops | bytes accessed | tf_op | source)
XLA Modules:
  0.0 142.7 jit_solution(2485650615964677769)
XLA Ops:
  0.6 1.4 %broadcast_in_dim.6 = bf16[16,32,256]{2,1,0:T(8,128)(2,1)} broadcast(bf16[32,256]{1,0:T(8,128)(2,1)} %param.4), dimensions={1,2} | broadcast | bytes 278528 | tf_op jit(solution)/shard_map/broadcast_in_dim | solution.py:151
  2.1 9.0 %all-to-all-start = ((bf16[16,32,256]{2,1,0:T(8,128)(2,1)}), bf16[16,32,256]{2,1,0:T(8,128)(2,1)S(1)}, u32[]{:S(2)}, u32[]{:S(2)}) async-start(bf16[16,32,256]{2,1,0:T(8,128)(2,1)} %broadcast_in_dim.6), calls=%async_computation | async-start | bytes 524288 | tf_op jit(solution)/shard_map/all_to_all | solution.py:150
  11.1 2.8 %broadcast_select_fusion.12 = (bf16[256,896]{1,0:T(8,128)(2,1)S(1)}, bf16[256,896]{1,0:T(8,128)(2,1)}, bf16[256,896]{1,0:T(8,128)(2,1)}, bf16[256,896]{1,0:T(8,128)(2,1)}) fusion(pred[]{:T(512)S(6)} %eq.7, bf16[256,1792]{1,0:T(8,128)(2,1)} %param.6, pred[]{:T(512)S(6)} %eq.6, bf16[256,1792]{1,0:T(8,128)(2,1)} %param.5), kind=kLoop, calls=%fused_computation.17 | loop fusion | flops 1835008 | bytes 3670018 | tf_op jit(solution)/shard_map/jit(_where)/select_n | solution.py:127
  13.9 3.8 %collective-permute-start = (bf16[256,896]{1,0:T(8,128)(2,1)}, bf16[256,896]{1,0:T(8,128)(2,1)S(1)}, u32[]{:S(2)}, u32[]{:S(2)}) collective-permute-start(bf16[256,896]{1,0:T(8,128)(2,1)} %get-tuple-element.29), channel_id=1, source_target_pairs={{0,32},{16,48},{32,0},{48,16},{64,96},{80,112},{96,64},{112,80},{1... | collective-permute-start | bytes 1376264 | tf_op jit(solution)/shard_map/ppermute | solution.py:139
  17.7 3.4 %collective-permute-start.1 = (bf16[256,896]{1,0:T(8,128)(2,1)}, bf16[256,896]{1,0:T(8,128)(2,1)S(1)}, u32[]{:S(2)}, u32[]{:S(2)}) collective-permute-start(bf16[256,896]{1,0:T(8,128)(2,1)} %get-tuple-element.27), channel_id=1, source_target_pairs={{0,64},{16,80},{32,96},{48,112},{64,0},{80,16},{96,32},{112,48},{1... | collective-permute-start | bytes 1376264 | tf_op jit(solution)/shard_map/ppermute | solution.py:139
  21.1 2.0 %collective-permute-start.2 = (bf16[256,896]{1,0:T(8,128)(2,1)}, bf16[256,896]{1,0:T(8,128)(2,1)S(1)}, u32[]{:S(2)}, u32[]{:S(2)}) collective-permute-start(bf16[256,896]{1,0:T(8,128)(2,1)} %get-tuple-element.28), channel_id=1, source_target_pairs={{0,96},{16,112},{32,64},{48,80},{64,32},{80,48},{96,0},{112,16},{1... | collective-permute-start | bytes 1376264 | tf_op jit(solution)/shard_map/ppermute | solution.py:139
  23.1 0.1 pad_add_fusion.place
  23.2 0.0 all-to-all-done
  23.2 1.1 broadcast_in_dim.7
  24.3 4.8 %all-to-all-start.1 = ((bf16[4,16,32,256]{3,2,1,0:T(8,128)(2,1)}), bf16[4,16,32,256]{3,2,1,0:T(8,128)(2,1)S(1)}, u32[]{:S(2)}, u32[]{:S(2)}) async-start(bf16[4,16,32,256]{3,2,1,0:T(8,128)(2,1)} %broadcast_in_dim.7), calls=%async_computation.1 | async-start | bytes 2097152 | tf_op jit(solution)/shard_map/all_to_all | solution.py:154
  29.1 0.3 collective-permute-done.w1
  29.4 11.8 %collective-permute-done.1.w2 = bf16[256,896]{1,0:T(8,128)(2,1)S(1)} collective-permute-done((bf16[256,896]{1,0:T(8,128)(2,1)}, bf16[256,896]{1,0:T(8,128)(2,1)S(1)}, u32[]{:S(2)}, u32[]{:S(2)}) %collective-permute-start.1) | collective-permute-done | bytes 458784 | tf_op jit(solution)/shard_map/ppermute | solution.py:139
  41.2 0.0 collective-permute-done.2.w3
  41.2 0.5 all-to-all-done.1
  41.7 1.3 shard_map.76
  43.0 0.0 copy-start
  43.0 1.9 %collective-permute-start.3 = (f32[256,896]{1,0:T(8,128)S(1)}, f32[256,896]{1,0:T(8,128)S(1)}, u32[]{:S(2)}, u32[]{:S(2)}) collective-permute-start(f32[256,896]{1,0:T(8,128)S(1)} %get-tuple-element.13), channel_id=1, source_target_pairs={{0,16},{16,0},{32,48},{48,32},{64,80},{80,64},{96,112},{112,96},{1... | collective-permute-start | bytes 2752520 | tf_op jit(solution)/shard_map/ppermute | solution.py:162
  44.9 1.2 shard_map.77
  46.2 0.0 copy-done
  46.2 0.0 copy-start.2
  46.2 1.2 collective-permute-done.3
  47.4 0.9 add_convert_fusion
  48.2 9.6 %all-to-all-start.2 = ((bf16[8,32,896]{2,1,0:T(8,128)(2,1)}), bf16[8,32,896]{2,1,0:T(8,128)(2,1)S(1)}, u32[]{:S(2)}, u32[]{:S(2)}) async-start(bf16[8,32,896]{2,1,0:T(8,128)(2,1)} %bitcast.35), calls=%async_computation.2 | async-start | bytes 917504 | tf_op jit(solution)/shard_map/all_to_all | solution.py:165
  57.8 0.0 copy-done.2
  57.8 3.4 %collective-permute-start.5 = (bf16[16,896]{1,0:T(8,128)(2,1)S(1)}, bf16[16,896]{1,0:T(8,128)(2,1)S(1)}, u32[]{:S(2)}, u32[]{:S(2)}) collective-permute-start(bf16[16,896]{1,0:T(8,128)(2,1)S(1)} %broadcast_select_fusion.16), channel_id=1, source_target_pairs={{0,32},{16,48},{32,0},{48,16},{64,96},{80,112},{96,64},{112,80},{1... | collective-permute-start | bytes 86024 | tf_op jit(solution)/shard_map/ppermute | solution.py:171
  61.2 2.4 %collective-permute-done.5 = bf16[16,896]{1,0:T(8,128)(2,1)S(1)} collective-permute-done((bf16[16,896]{1,0:T(8,128)(2,1)S(1)}, bf16[16,896]{1,0:T(8,128)(2,1)S(1)}, u32[]{:S(2)}, u32[]{:S(2)}) %collective-permute-start.5) | collective-permute-done | bytes 28704 | tf_op jit(solution)/shard_map/ppermute | solution.py:171
  63.6 10.6 %all-to-all-done.2 = bf16[8,32,896]{2,1,0:T(8,128)(2,1)S(1)} async-done(((bf16[8,32,896]{2,1,0:T(8,128)(2,1)}), bf16[8,32,896]{2,1,0:T(8,128)(2,1)S(1)}, u32[]{:S(2)}, u32[]{:S(2)}) %all-to-all-start.2) | async-done | bytes 458784 | tf_op jit(solution)/shard_map/all_to_all | solution.py:165
  74.2 0.1 convert_reduce_fusion.1
  74.2 0.1 fusion.2
  74.3 0.8 broadcast_in_dim.8
  75.1 3.5 %all-to-all-start.3 = ((bf16[8,32,896]{2,1,0:T(8,128)(2,1)}), bf16[8,32,896]{2,1,0:T(8,128)(2,1)S(1)}, u32[]{:S(2)}, u32[]{:S(2)}) async-start(bf16[8,32,896]{2,1,0:T(8,128)(2,1)} %bitcast.8), calls=%async_computation.3 | async-start | bytes 917504 | tf_op jit(solution)/shard_map/all_to_all | solution.py:178
  78.7 3.4 %collective-permute-start.4 = (bf16[16,896]{1,0:T(8,128)(2,1)S(1)}, bf16[16,896]{1,0:T(8,128)(2,1)S(1)}, u32[]{:S(2)}, u32[]{:S(2)}) collective-permute-start(bf16[16,896]{1,0:T(8,128)(2,1)S(1)} %broadcast_select_fusion.20), channel_id=1, source_target_pairs={{0,32},{16,48},{32,0},{48,16},{64,96},{80,112},{96,64},{112,80},{1... | collective-permute-start | bytes 86024 | tf_op jit(solution)/shard_map/ppermute | solution.py:185
  82.1 2.4 %collective-permute-done.4 = bf16[16,896]{1,0:T(8,128)(2,1)S(1)} collective-permute-done((bf16[16,896]{1,0:T(8,128)(2,1)S(1)}, bf16[16,896]{1,0:T(8,128)(2,1)S(1)}, u32[]{:S(2)}, u32[]{:S(2)}) %collective-permute-start.4) | collective-permute-done | bytes 28704 | tf_op jit(solution)/shard_map/ppermute | solution.py:185
  84.5 10.6 %all-to-all-done.3 = bf16[8,32,896]{2,1,0:T(8,128)(2,1)S(1)} async-done(((bf16[8,32,896]{2,1,0:T(8,128)(2,1)}), bf16[8,32,896]{2,1,0:T(8,128)(2,1)S(1)}, u32[]{:S(2)}, u32[]{:S(2)}) %all-to-all-start.3) | async-done | bytes 458784 | tf_op jit(solution)/shard_map/all_to_all | solution.py:178
  95.1 1.9 %collective-permute-start.6 = (bf16[256,896]{1,0:T(8,128)(2,1)S(1)}, bf16[256,896]{1,0:T(8,128)(2,1)S(1)}, u32[]{:S(2)}, u32[]{:S(2)}) collective-permute-start(bf16[256,896]{1,0:T(8,128)(2,1)S(1)} %bitcast.32), channel_id=1, source_target_pairs={{0,16},{16,0},{32,48},{48,32},{64,80},{80,64},{96,112},{112,96},{1... | collective-permute-start | bytes 1376264 | tf_op jit(solution)/shard_map/ppermute | solution.py:188
  97.0 1.8 %collective-permute-done.6.other = bf16[256,896]{1,0:T(8,128)(2,1)S(1)} collective-permute-done((bf16[256,896]{1,0:T(8,128)(2,1)S(1)}, bf16[256,896]{1,0:T(8,128)(2,1)S(1)}, u32[]{:S(2)}, u32[]{:S(2)}) %collective-permute-start.6) | collective-permute-done | bytes 458784 | tf_op jit(solution)/shard_map/ppermute | solution.py:188
  98.8 2.8 %shard_map.78 = bf16[4,4,4,2,16,256]{5,4,3,2,1,0:T(8,128)(2,1)} custom-call(s32[2]{0:T(128)S(1)} %pad_add_fusion.place, bf16[256,896]{1,0:T(8,128)(2,1)S(1)} %bitcast.33, bf16[256,896]{1,0:T(8,128)(2,1)S(1)} %collective-permute-done.6.other, bf16[256,896]{1,0:T(8,128)(2,1)S(1)} %get-tuple-element.26.w0, bf16[256,896]{1,0:T(8,128)(2,1)S(1)} %collective-permute-done.w1, ...), custom_call_target="tpu_custom_call" | custom-call | flops 939524096 | bytes 4194304 | tf_op jit(solution)/shard_map/pallas_call | solution.py:190
  101.6 0.0 copy-start.1
  101.6 5.8 %all-to-all-start.4 = ((bf16[4,16,32,256]{3,2,1,0:T(8,128)(2,1)}), bf16[4,16,32,256]{3,2,1,0:T(8,128)(2,1)}, u32[]{:S(2)}, u32[]{:S(2)}) async-start(bf16[4,16,32,256]{3,2,1,0:T(8,128)(2,1)} %bitcast.10), calls=%async_computation.4 | async-start | bytes 2097152 | tf_op jit(solution)/shard_map/all_to_all | solution.py:193
  107.4 0.0 copy-done.1
  107.4 2.1 %shard_map.79 = (bf16[256,896]{1,0:T(8,128)(2,1)S(1)}, bf16[256,896]{1,0:T(8,128)(2,1)}, bf16[256,896]{1,0:T(8,128)(2,1)S(1)}, bf16[256,896]{1,0:T(8,128)(2,1)S(1)}) custom-call(s32[2]{0:T(128)S(1)} %pad_add_fusion.place, bf16[512,1024]{1,0:T(8,128)(2,1)S(1)} %copy-done.1, bf16[256,896]{1,0:T(8,128)(2,1)S(1)} %bitcast.34, ...), custom_call_target="tpu_custom_call" | custom-call | flops 939524096 | bytes 4194304 | tf_op jit(solution)/shard_map/pallas_call | solution.py:198
  109.5 3.4 %collective-permute-start.7 = (bf16[256,896]{1,0:T(8,128)(2,1)}, bf16[256,896]{1,0:T(8,128)(2,1)S(1)}, u32[]{:S(2)}, u32[]{:S(2)}) collective-permute-start(bf16[256,896]{1,0:T(8,128)(2,1)} %get-tuple-element.15), channel_id=1, source_target_pairs={{0,32},{16,48},{32,0},{48,16},{64,96},{80,112},{96,64},{112,80},{1... | collective-permute-start | bytes 1376264 | tf_op jit(solution)/shard_map/ppermute | solution.py:199
  112.8 2.5 %collective-permute-start.8 = (bf16[256,896]{1,0:T(8,128)(2,1)S(1)}, bf16[256,896]{1,0:T(8,128)(2,1)S(1)}, u32[]{:S(2)}, u32[]{:S(2)}) collective-permute-start(bf16[256,896]{1,0:T(8,128)(2,1)S(1)} %get-tuple-element.18), channel_id=1, source_target_pairs={{0,64},{16,80},{32,96},{48,112},{64,0},{80,16},{96,32},{112,48},{1... | collective-permute-start | bytes 1376264 | tf_op jit(solution)/shard_map/ppermute | solution.py:199
  115.3 3.4 %collective-permute-start.9 = (bf16[256,896]{1,0:T(8,128)(2,1)S(1)}, bf16[256,896]{1,0:T(8,128)(2,1)S(1)}, u32[]{:S(2)}, u32[]{:S(2)}) collective-permute-start(bf16[256,896]{1,0:T(8,128)(2,1)S(1)} %get-tuple-element.19), channel_id=1, source_target_pairs={{0,96},{16,112},{32,64},{48,80},{64,32},{80,48},{96,0},{112,16},{1... | collective-permute-start | bytes 1376264 | tf_op jit(solution)/shard_map/ppermute | solution.py:199
  118.7 0.6 pad_maximum_fusion.3
  119.3 2.4 %all-to-all-done.4 = bf16[4,16,32,256]{3,2,1,0:T(8,128)(2,1)} async-done(((bf16[4,16,32,256]{3,2,1,0:T(8,128)(2,1)}), bf16[4,16,32,256]{3,2,1,0:T(8,128)(2,1)}, u32[]{:S(2)}, u32[]{:S(2)}) %all-to-all-start.4) | async-done | bytes 1048608 | tf_op jit(solution)/shard_map/all_to_all | solution.py:193
  121.7 2.2 %reduce_sum.50 = bf16[16,32,256]{2,1,0:T(8,128)(2,1)} reduce(bf16[4,16,32,256]{3,2,1,0:T(8,128)(2,1)} %all-to-all-done.4, bf16[]{:T(256)} %constant.18.clone.1), dimensions={0}, to_apply=%region_2.3 | reduce | flops 393216 | bytes 1310722 | tf_op jit(solution)/shard_map/reduce_sum | solution.py:196
  123.9 1.1 collective-permute-done.7
  125.0 6.8 %all-to-all-start.5 = ((bf16[16,32,256]{2,1,0:T(8,128)(2,1)}), bf16[16,32,256]{2,1,0:T(8,128)(2,1)S(1)}, u32[]{:S(2)}, u32[]{:S(2)}) async-start(bf16[16,32,256]{2,1,0:T(8,128)(2,1)} %reduce_sum.50), calls=%async_computation.5 | async-start | bytes 524288 | tf_op jit(solution)/shard_map/all_to_all | solution.py:202
  131.7 6.6 %collective-permute-done.8 = bf16[256,896]{1,0:T(8,128)(2,1)S(1)} collective-permute-done((bf16[256,896]{1,0:T(8,128)(2,1)S(1)}, bf16[256,896]{1,0:T(8,128)(2,1)S(1)}, u32[]{:S(2)}, u32[]{:S(2)}) %collective-permute-start.8) | collective-permute-done | bytes 458784 | tf_op jit(solution)/shard_map/ppermute | solution.py:199
  138.3 0.0 collective-permute-done.9
  138.3 0.2 broadcast_select_fusion.9
  138.6 1.4 pad_maximum_fusion
  139.9 2.1 %all-to-all-done.5 = bf16[16,32,256]{2,1,0:T(8,128)(2,1)S(1)} async-done(((bf16[16,32,256]{2,1,0:T(8,128)(2,1)}), bf16[16,32,256]{2,1,0:T(8,128)(2,1)S(1)}, u32[]{:S(2)}, u32[]{:S(2)}) %all-to-all-start.5) | async-done | bytes 262176 | tf_op jit(solution)/shard_map/all_to_all | solution.py:202
  142.0 0.6 reduce_sum.51
  (7 shorter events, 0.1 us)
Async XLA Ops:
  2.1 21.1 %all-to-all-start = ((bf16[16,32,256]{2,1,0:T(8,128)(2,1)}), bf16[16,32,256]{2,1,0:T(8,128)(2,1)S(1)}, u32[]{:S(2)}, u32[]{:S(2)}) async-start(bf16[16,32,256]{2,1,0:T(8,128)(2,1)} %broadcast_in_dim.6), calls=%async_computation | async-start | bytes 524288 | tf_op jit(solution)/shard_map/all_to_all | solution.py:150
  13.9 15.5 %collective-permute-start = (bf16[256,896]{1,0:T(8,128)(2,1)}, bf16[256,896]{1,0:T(8,128)(2,1)S(1)}, u32[]{:S(2)}, u32[]{:S(2)}) collective-permute-start(bf16[256,896]{1,0:T(8,128)(2,1)} %get-tuple-element.29), channel_id=1, source_target_pairs={{0,32},{16,48},{32,0},{48,16},{64,96},{80,112},{96,64},{112,80},{1... | collective-permute-start | bytes 1376264 | tf_op jit(solution)/shard_map/ppermute | solution.py:139
  17.7 23.5 %collective-permute-start.1 = (bf16[256,896]{1,0:T(8,128)(2,1)}, bf16[256,896]{1,0:T(8,128)(2,1)S(1)}, u32[]{:S(2)}, u32[]{:S(2)}) collective-permute-start(bf16[256,896]{1,0:T(8,128)(2,1)} %get-tuple-element.27), channel_id=1, source_target_pairs={{0,64},{16,80},{32,96},{48,112},{64,0},{80,16},{96,32},{112,48},{1... | collective-permute-start | bytes 1376264 | tf_op jit(solution)/shard_map/ppermute | solution.py:139
  21.1 20.1 %collective-permute-start.2 = (bf16[256,896]{1,0:T(8,128)(2,1)}, bf16[256,896]{1,0:T(8,128)(2,1)S(1)}, u32[]{:S(2)}, u32[]{:S(2)}) collective-permute-start(bf16[256,896]{1,0:T(8,128)(2,1)} %get-tuple-element.28), channel_id=1, source_target_pairs={{0,96},{16,112},{32,64},{48,80},{64,32},{80,48},{96,0},{112,16},{1... | collective-permute-start | bytes 1376264 | tf_op jit(solution)/shard_map/ppermute | solution.py:139
  24.3 17.3 %all-to-all-start.1 = ((bf16[4,16,32,256]{3,2,1,0:T(8,128)(2,1)}), bf16[4,16,32,256]{3,2,1,0:T(8,128)(2,1)S(1)}, u32[]{:S(2)}, u32[]{:S(2)}) async-start(bf16[4,16,32,256]{3,2,1,0:T(8,128)(2,1)} %broadcast_in_dim.7), calls=%async_computation.1 | async-start | bytes 2097152 | tf_op jit(solution)/shard_map/all_to_all | solution.py:154
  43.0 3.2 %copy-start = (bf16[512,1024]{1,0:T(8,128)(2,1)}, bf16[512,1024]{1,0:T(8,128)(2,1)S(1)}, u32[]{:S(2)}) copy-start(bf16[512,1024]{1,0:T(8,128)(2,1)S(1)} %get-tuple-element.12.tokens) | copy-start | bytes 3145732
  43.0 4.4 %collective-permute-start.3 = (f32[256,896]{1,0:T(8,128)S(1)}, f32[256,896]{1,0:T(8,128)S(1)}, u32[]{:S(2)}, u32[]{:S(2)}) collective-permute-start(f32[256,896]{1,0:T(8,128)S(1)} %get-tuple-element.13), channel_id=1, source_target_pairs={{0,16},{16,0},{32,48},{48,32},{64,80},{80,64},{96,112},{112,96},{1... | collective-permute-start | bytes 2752520 | tf_op jit(solution)/shard_map/ppermute | solution.py:162
  46.2 11.6 %copy-start.2 = (bf16[16,1792]{1,0:T(8,128)(2,1)S(1)}, bf16[16,1792]{1,0:T(8,128)(2,1)}, u32[]{:S(2)}) copy-start(bf16[16,1792]{1,0:T(8,128)(2,1)} %param.7) | copy-start | bytes 172036
  48.2 26.0 %all-to-all-start.2 = ((bf16[8,32,896]{2,1,0:T(8,128)(2,1)}), bf16[8,32,896]{2,1,0:T(8,128)(2,1)S(1)}, u32[]{:S(2)}, u32[]{:S(2)}) async-start(bf16[8,32,896]{2,1,0:T(8,128)(2,1)} %bitcast.35), calls=%async_computation.2 | async-start | bytes 917504 | tf_op jit(solution)/shard_map/all_to_all | solution.py:165
  57.8 5.8 %collective-permute-start.5 = (bf16[16,896]{1,0:T(8,128)(2,1)S(1)}, bf16[16,896]{1,0:T(8,128)(2,1)S(1)}, u32[]{:S(2)}, u32[]{:S(2)}) collective-permute-start(bf16[16,896]{1,0:T(8,128)(2,1)S(1)} %broadcast_select_fusion.16), channel_id=1, source_target_pairs={{0,32},{16,48},{32,0},{48,16},{64,96},{80,112},{96,64},{112,80},{1... | collective-permute-start | bytes 86024 | tf_op jit(solution)/shard_map/ppermute | solution.py:171
  75.1 19.9 %all-to-all-start.3 = ((bf16[8,32,896]{2,1,0:T(8,128)(2,1)}), bf16[8,32,896]{2,1,0:T(8,128)(2,1)S(1)}, u32[]{:S(2)}, u32[]{:S(2)}) async-start(bf16[8,32,896]{2,1,0:T(8,128)(2,1)} %bitcast.8), calls=%async_computation.3 | async-start | bytes 917504 | tf_op jit(solution)/shard_map/all_to_all | solution.py:178
  78.7 5.8 %collective-permute-start.4 = (bf16[16,896]{1,0:T(8,128)(2,1)S(1)}, bf16[16,896]{1,0:T(8,128)(2,1)S(1)}, u32[]{:S(2)}, u32[]{:S(2)}) collective-permute-start(bf16[16,896]{1,0:T(8,128)(2,1)S(1)} %broadcast_select_fusion.20), channel_id=1, source_target_pairs={{0,32},{16,48},{32,0},{48,16},{64,96},{80,112},{96,64},{112,80},{1... | collective-permute-start | bytes 86024 | tf_op jit(solution)/shard_map/ppermute | solution.py:185
  95.1 3.7 %collective-permute-start.6 = (bf16[256,896]{1,0:T(8,128)(2,1)S(1)}, bf16[256,896]{1,0:T(8,128)(2,1)S(1)}, u32[]{:S(2)}, u32[]{:S(2)}) collective-permute-start(bf16[256,896]{1,0:T(8,128)(2,1)S(1)} %bitcast.32), channel_id=1, source_target_pairs={{0,16},{16,0},{32,48},{48,32},{64,80},{80,64},{96,112},{112,96},{1... | collective-permute-start | bytes 1376264 | tf_op jit(solution)/shard_map/ppermute | solution.py:188
  101.6 5.8 %copy-start.1 = (bf16[512,1024]{1,0:T(8,128)(2,1)S(1)}, bf16[512,1024]{1,0:T(8,128)(2,1)}, u32[]{:S(2)}) copy-start(bf16[512,1024]{1,0:T(8,128)(2,1)} %copy-done) | copy-start | bytes 3145732
  101.6 20.1 %all-to-all-start.4 = ((bf16[4,16,32,256]{3,2,1,0:T(8,128)(2,1)}), bf16[4,16,32,256]{3,2,1,0:T(8,128)(2,1)}, u32[]{:S(2)}, u32[]{:S(2)}) async-start(bf16[4,16,32,256]{3,2,1,0:T(8,128)(2,1)} %bitcast.10), calls=%async_computation.4 | async-start | bytes 2097152 | tf_op jit(solution)/shard_map/all_to_all | solution.py:193
  109.5 15.5 %collective-permute-start.7 = (bf16[256,896]{1,0:T(8,128)(2,1)}, bf16[256,896]{1,0:T(8,128)(2,1)S(1)}, u32[]{:S(2)}, u32[]{:S(2)}) collective-permute-start(bf16[256,896]{1,0:T(8,128)(2,1)} %get-tuple-element.15), channel_id=1, source_target_pairs={{0,32},{16,48},{32,0},{48,16},{64,96},{80,112},{96,64},{112,80},{1... | collective-permute-start | bytes 1376264 | tf_op jit(solution)/shard_map/ppermute | solution.py:199
  112.8 25.5 %collective-permute-start.8 = (bf16[256,896]{1,0:T(8,128)(2,1)S(1)}, bf16[256,896]{1,0:T(8,128)(2,1)S(1)}, u32[]{:S(2)}, u32[]{:S(2)}) collective-permute-start(bf16[256,896]{1,0:T(8,128)(2,1)S(1)} %get-tuple-element.18), channel_id=1, source_target_pairs={{0,64},{16,80},{32,96},{48,112},{64,0},{80,16},{96,32},{112,48},{1... | collective-permute-start | bytes 1376264 | tf_op jit(solution)/shard_map/ppermute | solution.py:199
  115.3 23.0 %collective-permute-start.9 = (bf16[256,896]{1,0:T(8,128)(2,1)S(1)}, bf16[256,896]{1,0:T(8,128)(2,1)S(1)}, u32[]{:S(2)}, u32[]{:S(2)}) collective-permute-start(bf16[256,896]{1,0:T(8,128)(2,1)S(1)} %get-tuple-element.19), channel_id=1, source_target_pairs={{0,96},{16,112},{32,64},{48,80},{64,32},{80,48},{96,0},{112,16},{1... | collective-permute-start | bytes 1376264 | tf_op jit(solution)/shard_map/ppermute | solution.py:199
  125.0 17.1 %all-to-all-start.5 = ((bf16[16,32,256]{2,1,0:T(8,128)(2,1)}), bf16[16,32,256]{2,1,0:T(8,128)(2,1)S(1)}, u32[]{:S(2)}, u32[]{:S(2)}) async-start(bf16[16,32,256]{2,1,0:T(8,128)(2,1)} %reduce_sum.50), calls=%async_computation.5 | async-start | bytes 524288 | tf_op jit(solution)/shard_map/all_to_all | solution.py:202

commit v5 on v4

--- a/solution.py
+++ b/solution.py
@@ -27,12 +27,12 @@
     return jax.ShapeDtypeStruct(shape, dtype)
 
 
-def call(kernel, n_in, out_shape, flops):
+def call(kernel, n_in, out_shape, flops, first=SMEM):
     many = isinstance(out_shape, list)
     return pl.pallas_call(
         kernel,
         out_shape=out_shape,
-        in_specs=[SMEM] + [VMEM] * n_in,
+        in_specs=[first] + [VMEM] * n_in,
         out_specs=[VMEM] * len(out_shape) if many else VMEM,
         compiler_params=PARAMS,
         cost_estimate=pl.CostEstimate(flops=flops, bytes_accessed=4 << 20, transcendentals=0),
@@ -43,7 +43,8 @@
     return [slice(i, min(i + step, n)) for i in range(0, n, step)]
 
 
-def arrived(w1, w2, w3, out):
+def arrived(*refs):
+    out = refs[-1]
     out[...] = jnp.zeros_like(out)
 
 
@@ -65,7 +66,7 @@
                 tokens[half:, k * width : (k + 1) * width], w[:, s], preferred_element_type=F32
             )
             total = term if total is None else total + term
-        sent[:, s] = total
+        sent[:, s] = total.astype(BF16)
 
 
 def keep_sums(place, tokens, w0, w1, w2, w3, out):
@@ -108,6 +109,11 @@
             out[:, s] = term.astype(BF16)
 
 
+def sum_first(x, out):
+    terms = [x[i].astype(F32) for i in range(x.shape[0])]
+    out[...] = ((terms[0] + terms[1]) + (terms[2] + terms[3])).astype(BF16)
+
+
 def after(x, *others):
     return lax.optimization_barrier((x, *others))[0]
 
@@ -133,35 +139,37 @@
     def pair(mine, other):
         return pick(y0, mine, other), pick(y0, other, mine)
 
-    pieces = by_member(
-        [gate_weight[:, :half], gate_weight[:, half:], up_weight[:, :half], up_weight[:, half:]]
-    )
-    weights = [lax.ppermute(pieces[k], "dp", QUAD_SWAP[k]) for k in (1, 2, 3)]
+    def pieces(gate, up):
+        return by_member([gate[:, :half], gate[:, half:], up[:, :half], up[:, half:]])
+
+    sends = pieces(gate_weight, up_weight)
+    weights = [lax.ppermute(sends[k], "dp", QUAD_SWAP[k]) for k in (1, 2, 3)]
     mark = pl.pallas_call(
         arrived,
         out_shape=struct((8, 128), F32),
-        in_specs=[pl.BlockSpec(memory_space=pl.ANY)] * 3,
+        in_specs=[pl.BlockSpec(memory_space=pl.ANY)] * 2,
         out_specs=VMEM,
         compiler_params=PARAMS,
         cost_estimate=pl.CostEstimate(flops=MARK_FLOPS, bytes_accessed=4096, transcendentals=0),
-    )(*weights)
-    weights = [pieces[0], *weights]
+    )(*weights[:2])
 
     raw = lax.all_to_all(
         jnp.broadcast_to(activations[None], (16, rows, width)), ("dp", "tensor"), 0, 0,
         axis_index_groups=QUAD_YHI_GROUPS,
     )
+    raw, gate, up = lax.optimization_barrier((raw, gate_weight, up_weight))
+    weights = [pieces(gate, up)[0], *weights]
     raw = lax.all_to_all(
         jnp.broadcast_to(raw[None], (4, 16, rows, width)), "tensor", 0, 0, axis_index_groups=X_GROUPS
     )
     raw = raw.reshape(4, 4, 4, 2, block, width)
 
     tokens, sent = call(
-        arrange_and_send, 6, [struct((2 * count, 4 * width)), struct((count, half), F32)], flops
+        arrange_and_send, 6, [struct((2 * count, 4 * width)), struct((count, half))], flops
     )(place, mark, raw, *weights)
     got = lax.ppermute(sent, "dp", CORE_SWAP)
     kept = call(keep_sums, 5, struct((count, half), F32), flops)(place, tokens, *weights)
-    part = (kept + got).astype(BF16)
+    part = (kept + got.astype(F32)).astype(BF16)
     part = lax.all_to_all(part.reshape(8, 2 * block, half), "dp", 0, 0, axis_index_groups=Z_GROUPS)
     gate_pre = jnp.sum(part[0::2].astype(F32), 0)
     up_pre = jnp.sum(part[1::2].astype(F32), 0)
@@ -193,12 +201,11 @@
     total = lax.all_to_all(
         total.reshape(4, 16, rows, width), "tensor", 0, 0, axis_index_groups=X_GROUPS
     )
-    total = jnp.sum(total.astype(F32), 0).astype(BF16)
+    total = call(sum_first, 0, struct((16, rows, width)), 1 << 20, VMEM)(total)
 
     grads = call(weight_parts, 3, [struct((width, half))] * 4, 2 * flops)(place, tokens, own, other)
     grads = [grads[0]] + [lax.ppermute(grads[k], "dp", QUAD_SWAP[k]) for k in (1, 2, 3)]
 
-    total = after(total, grads[1])
     total = lax.all_to_all(total, ("dp", "tensor"), 0, 0, axis_index_groups=QUAD_YHI_GROUPS)
     input_grad = jnp.sum(total.astype(F32), 0).astype(BF16)
 

time: 144 us -> 142 us (0.986)
  the two profiles are of different devices: /device:TPU:2 before, /device:TPU:1 now
where the time goes in v5:
time: 142 us; the launch traced here: 140 us
  starting transfers between devices  66.7 us (47%)
  waiting for transfers between devices  53.7 us (38%)
  Pallas kernels  8.85 us (6%)
  other arithmetic  6.69 us (5%)
  local copies, waits for them, and re-layouts  3.4 us (2%)
    ppermute x3, waiting for transfers between devices, per_device(): weights = [lax.ppermute(sends[k], 'dp', QUAD_SWAP[k]) for k in (1, 2, 3)]  11.9 us
    all_to_all x1, waiting for transfers between devices, per_device(): lax.all_to_all(part.reshape(8, 2 * block, half), 'dp', 0, 0, axis_index_g...  11.6 us
    all_to_all x1, waiting for transfers between devices, per_device(): lax.all_to_all(jnp.broadcast_to(jnp.stack([gate_back, up_back])[None], (4...  11.5 us
    all_to_all x1, starting transfers between devices, per_device(): lax.all_to_all(jnp.broadcast_to(activations[None], (16, rows, width)), ('...  9.56 us
    all_to_all x1, starting transfers between devices, per_device(): lax.all_to_all(part.reshape(8, 2 * block, half), 'dp', 0, 0, axis_index_g...  9.3 us
    ppermute x3, starting transfers between devices, per_device(): weights = [lax.ppermute(sends[k], 'dp', QUAD_SWAP[k]) for k in (1, 2, 3)]  8.36 us
    ppermute x3, starting transfers between devices, per_device(): lax.ppermute(grads[k], 'dp', QUAD_SWAP[k])  8.36 us
    ppermute x3, waiting for transfers between devices, per_device(): lax.ppermute(grads[k], 'dp', QUAD_SWAP[k])  8.33 us
  transfers between devices with their start and end apart: 16, of which 13 were waited for; matrix products, arithmetic and copies ran while one was open for 4% of the time, Pallas kernels for 3%

profile of v5, /device:TPU:1, one launch (start us, length us, event | category | flops | bytes accessed | tf_op | source)
XLA Modules:
  0.0 140.2 jit_solution(6507075509470100631)
XLA Ops:
  0.6 1.4 %broadcast_in_dim.6 = bf16[16,32,256]{2,1,0:T(8,128)(2,1)} broadcast(bf16[32,256]{1,0:T(8,128)(2,1)} %param.4), dimensions={1,2} | broadcast | bytes 278528 | tf_op jit(solution)/shard_map/broadcast_in_dim | solution.py:157
  2.1 9.6 %all-to-all-start = ((bf16[16,32,256]{2,1,0:T(8,128)(2,1)}), bf16[16,32,256]{2,1,0:T(8,128)(2,1)S(1)}, u32[]{:S(2)}, u32[]{:S(2)}) async-start(bf16[16,32,256]{2,1,0:T(8,128)(2,1)} %broadcast_in_dim.6), calls=%async_computation | async-start | bytes 524288 | tf_op jit(solution)/shard_map/all_to_all | solution.py:156
  11.7 2.5 %broadcast_select_fusion.10 = (bf16[256,896]{1,0:T(8,128)(2,1)}, bf16[256,896]{1,0:T(8,128)(2,1)S(1)}, bf16[256,896]{1,0:T(8,128)(2,1)}) fusion(pred[]{:T(512)S(6)} %eq.7, bf16[256,1792]{1,0:T(8,128)(2,1)} %param.5, pred[]{:T(512)S(6)} %eq.6, bf16[256,1792]{1,0:T(8,128)(2,1)} %param.6), kind=kLoop, calls=%fused_computation.17 | loop fusion | flops 1605632 | bytes 3211266 | tf_op jit(solution)/shard_map/jit(_where)/select_n | solution.py:133
  14.2 3.2 %collective-permute-start = (bf16[256,896]{1,0:T(8,128)(2,1)}, bf16[256,896]{1,0:T(8,128)(2,1)S(1)}, u32[]{:S(2)}, u32[]{:S(2)}) collective-permute-start(bf16[256,896]{1,0:T(8,128)(2,1)} %get-tuple-element.32), channel_id=1, source_target_pairs={{0,32},{16,48},{32,0},{48,16},{64,96},{80,112},{96,64},{112,80},{1... | collective-permute-start | bytes 1376264 | tf_op jit(solution)/shard_map/ppermute | solution.py:146
  17.5 3.1 %collective-permute-start.1 = (bf16[256,896]{1,0:T(8,128)(2,1)S(1)}, bf16[256,896]{1,0:T(8,128)(2,1)S(1)}, u32[]{:S(2)}, u32[]{:S(2)}) collective-permute-start(bf16[256,896]{1,0:T(8,128)(2,1)S(1)} %get-tuple-element.31), channel_id=1, source_target_pairs={{0,64},{16,80},{32,96},{48,112},{64,0},{80,16},{96,32},{112,48},{1... | collective-permute-start | bytes 1376264 | tf_op jit(solution)/shard_map/ppermute | solution.py:146
  20.6 2.0 %collective-permute-start.2 = (bf16[256,896]{1,0:T(8,128)(2,1)}, bf16[256,896]{1,0:T(8,128)(2,1)S(1)}, u32[]{:S(2)}, u32[]{:S(2)}) collective-permute-start(bf16[256,896]{1,0:T(8,128)(2,1)} %get-tuple-element.30), channel_id=1, source_target_pairs={{0,96},{16,112},{32,64},{48,80},{64,32},{80,48},{96,0},{112,16},{1... | collective-permute-start | bytes 1376264 | tf_op jit(solution)/shard_map/ppermute | solution.py:146
  22.6 0.1 pad_add_fusion.place
  22.7 0.0 all-to-all-done
  22.7 1.1 broadcast_in_dim.7
  23.8 4.0 %all-to-all-start.1 = ((bf16[4,16,32,256]{3,2,1,0:T(8,128)(2,1)}), bf16[4,16,32,256]{3,2,1,0:T(8,128)(2,1)S(1)}, u32[]{:S(2)}, u32[]{:S(2)}) async-start(bf16[4,16,32,256]{3,2,1,0:T(8,128)(2,1)} %broadcast_in_dim.7), calls=%async_computation.1 | async-start | bytes 2097152 | tf_op jit(solution)/shard_map/all_to_all | solution.py:162
  27.8 0.0 copy-start.2
  27.8 0.0 copy-start.3
  27.8 1.6 %collective-permute-done.refs_0_.w1 = bf16[256,896]{1,0:T(8,128)(2,1)S(1)} collective-permute-done((bf16[256,896]{1,0:T(8,128)(2,1)}, bf16[256,896]{1,0:T(8,128)(2,1)S(1)}, u32[]{:S(2)}, u32[]{:S(2)}) %collective-permute-start) | collective-permute-done | bytes 458784 | tf_op jit(solution)/shard_map/ppermute | solution.py:146
  29.5 1.0 collective-permute-done.1.refs_1_.w2
  30.4 0.0 copy-done.2
  30.4 0.0 copy-done.3
  30.4 0.1 select_select_fusion.w0
  30.6 9.3 %collective-permute-done.2.w3 = bf16[256,896]{1,0:T(8,128)(2,1)S(1)} collective-permute-done((bf16[256,896]{1,0:T(8,128)(2,1)}, bf16[256,896]{1,0:T(8,128)(2,1)S(1)}, u32[]{:S(2)}, u32[]{:S(2)}) %collective-permute-start.2) | collective-permute-done | bytes 458784 | tf_op jit(solution)/shard_map/ppermute | solution.py:146
  39.8 1.0 all-to-all-done.1
  40.9 1.3 shard_map.76
  42.2 0.0 copy-start
  42.2 4.9 %collective-permute-start.3 = (bf16[256,896]{1,0:T(8,128)(2,1)S(1)}, bf16[256,896]{1,0:T(8,128)(2,1)S(1)}, u32[]{:S(2)}, u32[]{:S(2)}) collective-permute-start(bf16[256,896]{1,0:T(8,128)(2,1)S(1)} %get-tuple-element.18), channel_id=1, source_target_pairs={{0,16},{16,0},{32,48},{48,32},{64,80},{80,64},{96,112},{112,96},{1... | collective-permute-start | bytes 1376264 | tf_op jit(solution)/shard_map/ppermute | solution.py:170
  47.1 1.3 shard_map.77
  48.4 0.0 copy-done
  48.4 0.0 copy-start.4
  48.4 0.1 collective-permute-done.3
  48.5 0.8 add_convert_fusion
  49.4 9.3 %all-to-all-start.2 = ((bf16[8,32,896]{2,1,0:T(8,128)(2,1)}), bf16[8,32,896]{2,1,0:T(8,128)(2,1)S(1)}, u32[]{:S(2)}, u32[]{:S(2)}) async-start(bf16[8,32,896]{2,1,0:T(8,128)(2,1)} %bitcast.3), calls=%async_computation.2 | async-start | bytes 917504 | tf_op jit(solution)/shard_map/all_to_all | solution.py:173
  58.7 0.0 copy-done.4
  58.7 3.1 %collective-permute-start.5 = (bf16[16,896]{1,0:T(8,128)(2,1)S(1)}, bf16[16,896]{1,0:T(8,128)(2,1)S(1)}, u32[]{:S(2)}, u32[]{:S(2)}) collective-permute-start(bf16[16,896]{1,0:T(8,128)(2,1)S(1)} %broadcast_select_fusion.12), channel_id=1, source_target_pairs={{0,32},{16,48},{32,0},{48,16},{64,96},{80,112},{96,64},{112,80},{1... | collective-permute-start | bytes 86024 | tf_op jit(solution)/shard_map/ppermute | solution.py:179
  61.8 1.8 %collective-permute-done.5 = bf16[16,896]{1,0:T(8,128)(2,1)S(1)} collective-permute-done((bf16[16,896]{1,0:T(8,128)(2,1)S(1)}, bf16[16,896]{1,0:T(8,128)(2,1)S(1)}, u32[]{:S(2)}, u32[]{:S(2)}) %collective-permute-start.5) | collective-permute-done | bytes 28704 | tf_op jit(solution)/shard_map/ppermute | solution.py:179
  63.6 11.6 %all-to-all-done.2 = bf16[8,32,896]{2,1,0:T(8,128)(2,1)S(1)} async-done(((bf16[8,32,896]{2,1,0:T(8,128)(2,1)}), bf16[8,32,896]{2,1,0:T(8,128)(2,1)S(1)}, u32[]{:S(2)}, u32[]{:S(2)}) %all-to-all-start.2) | async-done | bytes 458784 | tf_op jit(solution)/shard_map/all_to_all | solution.py:173
  75.2 0.1 convert_reduce_fusion.1
  75.3 0.1 fusion.2
  75.4 0.8 broadcast_in_dim.8
  76.2 3.5 %all-to-all-start.3 = ((bf16[8,32,896]{2,1,0:T(8,128)(2,1)}), bf16[8,32,896]{2,1,0:T(8,128)(2,1)S(1)}, u32[]{:S(2)}, u32[]{:S(2)}) async-start(bf16[8,32,896]{2,1,0:T(8,128)(2,1)} %bitcast.8), calls=%async_computation.3 | async-start | bytes 917504 | tf_op jit(solution)/shard_map/all_to_all | solution.py:186
  79.8 3.1 %collective-permute-start.4 = (bf16[16,896]{1,0:T(8,128)(2,1)S(1)}, bf16[16,896]{1,0:T(8,128)(2,1)S(1)}, u32[]{:S(2)}, u32[]{:S(2)}) collective-permute-start(bf16[16,896]{1,0:T(8,128)(2,1)S(1)} %broadcast_select_fusion.16), channel_id=1, source_target_pairs={{0,32},{16,48},{32,0},{48,16},{64,96},{80,112},{96,64},{112,80},{1... | collective-permute-start | bytes 86024 | tf_op jit(solution)/shard_map/ppermute | solution.py:193
  82.9 1.8 %collective-permute-done.4 = bf16[16,896]{1,0:T(8,128)(2,1)S(1)} collective-permute-done((bf16[16,896]{1,0:T(8,128)(2,1)S(1)}, bf16[16,896]{1,0:T(8,128)(2,1)S(1)}, u32[]{:S(2)}, u32[]{:S(2)}) %collective-permute-start.4) | collective-permute-done | bytes 28704 | tf_op jit(solution)/shard_map/ppermute | solution.py:193
  84.7 0.0 copy-start.5
  84.7 11.5 %all-to-all-done.3 = bf16[8,32,896]{2,1,0:T(8,128)(2,1)S(1)} async-done(((bf16[8,32,896]{2,1,0:T(8,128)(2,1)}), bf16[8,32,896]{2,1,0:T(8,128)(2,1)S(1)}, u32[]{:S(2)}, u32[]{:S(2)}) %all-to-all-start.3) | async-done | bytes 458784 | tf_op jit(solution)/shard_map/all_to_all | solution.py:186
  96.2 2.4 %collective-permute-start.6 = (bf16[256,896]{1,0:T(8,128)(2,1)S(1)}, bf16[256,896]{1,0:T(8,128)(2,1)S(1)}, u32[]{:S(2)}, u32[]{:S(2)}) collective-permute-start(bf16[256,896]{1,0:T(8,128)(2,1)S(1)} %bitcast.32), channel_id=1, source_target_pairs={{0,16},{16,0},{32,48},{48,32},{64,80},{80,64},{96,112},{112,96},{1... | collective-permute-start | bytes 1376264 | tf_op jit(solution)/shard_map/ppermute | solution.py:196
  98.6 1.4 %collective-permute-done.6.other = bf16[256,896]{1,0:T(8,128)(2,1)S(1)} collective-permute-done((bf16[256,896]{1,0:T(8,128)(2,1)S(1)}, bf16[256,896]{1,0:T(8,128)(2,1)S(1)}, u32[]{:S(2)}, u32[]{:S(2)}) %collective-permute-start.6) | collective-permute-done | bytes 458784 | tf_op jit(solution)/shard_map/ppermute | solution.py:196
  100.0 2.8 %shard_map.78 = bf16[4,4,4,2,16,256]{5,4,3,2,1,0:T(8,128)(2,1)} custom-call(s32[2]{0:T(128)S(1)} %pad_add_fusion.place, bf16[256,896]{1,0:T(8,128)(2,1)S(1)} %bitcast.33, bf16[256,896]{1,0:T(8,128)(2,1)S(1)} %collective-permute-done.6.other, bf16[256,896]{1,0:T(8,128)(2,1)S(1)} %select_select_fusion.w0, ...), custom_call_target="tpu_custom_call" | custom-call | flops 939524096 | bytes 4194304 | tf_op jit(solution)/shard_map/pallas_call | solution.py:198
  102.8 0.0 copy-done.5
  102.8 0.0 copy-start.1
  102.8 3.6 %all-to-all-start.4 = ((bf16[4,16,32,256]{3,2,1,0:T(8,128)(2,1)}), bf16[4,16,32,256]{3,2,1,0:T(8,128)(2,1)S(1)}, u32[]{:S(2)}, u32[]{:S(2)}) async-start(bf16[4,16,32,256]{3,2,1,0:T(8,128)(2,1)} %bitcast.10), calls=%async_computation.4 | async-start | bytes 2097152 | tf_op jit(solution)/shard_map/all_to_all | solution.py:201
  106.5 0.0 copy-done.1
  106.5 0.0 copy-start.6
  106.5 2.6 %shard_map.80 = (bf16[256,896]{1,0:T(8,128)(2,1)S(1)}, bf16[256,896]{1,0:T(8,128)(2,1)}, bf16[256,896]{1,0:T(8,128)(2,1)}, bf16[256,896]{1,0:T(8,128)(2,1)}) custom-call(s32[2]{0:T(128)S(1)} %pad_add_fusion.place, bf16[512,1024]{1,0:T(8,128)(2,1)S(1)} %copy-done.1, bf16[256,896]{1,0:T(8,128)(2,1)S(1)} %bitcast.34, ...), custom_call_target="tpu_custom_call" | custom-call | flops 939524096 | bytes 4194304 | tf_op jit(solution)/shard_map/pallas_call | solution.py:206
  109.1 3.1 %collective-permute-start.7 = (bf16[256,896]{1,0:T(8,128)(2,1)}, bf16[256,896]{1,0:T(8,128)(2,1)S(1)}, u32[]{:S(2)}, u32[]{:S(2)}) collective-permute-start(bf16[256,896]{1,0:T(8,128)(2,1)} %get-tuple-element.21), channel_id=1, source_target_pairs={{0,32},{16,48},{32,0},{48,16},{64,96},{80,112},{96,64},{112,80},{1... | collective-permute-start | bytes 1376264 | tf_op jit(solution)/shard_map/ppermute | solution.py:207
  112.2 2.2 %collective-permute-start.8 = (bf16[256,896]{1,0:T(8,128)(2,1)}, bf16[256,896]{1,0:T(8,128)(2,1)S(1)}, u32[]{:S(2)}, u32[]{:S(2)}) collective-permute-start(bf16[256,896]{1,0:T(8,128)(2,1)} %get-tuple-element.22), channel_id=1, source_target_pairs={{0,64},{16,80},{32,96},{48,112},{64,0},{80,16},{96,32},{112,48},{1... | collective-permute-start | bytes 1376264 | tf_op jit(solution)/shard_map/ppermute | solution.py:207
  114.4 3.1 %collective-permute-start.9 = (bf16[256,896]{1,0:T(8,128)(2,1)}, bf16[256,896]{1,0:T(8,128)(2,1)S(1)}, u32[]{:S(2)}, u32[]{:S(2)}) collective-permute-start(bf16[256,896]{1,0:T(8,128)(2,1)} %get-tuple-element.23), channel_id=1, source_target_pairs={{0,96},{16,112},{32,64},{48,80},{64,32},{80,48},{96,0},{112,16},{1... | collective-permute-start | bytes 1376264 | tf_op jit(solution)/shard_map/ppermute | solution.py:207
  117.5 0.0 copy-done.6
  117.5 0.6 pad_maximum_fusion.3
  118.1 3.1 %all-to-all-done.4.x = bf16[4,16,32,256]{3,2,1,0:T(8,128)(2,1)S(1)} async-done(((bf16[4,16,32,256]{3,2,1,0:T(8,128)(2,1)}), bf16[4,16,32,256]{3,2,1,0:T(8,128)(2,1)S(1)}, u32[]{:S(2)}, u32[]{:S(2)}) %all-to-all-start.4) | async-done | bytes 1048608 | tf_op jit(solution)/shard_map/all_to_all | solution.py:201
  121.3 0.8 shard_map.79
  122.1 6.5 %all-to-all-start.5 = ((bf16[16,32,256]{2,1,0:T(8,128)(2,1)}), bf16[16,32,256]{2,1,0:T(8,128)(2,1)S(1)}, u32[]{:S(2)}, u32[]{:S(2)}) async-start(bf16[16,32,256]{2,1,0:T(8,128)(2,1)} %shard_map.79), calls=%async_computation.5 | async-start | bytes 524288 | tf_op jit(solution)/shard_map/all_to_all | solution.py:209
  128.6 0.0 collective-permute-done.7
  128.6 8.3 %collective-permute-done.8 = bf16[256,896]{1,0:T(8,128)(2,1)S(1)} collective-permute-done((bf16[256,896]{1,0:T(8,128)(2,1)}, bf16[256,896]{1,0:T(8,128)(2,1)S(1)}, u32[]{:S(2)}, u32[]{:S(2)}) %collective-permute-start.8) | collective-permute-done | bytes 458784 | tf_op jit(solution)/shard_map/ppermute | solution.py:207
  136.9 0.0 collective-permute-done.9
  136.9 0.2 broadcast_select_fusion.7
  137.2 1.4 pad_maximum_fusion
  138.5 1.1 all-to-all-done.5
  139.6 0.6 reduce_sum.38
  (7 shorter events, 0.1 us)
Async XLA Ops:
  2.1 20.6 %all-to-all-start = ((bf16[16,32,256]{2,1,0:T(8,128)(2,1)}), bf16[16,32,256]{2,1,0:T(8,128)(2,1)S(1)}, u32[]{:S(2)}, u32[]{:S(2)}) async-start(bf16[16,32,256]{2,1,0:T(8,128)(2,1)} %broadcast_in_dim.6), calls=%async_computation | async-start | bytes 524288 | tf_op jit(solution)/shard_map/all_to_all | solution.py:156
  14.2 15.2 %collective-permute-start = (bf16[256,896]{1,0:T(8,128)(2,1)}, bf16[256,896]{1,0:T(8,128)(2,1)S(1)}, u32[]{:S(2)}, u32[]{:S(2)}) collective-permute-start(bf16[256,896]{1,0:T(8,128)(2,1)} %get-tuple-element.32), channel_id=1, source_target_pairs={{0,32},{16,48},{32,0},{48,16},{64,96},{80,112},{96,64},{112,80},{1... | collective-permute-start | bytes 1376264 | tf_op jit(solution)/shard_map/ppermute | solution.py:146
  17.5 13.0 %collective-permute-start.1 = (bf16[256,896]{1,0:T(8,128)(2,1)S(1)}, bf16[256,896]{1,0:T(8,128)(2,1)S(1)}, u32[]{:S(2)}, u32[]{:S(2)}) collective-permute-start(bf16[256,896]{1,0:T(8,128)(2,1)S(1)} %get-tuple-element.31), channel_id=1, source_target_pairs={{0,64},{16,80},{32,96},{48,112},{64,0},{80,16},{96,32},{112,48},{1... | collective-permute-start | bytes 1376264 | tf_op jit(solution)/shard_map/ppermute | solution.py:146
  20.6 19.3 %collective-permute-start.2 = (bf16[256,896]{1,0:T(8,128)(2,1)}, bf16[256,896]{1,0:T(8,128)(2,1)S(1)}, u32[]{:S(2)}, u32[]{:S(2)}) collective-permute-start(bf16[256,896]{1,0:T(8,128)(2,1)} %get-tuple-element.30), channel_id=1, source_target_pairs={{0,96},{16,112},{32,64},{48,80},{64,32},{80,48},{96,0},{112,16},{1... | collective-permute-start | bytes 1376264 | tf_op jit(solution)/shard_map/ppermute | solution.py:146
  23.8 17.1 %all-to-all-start.1 = ((bf16[4,16,32,256]{3,2,1,0:T(8,128)(2,1)}), bf16[4,16,32,256]{3,2,1,0:T(8,128)(2,1)S(1)}, u32[]{:S(2)}, u32[]{:S(2)}) async-start(bf16[4,16,32,256]{3,2,1,0:T(8,128)(2,1)} %broadcast_in_dim.7), calls=%async_computation.1 | async-start | bytes 2097152 | tf_op jit(solution)/shard_map/all_to_all | solution.py:162
  27.8 2.6 %copy-start.2 = (bf16[256,1792]{1,0:T(8,128)(2,1)S(1)}, bf16[256,1792]{1,0:T(8,128)(2,1)}, u32[]{:S(2)}) copy-start(bf16[256,1792]{1,0:T(8,128)(2,1)} %param.5) | copy-start | bytes 2752516
  27.8 2.6 %copy-start.3 = (bf16[256,1792]{1,0:T(8,128)(2,1)S(1)}, bf16[256,1792]{1,0:T(8,128)(2,1)}, u32[]{:S(2)}) copy-start(bf16[256,1792]{1,0:T(8,128)(2,1)} %param.6) | copy-start | bytes 2752516
  42.2 6.2 %copy-start = (bf16[512,1024]{1,0:T(8,128)(2,1)}, bf16[512,1024]{1,0:T(8,128)(2,1)S(1)}, u32[]{:S(2)}) copy-start(bf16[512,1024]{1,0:T(8,128)(2,1)S(1)} %get-tuple-element.17.tokens) | copy-start | bytes 3145732
  42.2 6.3 %collective-permute-start.3 = (bf16[256,896]{1,0:T(8,128)(2,1)S(1)}, bf16[256,896]{1,0:T(8,128)(2,1)S(1)}, u32[]{:S(2)}, u32[]{:S(2)}) collective-permute-start(bf16[256,896]{1,0:T(8,128)(2,1)S(1)} %get-tuple-element.18), channel_id=1, source_target_pairs={{0,16},{16,0},{32,48},{48,32},{64,80},{80,64},{96,112},{112,96},{1... | collective-permute-start | bytes 1376264 | tf_op jit(solution)/shard_map/ppermute | solution.py:170
  48.4 10.3 %copy-start.4 = (bf16[16,1792]{1,0:T(8,128)(2,1)S(1)}, bf16[16,1792]{1,0:T(8,128)(2,1)}, u32[]{:S(2)}) copy-start(bf16[16,1792]{1,0:T(8,128)(2,1)} %param.7) | copy-start | bytes 172036
  49.4 25.9 %all-to-all-start.2 = ((bf16[8,32,896]{2,1,0:T(8,128)(2,1)}), bf16[8,32,896]{2,1,0:T(8,128)(2,1)S(1)}, u32[]{:S(2)}, u32[]{:S(2)}) async-start(bf16[8,32,896]{2,1,0:T(8,128)(2,1)} %bitcast.3), calls=%async_computation.2 | async-start | bytes 917504 | tf_op jit(solution)/shard_map/all_to_all | solution.py:173
  58.7 4.9 %collective-permute-start.5 = (bf16[16,896]{1,0:T(8,128)(2,1)S(1)}, bf16[16,896]{1,0:T(8,128)(2,1)S(1)}, u32[]{:S(2)}, u32[]{:S(2)}) collective-permute-start(bf16[16,896]{1,0:T(8,128)(2,1)S(1)} %broadcast_select_fusion.12), channel_id=1, source_target_pairs={{0,32},{16,48},{32,0},{48,16},{64,96},{80,112},{96,64},{112,80},{1... | collective-permute-start | bytes 86024 | tf_op jit(solution)/shard_map/ppermute | solution.py:179
  76.2 20.0 %all-to-all-start.3 = ((bf16[8,32,896]{2,1,0:T(8,128)(2,1)}), bf16[8,32,896]{2,1,0:T(8,128)(2,1)S(1)}, u32[]{:S(2)}, u32[]{:S(2)}) async-start(bf16[8,32,896]{2,1,0:T(8,128)(2,1)} %bitcast.8), calls=%async_computation.3 | async-start | bytes 917504 | tf_op jit(solution)/shard_map/all_to_all | solution.py:186
  79.8 4.9 %collective-permute-start.4 = (bf16[16,896]{1,0:T(8,128)(2,1)S(1)}, bf16[16,896]{1,0:T(8,128)(2,1)S(1)}, u32[]{:S(2)}, u32[]{:S(2)}) collective-permute-start(bf16[16,896]{1,0:T(8,128)(2,1)S(1)} %broadcast_select_fusion.16), channel_id=1, source_target_pairs={{0,32},{16,48},{32,0},{48,16},{64,96},{80,112},{96,64},{112,80},{1... | collective-permute-start | bytes 86024 | tf_op jit(solution)/shard_map/ppermute | solution.py:193
  84.7 18.1 %copy-start.5 = (bf16[16,896]{1,0:T(8,128)(2,1)}, bf16[16,896]{1,0:T(8,128)(2,1)S(1)}, u32[]{:S(2)}) copy-start(bf16[16,896]{1,0:T(8,128)(2,1)S(1)} %collective-permute-done.4) | copy-start | bytes 86020
  96.2 3.8 %collective-permute-start.6 = (bf16[256,896]{1,0:T(8,128)(2,1)S(1)}, bf16[256,896]{1,0:T(8,128)(2,1)S(1)}, u32[]{:S(2)}, u32[]{:S(2)}) collective-permute-start(bf16[256,896]{1,0:T(8,128)(2,1)S(1)} %bitcast.32), channel_id=1, source_target_pairs={{0,16},{16,0},{32,48},{48,32},{64,80},{80,64},{96,112},{112,96},{1... | collective-permute-start | bytes 1376264 | tf_op jit(solution)/shard_map/ppermute | solution.py:196
  102.8 3.7 %copy-start.1 = (bf16[512,1024]{1,0:T(8,128)(2,1)S(1)}, bf16[512,1024]{1,0:T(8,128)(2,1)}, u32[]{:S(2)}) copy-start(bf16[512,1024]{1,0:T(8,128)(2,1)} %copy-done) | copy-start | bytes 3145732
  102.8 18.5 %all-to-all-start.4 = ((bf16[4,16,32,256]{3,2,1,0:T(8,128)(2,1)}), bf16[4,16,32,256]{3,2,1,0:T(8,128)(2,1)S(1)}, u32[]{:S(2)}, u32[]{:S(2)}) async-start(bf16[4,16,32,256]{3,2,1,0:T(8,128)(2,1)} %bitcast.10), calls=%async_computation.4 | async-start | bytes 2097152 | tf_op jit(solution)/shard_map/all_to_all | solution.py:201
  106.5 11.0 %copy-start.6 = (bf16[16,896]{1,0:T(8,128)(2,1)S(1)}, bf16[16,896]{1,0:T(8,128)(2,1)}, u32[]{:S(2)}) copy-start(bf16[16,896]{1,0:T(8,128)(2,1)} %copy-done.5) | copy-start | bytes 86020
  109.1 19.5 %collective-permute-start.7 = (bf16[256,896]{1,0:T(8,128)(2,1)}, bf16[256,896]{1,0:T(8,128)(2,1)S(1)}, u32[]{:S(2)}, u32[]{:S(2)}) collective-permute-start(bf16[256,896]{1,0:T(8,128)(2,1)} %get-tuple-element.21), channel_id=1, source_target_pairs={{0,32},{16,48},{32,0},{48,16},{64,96},{80,112},{96,64},{112,80},{1... | collective-permute-start | bytes 1376264 | tf_op jit(solution)/shard_map/ppermute | solution.py:207
  112.2 24.7 %collective-permute-start.8 = (bf16[256,896]{1,0:T(8,128)(2,1)}, bf16[256,896]{1,0:T(8,128)(2,1)S(1)}, u32[]{:S(2)}, u32[]{:S(2)}) collective-permute-start(bf16[256,896]{1,0:T(8,128)(2,1)} %get-tuple-element.22), channel_id=1, source_target_pairs={{0,64},{16,80},{32,96},{48,112},{64,0},{80,16},{96,32},{112,48},{1... | collective-permute-start | bytes 1376264 | tf_op jit(solution)/shard_map/ppermute | solution.py:207
  114.4 22.5 %collective-permute-start.9 = (bf16[256,896]{1,0:T(8,128)(2,1)}, bf16[256,896]{1,0:T(8,128)(2,1)S(1)}, u32[]{:S(2)}, u32[]{:S(2)}) collective-permute-start(bf16[256,896]{1,0:T(8,128)(2,1)} %get-tuple-element.23), channel_id=1, source_target_pairs={{0,96},{16,112},{32,64},{48,80},{64,32},{80,48},{96,0},{112,16},{1... | collective-permute-start | bytes 1376264 | tf_op jit(solution)/shard_map/ppermute | solution.py:207
  122.1 17.5 %all-to-all-start.5 = ((bf16[16,32,256]{2,1,0:T(8,128)(2,1)}), bf16[16,32,256]{2,1,0:T(8,128)(2,1)S(1)}, u32[]{:S(2)}, u32[]{:S(2)}) async-start(bf16[16,32,256]{2,1,0:T(8,128)(2,1)} %shard_map.79), calls=%async_computation.5 | async-start | bytes 524288 | tf_op jit(solution)/shard_map/all_to_all | solution.py:209

commit v6 on v5

--- a/solution.py
+++ b/solution.py
@@ -21,19 +21,21 @@
 MARK_FLOPS = 30_000_000_000
 VMEM = pl.BlockSpec(memory_space=pltpu.VMEM)
 SMEM = pl.BlockSpec(memory_space=pltpu.SMEM)
+ANY = pl.BlockSpec(memory_space=pl.ANY)
 
 
 def struct(shape, dtype=BF16):
     return jax.ShapeDtypeStruct(shape, dtype)
 
 
-def call(kernel, n_in, out_shape, flops, first=SMEM):
+def call(kernel, n_in, out_shape, flops, first=SMEM, last=VMEM, scratch=()):
     many = isinstance(out_shape, list)
     return pl.pallas_call(
         kernel,
         out_shape=out_shape,
         in_specs=[first] + [VMEM] * n_in,
-        out_specs=[VMEM] * len(out_shape) if many else VMEM,
+        out_specs=[last] * len(out_shape) if many else last,
+        scratch_shapes=scratch,
         compiler_params=PARAMS,
         cost_estimate=pl.CostEstimate(flops=flops, bytes_accessed=4 << 20, transcendentals=0),
     )
@@ -82,31 +84,41 @@
         out[:, s] = total
 
 
-def input_parts(place, own, other, w0, w1, w2, w3, out):
+def input_parts(place, own, other, w0, w1, w2, w3, out, held, sems):
     block = out.shape[-2]
-    for part, back in enumerate((own, other)):
-        core = place[1] ^ part
-        for k, w in enumerate((w0, w1, w2, w3)):
-            member = place[0] ^ k
+    copies = []
+    for k, w in enumerate((w0, w1, w2, w3)):
+        for part, back in enumerate((own, other)):
+            core = place[1] ^ part
             term = lax.dot_general(
                 back[...], w[...], (((1,), (1,)), ((), ())), preferred_element_type=F32
             ).astype(BF16)
             for h in range(4):
                 for x in range(4):
                     row = (h * 4 + x) * block
-                    out[x, member, h, core] = term[row : row + block]
-
-
-def weight_parts(place, tokens, own, other, *outs):
+                    held[k, x, h, core] = term[row : row + block]
+        copies.append(pltpu.make_async_copy(held.at[k], out.at[:, place[0] ^ k], sems.at[k]))
+        copies[-1].start()
+    for copy in copies:
+        copy.wait()
+
+
+def weight_parts(place, tokens, own, other, *refs):
+    outs, held, sems = refs[:4], refs[4], refs[5]
     width, n = outs[0].shape
     half = own.shape[0]
     dims = (((0,), (0,)), ((), ()))
-    for k, out in enumerate(outs):
+    copies = []
+    for k in (1, 2, 3, 0):
         for s in spans(n):
             cols = slice(k * width, (k + 1) * width)
             term = lax.dot_general(tokens[:half, cols], own[:, s], dims, preferred_element_type=F32)
             term += lax.dot_general(tokens[half:, cols], other[:, s], dims, preferred_element_type=F32)
-            out[:, s] = term.astype(BF16)
+            held[k, :, s] = term.astype(BF16)
+        copies.append(pltpu.make_async_copy(held.at[k], outs[k], sems.at[k]))
+        copies[-1].start()
+    for copy in copies:
+        copy.wait()
 
 
 def sum_first(x, out):
@@ -147,7 +159,7 @@
     mark = pl.pallas_call(
         arrived,
         out_shape=struct((8, 128), F32),
-        in_specs=[pl.BlockSpec(memory_space=pl.ANY)] * 2,
+        in_specs=[ANY] * 2,
         out_specs=VMEM,
         compiler_params=PARAMS,
         cost_estimate=pl.CostEstimate(flops=MARK_FLOPS, bytes_accessed=4096, transcendentals=0),
@@ -195,15 +207,20 @@
     hidden = jnp.concatenate(pair(mine, other), 1)
     other = lax.ppermute(own, "dp", CORE_SWAP)
 
-    total = call(input_parts, 6, struct((4, 4, 4, 2, block, width)), 2 * flops)(
-        place, own, other, *weights
-    )
+    sems = pltpu.SemaphoreType.DMA((4,))
+    scratch = [pltpu.VMEM((4, 4, 4, 2, block, width), BF16), sems]
+    total = call(
+        input_parts, 6, struct((4, 4, 4, 2, block, width)), 2 * flops, last=ANY, scratch=scratch
+    )(place, own, other, *weights)
     total = lax.all_to_all(
         total.reshape(4, 16, rows, width), "tensor", 0, 0, axis_index_groups=X_GROUPS
     )
     total = call(sum_first, 0, struct((16, rows, width)), 1 << 20, VMEM)(total)
 
-    grads = call(weight_parts, 3, [struct((width, half))] * 4, 2 * flops)(place, tokens, own, other)
+    scratch = [pltpu.VMEM((4, width, half), BF16), sems]
+    grads = call(
+        weight_parts, 3, [struct((width, half))] * 4, 2 * flops, last=ANY, scratch=scratch
+    )(place, tokens, own, other)
     grads = [grads[0]] + [lax.ppermute(grads[k], "dp", QUAD_SWAP[k]) for k in (1, 2, 3)]
 
     total = lax.all_to_all(total, ("dp", "tensor"), 0, 0, axis_index_groups=QUAD_YHI_GROUPS)

time: 142 us -> 142 us (level)
  no operation moved by 1% of the time
where the time goes in v6:
time: 142 us; the launch traced here: 140 us
  starting transfers between devices  66.7 us (47%)
  waiting for transfers between devices  53.7 us (38%)
  Pallas kernels  8.37 us (6%)
  other arithmetic  6.69 us (5%)
  local copies, waits for them, and re-layouts  3.4 us (2%)
    ppermute x3, waiting for transfers between devices, per_device(): weights = [lax.ppermute(sends[k], 'dp', QUAD_SWAP[k]) for k in (1, 2, 3)]  11.9 us
    all_to_all x1, waiting for transfers between devices, per_device(): lax.all_to_all(part.reshape(8, 2 * block, half), 'dp', 0, 0, axis_index_g...  11.6 us
    all_to_all x1, waiting for transfers between devices, per_device(): lax.all_to_all(jnp.broadcast_to(jnp.stack([gate_back, up_back])[None], (4...  11.5 us
    all_to_all x1, starting transfers between devices, per_device(): lax.all_to_all(jnp.broadcast_to(activations[None], (16, rows, width)), ('...  9.56 us
    all_to_all x1, starting transfers between devices, per_device(): lax.all_to_all(part.reshape(8, 2 * block, half), 'dp', 0, 0, axis_index_g...  9.3 us
    ppermute x3, starting transfers between devices, per_device(): lax.ppermute(grads[k], 'dp', QUAD_SWAP[k])  8.37 us
    ppermute x3, starting transfers between devices, per_device(): weights = [lax.ppermute(sends[k], 'dp', QUAD_SWAP[k]) for k in (1, 2, 3)]  8.36 us
    ppermute x3, waiting for transfers between devices, per_device(): lax.ppermute(grads[k], 'dp', QUAD_SWAP[k])  8.12 us
  transfers between devices with their start and end apart: 16, of which 13 were waited for; matrix products, arithmetic and copies ran while one was open for 4% of the time, Pallas kernels for 3%

profile of v6, /device:TPU:1, one launch (start us, length us, event | category | flops | bytes accessed | tf_op | source)
XLA Modules:
  0.0 139.8 jit_solution(4605008034060744604)
XLA Ops:
  0.6 1.4 %broadcast_in_dim.6 = bf16[16,32,256]{2,1,0:T(8,128)(2,1)} broadcast(bf16[32,256]{1,0:T(8,128)(2,1)} %param.4), dimensions={1,2} | broadcast | bytes 278528 | tf_op jit(solution)/shard_map/broadcast_in_dim | solution.py:169
  2.1 9.6 %all-to-all-start = ((bf16[16,32,256]{2,1,0:T(8,128)(2,1)}), bf16[16,32,256]{2,1,0:T(8,128)(2,1)S(1)}, u32[]{:S(2)}, u32[]{:S(2)}) async-start(bf16[16,32,256]{2,1,0:T(8,128)(2,1)} %broadcast_in_dim.6), calls=%async_computation | async-start | bytes 524288 | tf_op jit(solution)/shard_map/all_to_all | solution.py:168
  11.7 2.5 %broadcast_select_fusion.10 = (bf16[256,896]{1,0:T(8,128)(2,1)}, bf16[256,896]{1,0:T(8,128)(2,1)S(1)}, bf16[256,896]{1,0:T(8,128)(2,1)}) fusion(pred[]{:T(512)S(6)} %eq.7, bf16[256,1792]{1,0:T(8,128)(2,1)} %param.5, pred[]{:T(512)S(6)} %eq.6, bf16[256,1792]{1,0:T(8,128)(2,1)} %param.6), kind=kLoop, calls=%fused_computation.17 | loop fusion | flops 1605632 | bytes 3211266 | tf_op jit(solution)/shard_map/jit(_where)/select_n | solution.py:145
  14.2 3.2 %collective-permute-start = (bf16[256,896]{1,0:T(8,128)(2,1)}, bf16[256,896]{1,0:T(8,128)(2,1)S(1)}, u32[]{:S(2)}, u32[]{:S(2)}) collective-permute-start(bf16[256,896]{1,0:T(8,128)(2,1)} %get-tuple-element.32), channel_id=1, source_target_pairs={{0,32},{16,48},{32,0},{48,16},{64,96},{80,112},{96,64},{112,80},{1... | collective-permute-start | bytes 1376264 | tf_op jit(solution)/shard_map/ppermute | solution.py:158
  17.5 3.1 %collective-permute-start.1 = (bf16[256,896]{1,0:T(8,128)(2,1)S(1)}, bf16[256,896]{1,0:T(8,128)(2,1)S(1)}, u32[]{:S(2)}, u32[]{:S(2)}) collective-permute-start(bf16[256,896]{1,0:T(8,128)(2,1)S(1)} %get-tuple-element.31), channel_id=1, source_target_pairs={{0,64},{16,80},{32,96},{48,112},{64,0},{80,16},{96,32},{112,48},{1... | collective-permute-start | bytes 1376264 | tf_op jit(solution)/shard_map/ppermute | solution.py:158
  20.6 2.0 %collective-permute-start.2 = (bf16[256,896]{1,0:T(8,128)(2,1)}, bf16[256,896]{1,0:T(8,128)(2,1)S(1)}, u32[]{:S(2)}, u32[]{:S(2)}) collective-permute-start(bf16[256,896]{1,0:T(8,128)(2,1)} %get-tuple-element.30), channel_id=1, source_target_pairs={{0,96},{16,112},{32,64},{48,80},{64,32},{80,48},{96,0},{112,16},{1... | collective-permute-start | bytes 1376264 | tf_op jit(solution)/shard_map/ppermute | solution.py:158
  22.6 0.1 pad_add_fusion.place
  22.7 0.0 all-to-all-done
  22.7 1.1 broadcast_in_dim.7
  23.8 4.0 %all-to-all-start.1 = ((bf16[4,16,32,256]{3,2,1,0:T(8,128)(2,1)}), bf16[4,16,32,256]{3,2,1,0:T(8,128)(2,1)S(1)}, u32[]{:S(2)}, u32[]{:S(2)}) async-start(bf16[4,16,32,256]{3,2,1,0:T(8,128)(2,1)} %broadcast_in_dim.7), calls=%async_computation.1 | async-start | bytes 2097152 | tf_op jit(solution)/shard_map/all_to_all | solution.py:174
  27.8 0.0 copy-start.2
  27.8 0.0 copy-start.3
  27.8 1.6 %collective-permute-done.refs_0_.w1 = bf16[256,896]{1,0:T(8,128)(2,1)S(1)} collective-permute-done((bf16[256,896]{1,0:T(8,128)(2,1)}, bf16[256,896]{1,0:T(8,128)(2,1)S(1)}, u32[]{:S(2)}, u32[]{:S(2)}) %collective-permute-start) | collective-permute-done | bytes 458784 | tf_op jit(solution)/shard_map/ppermute | solution.py:158
  29.5 1.0 collective-permute-done.1.refs_1_.w2
  30.4 0.0 copy-done.2
  30.4 0.0 copy-done.3
  30.4 0.1 select_select_fusion.w0
  30.6 9.3 %collective-permute-done.2.w3 = bf16[256,896]{1,0:T(8,128)(2,1)S(1)} collective-permute-done((bf16[256,896]{1,0:T(8,128)(2,1)}, bf16[256,896]{1,0:T(8,128)(2,1)S(1)}, u32[]{:S(2)}, u32[]{:S(2)}) %collective-permute-start.2) | collective-permute-done | bytes 458784 | tf_op jit(solution)/shard_map/ppermute | solution.py:158
  39.8 1.0 all-to-all-done.1
  40.9 1.3 shard_map.76
  42.2 0.0 copy-start
  42.2 4.9 %collective-permute-start.3 = (bf16[256,896]{1,0:T(8,128)(2,1)S(1)}, bf16[256,896]{1,0:T(8,128)(2,1)S(1)}, u32[]{:S(2)}, u32[]{:S(2)}) collective-permute-start(bf16[256,896]{1,0:T(8,128)(2,1)S(1)} %get-tuple-element.18), channel_id=1, source_target_pairs={{0,16},{16,0},{32,48},{48,32},{64,80},{80,64},{96,112},{112,96},{1... | collective-permute-start | bytes 1376264 | tf_op jit(solution)/shard_map/ppermute | solution.py:182
  47.1 1.3 shard_map.77
  48.4 0.0 copy-done
  48.4 0.0 copy-start.4
  48.4 0.1 collective-permute-done.3
  48.5 0.8 add_convert_fusion
  49.4 9.3 %all-to-all-start.2 = ((bf16[8,32,896]{2,1,0:T(8,128)(2,1)}), bf16[8,32,896]{2,1,0:T(8,128)(2,1)S(1)}, u32[]{:S(2)}, u32[]{:S(2)}) async-start(bf16[8,32,896]{2,1,0:T(8,128)(2,1)} %bitcast.3), calls=%async_computation.2 | async-start | bytes 917504 | tf_op jit(solution)/shard_map/all_to_all | solution.py:185
  58.7 0.0 copy-done.4
  58.7 3.1 %collective-permute-start.5 = (bf16[16,896]{1,0:T(8,128)(2,1)S(1)}, bf16[16,896]{1,0:T(8,128)(2,1)S(1)}, u32[]{:S(2)}, u32[]{:S(2)}) collective-permute-start(bf16[16,896]{1,0:T(8,128)(2,1)S(1)} %broadcast_select_fusion.12), channel_id=1, source_target_pairs={{0,32},{16,48},{32,0},{48,16},{64,96},{80,112},{96,64},{112,80},{1... | collective-permute-start | bytes 86024 | tf_op jit(solution)/shard_map/ppermute | solution.py:191
  61.8 1.8 %collective-permute-done.5 = bf16[16,896]{1,0:T(8,128)(2,1)S(1)} collective-permute-done((bf16[16,896]{1,0:T(8,128)(2,1)S(1)}, bf16[16,896]{1,0:T(8,128)(2,1)S(1)}, u32[]{:S(2)}, u32[]{:S(2)}) %collective-permute-start.5) | collective-permute-done | bytes 28704 | tf_op jit(solution)/shard_map/ppermute | solution.py:191
  63.6 11.6 %all-to-all-done.2 = bf16[8,32,896]{2,1,0:T(8,128)(2,1)S(1)} async-done(((bf16[8,32,896]{2,1,0:T(8,128)(2,1)}), bf16[8,32,896]{2,1,0:T(8,128)(2,1)S(1)}, u32[]{:S(2)}, u32[]{:S(2)}) %all-to-all-start.2) | async-done | bytes 458784 | tf_op jit(solution)/shard_map/all_to_all | solution.py:185
  75.2 0.1 convert_reduce_fusion.1
  75.3 0.1 fusion.2
  75.4 0.8 broadcast_in_dim.8
  76.2 3.5 %all-to-all-start.3 = ((bf16[8,32,896]{2,1,0:T(8,128)(2,1)}), bf16[8,32,896]{2,1,0:T(8,128)(2,1)S(1)}, u32[]{:S(2)}, u32[]{:S(2)}) async-start(bf16[8,32,896]{2,1,0:T(8,128)(2,1)} %bitcast.8), calls=%async_computation.3 | async-start | bytes 917504 | tf_op jit(solution)/shard_map/all_to_all | solution.py:198
  79.8 3.1 %collective-permute-start.4 = (bf16[16,896]{1,0:T(8,128)(2,1)S(1)}, bf16[16,896]{1,0:T(8,128)(2,1)S(1)}, u32[]{:S(2)}, u32[]{:S(2)}) collective-permute-start(bf16[16,896]{1,0:T(8,128)(2,1)S(1)} %broadcast_select_fusion.16), channel_id=1, source_target_pairs={{0,32},{16,48},{32,0},{48,16},{64,96},{80,112},{96,64},{112,80},{1... | collective-permute-start | bytes 86024 | tf_op jit(solution)/shard_map/ppermute | solution.py:205
  82.9 1.8 %collective-permute-done.4 = bf16[16,896]{1,0:T(8,128)(2,1)S(1)} collective-permute-done((bf16[16,896]{1,0:T(8,128)(2,1)S(1)}, bf16[16,896]{1,0:T(8,128)(2,1)S(1)}, u32[]{:S(2)}, u32[]{:S(2)}) %collective-permute-start.4) | collective-permute-done | bytes 28704 | tf_op jit(solution)/shard_map/ppermute | solution.py:205
  84.7 0.0 copy-start.5
  84.7 11.5 %all-to-all-done.3 = bf16[8,32,896]{2,1,0:T(8,128)(2,1)S(1)} async-done(((bf16[8,32,896]{2,1,0:T(8,128)(2,1)}), bf16[8,32,896]{2,1,0:T(8,128)(2,1)S(1)}, u32[]{:S(2)}, u32[]{:S(2)}) %all-to-all-start.3) | async-done | bytes 458784 | tf_op jit(solution)/shard_map/all_to_all | solution.py:198
  96.2 2.4 %collective-permute-start.6 = (bf16[256,896]{1,0:T(8,128)(2,1)S(1)}, bf16[256,896]{1,0:T(8,128)(2,1)S(1)}, u32[]{:S(2)}, u32[]{:S(2)}) collective-permute-start(bf16[256,896]{1,0:T(8,128)(2,1)S(1)} %bitcast.32), channel_id=1, source_target_pairs={{0,16},{16,0},{32,48},{48,32},{64,80},{80,64},{96,112},{112,96},{1... | collective-permute-start | bytes 1376264 | tf_op jit(solution)/shard_map/ppermute | solution.py:208
  98.6 1.4 %collective-permute-done.6.other = bf16[256,896]{1,0:T(8,128)(2,1)S(1)} collective-permute-done((bf16[256,896]{1,0:T(8,128)(2,1)S(1)}, bf16[256,896]{1,0:T(8,128)(2,1)S(1)}, u32[]{:S(2)}, u32[]{:S(2)}) %collective-permute-start.6) | collective-permute-done | bytes 458784 | tf_op jit(solution)/shard_map/ppermute | solution.py:208
  100.0 2.6 %shard_map.78 = bf16[4,4,4,2,16,256]{5,4,3,2,1,0:T(8,128)(2,1)} custom-call(s32[2]{0:T(128)S(1)} %pad_add_fusion.place, bf16[256,896]{1,0:T(8,128)(2,1)S(1)} %bitcast.33, bf16[256,896]{1,0:T(8,128)(2,1)S(1)} %collective-permute-done.6.other, bf16[256,896]{1,0:T(8,128)(2,1)S(1)} %select_select_fusion.w0, ...), custom_call_target="tpu_custom_call" | custom-call | flops 939524096 | bytes 4194304 | tf_op jit(solution)/shard_map/pallas_call | solution.py:212
  102.6 0.0 copy-done.5
  102.6 0.0 copy-start.1
  102.6 3.7 %all-to-all-start.4 = ((bf16[4,16,32,256]{3,2,1,0:T(8,128)(2,1)}), bf16[4,16,32,256]{3,2,1,0:T(8,128)(2,1)S(1)}, u32[]{:S(2)}, u32[]{:S(2)}) async-start(bf16[4,16,32,256]{3,2,1,0:T(8,128)(2,1)} %bitcast.10), calls=%async_computation.4 | async-start | bytes 2097152 | tf_op jit(solution)/shard_map/all_to_all | solution.py:215
  106.3 0.0 copy-done.1
  106.3 0.0 copy-start.6
  106.3 2.4 %shard_map.80 = (bf16[256,896]{1,0:T(8,128)(2,1)S(1)}, bf16[256,896]{1,0:T(8,128)(2,1)}, bf16[256,896]{1,0:T(8,128)(2,1)}, bf16[256,896]{1,0:T(8,128)(2,1)}) custom-call(s32[2]{0:T(128)S(1)} %pad_add_fusion.place, bf16[512,1024]{1,0:T(8,128)(2,1)S(1)} %copy-done.1, bf16[256,896]{1,0:T(8,128)(2,1)S(1)} %bitcast.34, ...), custom_call_target="tpu_custom_call" | custom-call | flops 939524096 | bytes 4194304 | tf_op jit(solution)/shard_map/pallas_call | solution.py:221
  108.7 3.1 %collective-permute-start.7 = (bf16[256,896]{1,0:T(8,128)(2,1)}, bf16[256,896]{1,0:T(8,128)(2,1)S(1)}, u32[]{:S(2)}, u32[]{:S(2)}) collective-permute-start(bf16[256,896]{1,0:T(8,128)(2,1)} %get-tuple-element.21), channel_id=1, source_target_pairs={{0,32},{16,48},{32,0},{48,16},{64,96},{80,112},{96,64},{112,80},{1... | collective-permute-start | bytes 1376264 | tf_op jit(solution)/shard_map/ppermute | solution.py:224
  111.8 2.2 %collective-permute-start.8 = (bf16[256,896]{1,0:T(8,128)(2,1)}, bf16[256,896]{1,0:T(8,128)(2,1)S(1)}, u32[]{:S(2)}, u32[]{:S(2)}) collective-permute-start(bf16[256,896]{1,0:T(8,128)(2,1)} %get-tuple-element.22), channel_id=1, source_target_pairs={{0,64},{16,80},{32,96},{48,112},{64,0},{80,16},{96,32},{112,48},{1... | collective-permute-start | bytes 1376264 | tf_op jit(solution)/shard_map/ppermute | solution.py:224
  114.0 3.1 %collective-permute-start.9 = (bf16[256,896]{1,0:T(8,128)(2,1)}, bf16[256,896]{1,0:T(8,128)(2,1)S(1)}, u32[]{:S(2)}, u32[]{:S(2)}) collective-permute-start(bf16[256,896]{1,0:T(8,128)(2,1)} %get-tuple-element.23), channel_id=1, source_target_pairs={{0,96},{16,112},{32,64},{48,80},{64,32},{80,48},{96,0},{112,16},{1... | collective-permute-start | bytes 1376264 | tf_op jit(solution)/shard_map/ppermute | solution.py:224
  117.1 0.0 copy-done.6
  117.1 0.6 pad_maximum_fusion.3
  117.7 3.4 %all-to-all-done.4.x = bf16[4,16,32,256]{3,2,1,0:T(8,128)(2,1)S(1)} async-done(((bf16[4,16,32,256]{3,2,1,0:T(8,128)(2,1)}), bf16[4,16,32,256]{3,2,1,0:T(8,128)(2,1)S(1)}, u32[]{:S(2)}, u32[]{:S(2)}) %all-to-all-start.4) | async-done | bytes 1048608 | tf_op jit(solution)/shard_map/all_to_all | solution.py:215
  121.1 0.8 shard_map.79
  121.9 6.5 %all-to-all-start.5 = ((bf16[16,32,256]{2,1,0:T(8,128)(2,1)}), bf16[16,32,256]{2,1,0:T(8,128)(2,1)S(1)}, u32[]{:S(2)}, u32[]{:S(2)}) async-start(bf16[16,32,256]{2,1,0:T(8,128)(2,1)} %shard_map.79), calls=%async_computation.5 | async-start | bytes 524288 | tf_op jit(solution)/shard_map/all_to_all | solution.py:226
  128.4 0.0 collective-permute-done.7
  128.4 8.1 %collective-permute-done.8 = bf16[256,896]{1,0:T(8,128)(2,1)S(1)} collective-permute-done((bf16[256,896]{1,0:T(8,128)(2,1)}, bf16[256,896]{1,0:T(8,128)(2,1)S(1)}, u32[]{:S(2)}, u32[]{:S(2)}) %collective-permute-start.8) | collective-permute-done | bytes 458784 | tf_op jit(solution)/shard_map/ppermute | solution.py:224
  136.5 0.0 collective-permute-done.9
  136.5 0.2 broadcast_select_fusion.7
  136.8 1.4 pad_maximum_fusion
  138.1 1.0 all-to-all-done.5
  139.2 0.6 reduce_sum.38
  (7 shorter events, 0.1 us)
Async XLA Ops:
  2.1 20.6 %all-to-all-start = ((bf16[16,32,256]{2,1,0:T(8,128)(2,1)}), bf16[16,32,256]{2,1,0:T(8,128)(2,1)S(1)}, u32[]{:S(2)}, u32[]{:S(2)}) async-start(bf16[16,32,256]{2,1,0:T(8,128)(2,1)} %broadcast_in_dim.6), calls=%async_computation | async-start | bytes 524288 | tf_op jit(solution)/shard_map/all_to_all | solution.py:168
  14.2 15.2 %collective-permute-start = (bf16[256,896]{1,0:T(8,128)(2,1)}, bf16[256,896]{1,0:T(8,128)(2,1)S(1)}, u32[]{:S(2)}, u32[]{:S(2)}) collective-permute-start(bf16[256,896]{1,0:T(8,128)(2,1)} %get-tuple-element.32), channel_id=1, source_target_pairs={{0,32},{16,48},{32,0},{48,16},{64,96},{80,112},{96,64},{112,80},{1... | collective-permute-start | bytes 1376264 | tf_op jit(solution)/shard_map/ppermute | solution.py:158
  17.5 13.0 %collective-permute-start.1 = (bf16[256,896]{1,0:T(8,128)(2,1)S(1)}, bf16[256,896]{1,0:T(8,128)(2,1)S(1)}, u32[]{:S(2)}, u32[]{:S(2)}) collective-permute-start(bf16[256,896]{1,0:T(8,128)(2,1)S(1)} %get-tuple-element.31), channel_id=1, source_target_pairs={{0,64},{16,80},{32,96},{48,112},{64,0},{80,16},{96,32},{112,48},{1... | collective-permute-start | bytes 1376264 | tf_op jit(solution)/shard_map/ppermute | solution.py:158
  20.6 19.3 %collective-permute-start.2 = (bf16[256,896]{1,0:T(8,128)(2,1)}, bf16[256,896]{1,0:T(8,128)(2,1)S(1)}, u32[]{:S(2)}, u32[]{:S(2)}) collective-permute-start(bf16[256,896]{1,0:T(8,128)(2,1)} %get-tuple-element.30), channel_id=1, source_target_pairs={{0,96},{16,112},{32,64},{48,80},{64,32},{80,48},{96,0},{112,16},{1... | collective-permute-start | bytes 1376264 | tf_op jit(solution)/shard_map/ppermute | solution.py:158
  23.8 17.1 %all-to-all-start.1 = ((bf16[4,16,32,256]{3,2,1,0:T(8,128)(2,1)}), bf16[4,16,32,256]{3,2,1,0:T(8,128)(2,1)S(1)}, u32[]{:S(2)}, u32[]{:S(2)}) async-start(bf16[4,16,32,256]{3,2,1,0:T(8,128)(2,1)} %broadcast_in_dim.7), calls=%async_computation.1 | async-start | bytes 2097152 | tf_op jit(solution)/shard_map/all_to_all | solution.py:174
  27.8 2.6 %copy-start.2 = (bf16[256,1792]{1,0:T(8,128)(2,1)S(1)}, bf16[256,1792]{1,0:T(8,128)(2,1)}, u32[]{:S(2)}) copy-start(bf16[256,1792]{1,0:T(8,128)(2,1)} %param.5) | copy-start | bytes 2752516
  27.8 2.6 %copy-start.3 = (bf16[256,1792]{1,0:T(8,128)(2,1)S(1)}, bf16[256,1792]{1,0:T(8,128)(2,1)}, u32[]{:S(2)}) copy-start(bf16[256,1792]{1,0:T(8,128)(2,1)} %param.6) | copy-start | bytes 2752516
  42.2 6.2 %copy-start = (bf16[512,1024]{1,0:T(8,128)(2,1)}, bf16[512,1024]{1,0:T(8,128)(2,1)S(1)}, u32[]{:S(2)}) copy-start(bf16[512,1024]{1,0:T(8,128)(2,1)S(1)} %get-tuple-element.17.tokens) | copy-start | bytes 3145732
  42.2 6.3 %collective-permute-start.3 = (bf16[256,896]{1,0:T(8,128)(2,1)S(1)}, bf16[256,896]{1,0:T(8,128)(2,1)S(1)}, u32[]{:S(2)}, u32[]{:S(2)}) collective-permute-start(bf16[256,896]{1,0:T(8,128)(2,1)S(1)} %get-tuple-element.18), channel_id=1, source_target_pairs={{0,16},{16,0},{32,48},{48,32},{64,80},{80,64},{96,112},{112,96},{1... | collective-permute-start | bytes 1376264 | tf_op jit(solution)/shard_map/ppermute | solution.py:182
  48.4 10.3 %copy-start.4 = (bf16[16,1792]{1,0:T(8,128)(2,1)S(1)}, bf16[16,1792]{1,0:T(8,128)(2,1)}, u32[]{:S(2)}) copy-start(bf16[16,1792]{1,0:T(8,128)(2,1)} %param.7) | copy-start | bytes 172036
  49.4 25.9 %all-to-all-start.2 = ((bf16[8,32,896]{2,1,0:T(8,128)(2,1)}), bf16[8,32,896]{2,1,0:T(8,128)(2,1)S(1)}, u32[]{:S(2)}, u32[]{:S(2)}) async-start(bf16[8,32,896]{2,1,0:T(8,128)(2,1)} %bitcast.3), calls=%async_computation.2 | async-start | bytes 917504 | tf_op jit(solution)/shard_map/all_to_all | solution.py:185
  58.7 4.9 %collective-permute-start.5 = (bf16[16,896]{1,0:T(8,128)(2,1)S(1)}, bf16[16,896]{1,0:T(8,128)(2,1)S(1)}, u32[]{:S(2)}, u32[]{:S(2)}) collective-permute-start(bf16[16,896]{1,0:T(8,128)(2,1)S(1)} %broadcast_select_fusion.12), channel_id=1, source_target_pairs={{0,32},{16,48},{32,0},{48,16},{64,96},{80,112},{96,64},{112,80},{1... | collective-permute-start | bytes 86024 | tf_op jit(solution)/shard_map/ppermute | solution.py:191
  76.2 20.0 %all-to-all-start.3 = ((bf16[8,32,896]{2,1,0:T(8,128)(2,1)}), bf16[8,32,896]{2,1,0:T(8,128)(2,1)S(1)}, u32[]{:S(2)}, u32[]{:S(2)}) async-start(bf16[8,32,896]{2,1,0:T(8,128)(2,1)} %bitcast.8), calls=%async_computation.3 | async-start | bytes 917504 | tf_op jit(solution)/shard_map/all_to_all | solution.py:198
  79.8 4.9 %collective-permute-start.4 = (bf16[16,896]{1,0:T(8,128)(2,1)S(1)}, bf16[16,896]{1,0:T(8,128)(2,1)S(1)}, u32[]{:S(2)}, u32[]{:S(2)}) collective-permute-start(bf16[16,896]{1,0:T(8,128)(2,1)S(1)} %broadcast_select_fusion.16), channel_id=1, source_target_pairs={{0,32},{16,48},{32,0},{48,16},{64,96},{80,112},{96,64},{112,80},{1... | collective-permute-start | bytes 86024 | tf_op jit(solution)/shard_map/ppermute | solution.py:205
  84.7 17.9 %copy-start.5 = (bf16[16,896]{1,0:T(8,128)(2,1)}, bf16[16,896]{1,0:T(8,128)(2,1)S(1)}, u32[]{:S(2)}) copy-start(bf16[16,896]{1,0:T(8,128)(2,1)S(1)} %collective-permute-done.4) | copy-start | bytes 86020
  96.2 3.8 %collective-permute-start.6 = (bf16[256,896]{1,0:T(8,128)(2,1)S(1)}, bf16[256,896]{1,0:T(8,128)(2,1)S(1)}, u32[]{:S(2)}, u32[]{:S(2)}) collective-permute-start(bf16[256,896]{1,0:T(8,128)(2,1)S(1)} %bitcast.32), channel_id=1, source_target_pairs={{0,16},{16,0},{32,48},{48,32},{64,80},{80,64},{96,112},{112,96},{1... | collective-permute-start | bytes 1376264 | tf_op jit(solution)/shard_map/ppermute | solution.py:208
  102.6 3.7 %copy-start.1 = (bf16[512,1024]{1,0:T(8,128)(2,1)S(1)}, bf16[512,1024]{1,0:T(8,128)(2,1)}, u32[]{:S(2)}) copy-start(bf16[512,1024]{1,0:T(8,128)(2,1)} %copy-done) | copy-start | bytes 3145732
  102.6 18.5 %all-to-all-start.4 = ((bf16[4,16,32,256]{3,2,1,0:T(8,128)(2,1)}), bf16[4,16,32,256]{3,2,1,0:T(8,128)(2,1)S(1)}, u32[]{:S(2)}, u32[]{:S(2)}) async-start(bf16[4,16,32,256]{3,2,1,0:T(8,128)(2,1)} %bitcast.10), calls=%async_computation.4 | async-start | bytes 2097152 | tf_op jit(solution)/shard_map/all_to_all | solution.py:215
  106.3 10.8 %copy-start.6 = (bf16[16,896]{1,0:T(8,128)(2,1)S(1)}, bf16[16,896]{1,0:T(8,128)(2,1)}, u32[]{:S(2)}) copy-start(bf16[16,896]{1,0:T(8,128)(2,1)} %copy-done.5) | copy-start | bytes 86020
  108.7 19.7 %collective-permute-start.7 = (bf16[256,896]{1,0:T(8,128)(2,1)}, bf16[256,896]{1,0:T(8,128)(2,1)S(1)}, u32[]{:S(2)}, u32[]{:S(2)}) collective-permute-start(bf16[256,896]{1,0:T(8,128)(2,1)} %get-tuple-element.21), channel_id=1, source_target_pairs={{0,32},{16,48},{32,0},{48,16},{64,96},{80,112},{96,64},{112,80},{1... | collective-permute-start | bytes 1376264 | tf_op jit(solution)/shard_map/ppermute | solution.py:224
  111.8 24.8 %collective-permute-start.8 = (bf16[256,896]{1,0:T(8,128)(2,1)}, bf16[256,896]{1,0:T(8,128)(2,1)S(1)}, u32[]{:S(2)}, u32[]{:S(2)}) collective-permute-start(bf16[256,896]{1,0:T(8,128)(2,1)} %get-tuple-element.22), channel_id=1, source_target_pairs={{0,64},{16,80},{32,96},{48,112},{64,0},{80,16},{96,32},{112,48},{1... | collective-permute-start | bytes 1376264 | tf_op jit(solution)/shard_map/ppermute | solution.py:224
  114.0 22.6 %collective-permute-start.9 = (bf16[256,896]{1,0:T(8,128)(2,1)}, bf16[256,896]{1,0:T(8,128)(2,1)S(1)}, u32[]{:S(2)}, u32[]{:S(2)}) collective-permute-start(bf16[256,896]{1,0:T(8,128)(2,1)} %get-tuple-element.23), channel_id=1, source_target_pairs={{0,96},{16,112},{32,64},{48,80},{64,32},{80,48},{96,0},{112,16},{1... | collective-permute-start | bytes 1376264 | tf_op jit(solution)/shard_map/ppermute | solution.py:224
  121.9 17.3 %all-to-all-start.5 = ((bf16[16,32,256]{2,1,0:T(8,128)(2,1)}), bf16[16,32,256]{2,1,0:T(8,128)(2,1)S(1)}, u32[]{:S(2)}, u32[]{:S(2)}) async-start(bf16[16,32,256]{2,1,0:T(8,128)(2,1)} %shard_map.79), calls=%async_computation.5 | async-start | bytes 524288 | tf_op jit(solution)/shard_map/all_to_all | solution.py:226

commit v7 on v6

--- a/solution.py
+++ b/solution.py
@@ -68,7 +68,7 @@
                 tokens[half:, k * width : (k + 1) * width], w[:, s], preferred_element_type=F32
             )
             total = term if total is None else total + term
-        sent[:, s] = total.astype(BF16)
+        sent[:, s] = total
 
 
 def keep_sums(place, tokens, w0, w1, w2, w3, out):
@@ -177,11 +177,11 @@
     raw = raw.reshape(4, 4, 4, 2, block, width)
 
     tokens, sent = call(
-        arrange_and_send, 6, [struct((2 * count, 4 * width)), struct((count, half))], flops
+        arrange_and_send, 6, [struct((2 * count, 4 * width)), struct((count, half), F32)], flops
     )(place, mark, raw, *weights)
     got = lax.ppermute(sent, "dp", CORE_SWAP)
     kept = call(keep_sums, 5, struct((count, half), F32), flops)(place, tokens, *weights)
-    part = (kept + got.astype(F32)).astype(BF16)
+    part = (kept + got).astype(BF16)
     part = lax.all_to_all(part.reshape(8, 2 * block, half), "dp", 0, 0, axis_index_groups=Z_GROUPS)
     gate_pre = jnp.sum(part[0::2].astype(F32), 0)
     up_pre = jnp.sum(part[1::2].astype(F32), 0)

time: 142 us -> 143 us (level)
  no operation moved by 1% of the time
where the time goes in v7:
time: 143 us; the launch traced here: 140 us
  starting transfers between devices  66.7 us (47%)
  waiting for transfers between devices  54.4 us (38%)
  Pallas kernels  8.36 us (6%)
  other arithmetic  6.7 us (5%)
  local copies, waits for them, and re-layouts  3.4 us (2%)
    ppermute x3, waiting for transfers between devices, per_device(): weights = [lax.ppermute(sends[k], 'dp', QUAD_SWAP[k]) for k in (1, 2, 3)]  11.9 us
    all_to_all x1, waiting for transfers between devices, per_device(): lax.all_to_all(part.reshape(8, 2 * block, half), 'dp', 0, 0, axis_index_g...  11.6 us
    all_to_all x1, waiting for transfers between devices, per_device(): lax.all_to_all(jnp.broadcast_to(jnp.stack([gate_back, up_back])[None], (4...  11.5 us
    all_to_all x1, starting transfers between devices, per_device(): lax.all_to_all(jnp.broadcast_to(activations[None], (16, rows, width)), ('...  9.56 us
    all_to_all x1, starting transfers between devices, per_device(): lax.all_to_all(part.reshape(8, 2 * block, half), 'dp', 0, 0, axis_index_g...  9.3 us
    ppermute x3, starting transfers between devices, per_device(): lax.ppermute(grads[k], 'dp', QUAD_SWAP[k])  8.37 us
    ppermute x3, starting transfers between devices, per_device(): weights = [lax.ppermute(sends[k], 'dp', QUAD_SWAP[k]) for k in (1, 2, 3)]  8.36 us
    ppermute x3, waiting for transfers between devices, per_device(): lax.ppermute(grads[k], 'dp', QUAD_SWAP[k])  8.13 us
  transfers between devices with their start and end apart: 16, of which 13 were waited for; matrix products, arithmetic and copies ran while one was open for 4% of the time, Pallas kernels for 3%

profile of v7, /device:TPU:1, one launch (start us, length us, event | category | flops | bytes accessed | tf_op | source)
XLA Modules:
  0.0 140.5 jit_solution(15381657904964677434)
XLA Ops:
  0.6 1.4 %broadcast_in_dim.6 = bf16[16,32,256]{2,1,0:T(8,128)(2,1)} broadcast(bf16[32,256]{1,0:T(8,128)(2,1)} %param.4), dimensions={1,2} | broadcast | bytes 278528 | tf_op jit(solution)/shard_map/broadcast_in_dim | solution.py:169
  2.1 9.6 %all-to-all-start = ((bf16[16,32,256]{2,1,0:T(8,128)(2,1)}), bf16[16,32,256]{2,1,0:T(8,128)(2,1)S(1)}, u32[]{:S(2)}, u32[]{:S(2)}) async-start(bf16[16,32,256]{2,1,0:T(8,128)(2,1)} %broadcast_in_dim.6), calls=%async_computation | async-start | bytes 524288 | tf_op jit(solution)/shard_map/all_to_all | solution.py:168
  11.7 2.5 %broadcast_select_fusion.10 = (bf16[256,896]{1,0:T(8,128)(2,1)}, bf16[256,896]{1,0:T(8,128)(2,1)S(1)}, bf16[256,896]{1,0:T(8,128)(2,1)}) fusion(pred[]{:T(512)S(6)} %eq.7, bf16[256,1792]{1,0:T(8,128)(2,1)} %param.5, pred[]{:T(512)S(6)} %eq.6, bf16[256,1792]{1,0:T(8,128)(2,1)} %param.6), kind=kLoop, calls=%fused_computation.17 | loop fusion | flops 1605632 | bytes 3211266 | tf_op jit(solution)/shard_map/jit(_where)/select_n | solution.py:145
  14.2 3.2 %collective-permute-start = (bf16[256,896]{1,0:T(8,128)(2,1)}, bf16[256,896]{1,0:T(8,128)(2,1)S(1)}, u32[]{:S(2)}, u32[]{:S(2)}) collective-permute-start(bf16[256,896]{1,0:T(8,128)(2,1)} %get-tuple-element.32), channel_id=1, source_target_pairs={{0,32},{16,48},{32,0},{48,16},{64,96},{80,112},{96,64},{112,80},{1... | collective-permute-start | bytes 1376264 | tf_op jit(solution)/shard_map/ppermute | solution.py:158
  17.5 3.1 %collective-permute-start.1 = (bf16[256,896]{1,0:T(8,128)(2,1)S(1)}, bf16[256,896]{1,0:T(8,128)(2,1)S(1)}, u32[]{:S(2)}, u32[]{:S(2)}) collective-permute-start(bf16[256,896]{1,0:T(8,128)(2,1)S(1)} %get-tuple-element.31), channel_id=1, source_target_pairs={{0,64},{16,80},{32,96},{48,112},{64,0},{80,16},{96,32},{112,48},{1... | collective-permute-start | bytes 1376264 | tf_op jit(solution)/shard_map/ppermute | solution.py:158
  20.6 2.0 %collective-permute-start.2 = (bf16[256,896]{1,0:T(8,128)(2,1)}, bf16[256,896]{1,0:T(8,128)(2,1)S(1)}, u32[]{:S(2)}, u32[]{:S(2)}) collective-permute-start(bf16[256,896]{1,0:T(8,128)(2,1)} %get-tuple-element.30), channel_id=1, source_target_pairs={{0,96},{16,112},{32,64},{48,80},{64,32},{80,48},{96,0},{112,16},{1... | collective-permute-start | bytes 1376264 | tf_op jit(solution)/shard_map/ppermute | solution.py:158
  22.6 0.1 pad_add_fusion.place
  22.7 0.0 all-to-all-done
  22.7 1.1 broadcast_in_dim.7
  23.8 4.0 %all-to-all-start.1 = ((bf16[4,16,32,256]{3,2,1,0:T(8,128)(2,1)}), bf16[4,16,32,256]{3,2,1,0:T(8,128)(2,1)S(1)}, u32[]{:S(2)}, u32[]{:S(2)}) async-start(bf16[4,16,32,256]{3,2,1,0:T(8,128)(2,1)} %broadcast_in_dim.7), calls=%async_computation.1 | async-start | bytes 2097152 | tf_op jit(solution)/shard_map/all_to_all | solution.py:174
  27.8 0.0 copy-start.2
  27.8 0.0 copy-start.3
  27.8 1.6 %collective-permute-done.refs_0_.w1 = bf16[256,896]{1,0:T(8,128)(2,1)S(1)} collective-permute-done((bf16[256,896]{1,0:T(8,128)(2,1)}, bf16[256,896]{1,0:T(8,128)(2,1)S(1)}, u32[]{:S(2)}, u32[]{:S(2)}) %collective-permute-start) | collective-permute-done | bytes 458784 | tf_op jit(solution)/shard_map/ppermute | solution.py:158
  29.5 1.0 collective-permute-done.1.refs_1_.w2
  30.4 0.0 copy-done.2
  30.4 0.0 copy-done.3
  30.4 0.1 select_select_fusion.w0
  30.6 9.3 %collective-permute-done.2.w3 = bf16[256,896]{1,0:T(8,128)(2,1)S(1)} collective-permute-done((bf16[256,896]{1,0:T(8,128)(2,1)}, bf16[256,896]{1,0:T(8,128)(2,1)S(1)}, u32[]{:S(2)}, u32[]{:S(2)}) %collective-permute-start.2) | collective-permute-done | bytes 458784 | tf_op jit(solution)/shard_map/ppermute | solution.py:158
  39.8 1.0 all-to-all-done.1
  40.9 1.3 shard_map.76
  42.2 0.0 copy-start
  42.2 4.9 %collective-permute-start.3 = (f32[256,896]{1,0:T(8,128)S(1)}, f32[256,896]{1,0:T(8,128)S(1)}, u32[]{:S(2)}, u32[]{:S(2)}) collective-permute-start(f32[256,896]{1,0:T(8,128)S(1)} %get-tuple-element.18), channel_id=1, source_target_pairs={{0,16},{16,0},{32,48},{48,32},{64,80},{80,64},{96,112},{112,96},{1... | collective-permute-start | bytes 2752520 | tf_op jit(solution)/shard_map/ppermute | solution.py:182
  47.1 1.3 shard_map.77
  48.4 0.0 copy-done
  48.4 0.0 copy-start.4
  48.4 0.8 collective-permute-done.3
  49.2 0.9 add_convert_fusion
  50.0 9.3 %all-to-all-start.2 = ((bf16[8,32,896]{2,1,0:T(8,128)(2,1)}), bf16[8,32,896]{2,1,0:T(8,128)(2,1)S(1)}, u32[]{:S(2)}, u32[]{:S(2)}) async-start(bf16[8,32,896]{2,1,0:T(8,128)(2,1)} %bitcast.3), calls=%async_computation.2 | async-start | bytes 917504 | tf_op jit(solution)/shard_map/all_to_all | solution.py:185
  59.4 0.0 copy-done.4
  59.4 3.1 %collective-permute-start.5 = (bf16[16,896]{1,0:T(8,128)(2,1)S(1)}, bf16[16,896]{1,0:T(8,128)(2,1)S(1)}, u32[]{:S(2)}, u32[]{:S(2)}) collective-permute-start(bf16[16,896]{1,0:T(8,128)(2,1)S(1)} %broadcast_select_fusion.12), channel_id=1, source_target_pairs={{0,32},{16,48},{32,0},{48,16},{64,96},{80,112},{96,64},{112,80},{1... | collective-permute-start | bytes 86024 | tf_op jit(solution)/shard_map/ppermute | solution.py:191
  62.5 1.8 %collective-permute-done.5 = bf16[16,896]{1,0:T(8,128)(2,1)S(1)} collective-permute-done((bf16[16,896]{1,0:T(8,128)(2,1)S(1)}, bf16[16,896]{1,0:T(8,128)(2,1)S(1)}, u32[]{:S(2)}, u32[]{:S(2)}) %collective-permute-start.5) | collective-permute-done | bytes 28704 | tf_op jit(solution)/shard_map/ppermute | solution.py:191
  64.3 11.6 %all-to-all-done.2 = bf16[8,32,896]{2,1,0:T(8,128)(2,1)S(1)} async-done(((bf16[8,32,896]{2,1,0:T(8,128)(2,1)}), bf16[8,32,896]{2,1,0:T(8,128)(2,1)S(1)}, u32[]{:S(2)}, u32[]{:S(2)}) %all-to-all-start.2) | async-done | bytes 458784 | tf_op jit(solution)/shard_map/all_to_all | solution.py:185
  75.9 0.1 convert_reduce_fusion.1
  76.0 0.1 fusion.2
  76.1 0.8 broadcast_in_dim.8
  76.9 3.5 %all-to-all-start.3 = ((bf16[8,32,896]{2,1,0:T(8,128)(2,1)}), bf16[8,32,896]{2,1,0:T(8,128)(2,1)S(1)}, u32[]{:S(2)}, u32[]{:S(2)}) async-start(bf16[8,32,896]{2,1,0:T(8,128)(2,1)} %bitcast.8), calls=%async_computation.3 | async-start | bytes 917504 | tf_op jit(solution)/shard_map/all_to_all | solution.py:198
  80.4 3.1 %collective-permute-start.4 = (bf16[16,896]{1,0:T(8,128)(2,1)S(1)}, bf16[16,896]{1,0:T(8,128)(2,1)S(1)}, u32[]{:S(2)}, u32[]{:S(2)}) collective-permute-start(bf16[16,896]{1,0:T(8,128)(2,1)S(1)} %broadcast_select_fusion.16), channel_id=1, source_target_pairs={{0,32},{16,48},{32,0},{48,16},{64,96},{80,112},{96,64},{112,80},{1... | collective-permute-start | bytes 86024 | tf_op jit(solution)/shard_map/ppermute | solution.py:205
  83.5 1.8 %collective-permute-done.4 = bf16[16,896]{1,0:T(8,128)(2,1)S(1)} collective-permute-done((bf16[16,896]{1,0:T(8,128)(2,1)S(1)}, bf16[16,896]{1,0:T(8,128)(2,1)S(1)}, u32[]{:S(2)}, u32[]{:S(2)}) %collective-permute-start.4) | collective-permute-done | bytes 28704 | tf_op jit(solution)/shard_map/ppermute | solution.py:205
  85.3 0.0 copy-start.5
  85.3 11.5 %all-to-all-done.3 = bf16[8,32,896]{2,1,0:T(8,128)(2,1)S(1)} async-done(((bf16[8,32,896]{2,1,0:T(8,128)(2,1)}), bf16[8,32,896]{2,1,0:T(8,128)(2,1)S(1)}, u32[]{:S(2)}, u32[]{:S(2)}) %all-to-all-start.3) | async-done | bytes 458784 | tf_op jit(solution)/shard_map/all_to_all | solution.py:198
  96.8 2.4 %collective-permute-start.6 = (bf16[256,896]{1,0:T(8,128)(2,1)S(1)}, bf16[256,896]{1,0:T(8,128)(2,1)S(1)}, u32[]{:S(2)}, u32[]{:S(2)}) collective-permute-start(bf16[256,896]{1,0:T(8,128)(2,1)S(1)} %bitcast.32), channel_id=1, source_target_pairs={{0,16},{16,0},{32,48},{48,32},{64,80},{80,64},{96,112},{112,96},{1... | collective-permute-start | bytes 1376264 | tf_op jit(solution)/shard_map/ppermute | solution.py:208
  99.2 1.4 %collective-permute-done.6.other = bf16[256,896]{1,0:T(8,128)(2,1)S(1)} collective-permute-done((bf16[256,896]{1,0:T(8,128)(2,1)S(1)}, bf16[256,896]{1,0:T(8,128)(2,1)S(1)}, u32[]{:S(2)}, u32[]{:S(2)}) %collective-permute-start.6) | collective-permute-done | bytes 458784 | tf_op jit(solution)/shard_map/ppermute | solution.py:208
  100.6 2.6 %shard_map.78 = bf16[4,4,4,2,16,256]{5,4,3,2,1,0:T(8,128)(2,1)} custom-call(s32[2]{0:T(128)S(1)} %pad_add_fusion.place, bf16[256,896]{1,0:T(8,128)(2,1)S(1)} %bitcast.33, bf16[256,896]{1,0:T(8,128)(2,1)S(1)} %collective-permute-done.6.other, bf16[256,896]{1,0:T(8,128)(2,1)S(1)} %select_select_fusion.w0, ...), custom_call_target="tpu_custom_call" | custom-call | flops 939524096 | bytes 4194304 | tf_op jit(solution)/shard_map/pallas_call | solution.py:212
  103.2 0.0 copy-done.5
  103.2 0.0 copy-start.1
  103.2 3.7 %all-to-all-start.4 = ((bf16[4,16,32,256]{3,2,1,0:T(8,128)(2,1)}), bf16[4,16,32,256]{3,2,1,0:T(8,128)(2,1)S(1)}, u32[]{:S(2)}, u32[]{:S(2)}) async-start(bf16[4,16,32,256]{3,2,1,0:T(8,128)(2,1)} %bitcast.10), calls=%async_computation.4 | async-start | bytes 2097152 | tf_op jit(solution)/shard_map/all_to_all | solution.py:215
  106.9 0.0 copy-done.1
  106.9 0.0 copy-start.6
  106.9 2.4 %shard_map.80 = (bf16[256,896]{1,0:T(8,128)(2,1)S(1)}, bf16[256,896]{1,0:T(8,128)(2,1)}, bf16[256,896]{1,0:T(8,128)(2,1)}, bf16[256,896]{1,0:T(8,128)(2,1)}) custom-call(s32[2]{0:T(128)S(1)} %pad_add_fusion.place, bf16[512,1024]{1,0:T(8,128)(2,1)S(1)} %copy-done.1, bf16[256,896]{1,0:T(8,128)(2,1)S(1)} %bitcast.34, ...), custom_call_target="tpu_custom_call" | custom-call | flops 939524096 | bytes 4194304 | tf_op jit(solution)/shard_map/pallas_call | solution.py:221
  109.3 3.1 %collective-permute-start.7 = (bf16[256,896]{1,0:T(8,128)(2,1)}, bf16[256,896]{1,0:T(8,128)(2,1)S(1)}, u32[]{:S(2)}, u32[]{:S(2)}) collective-permute-start(bf16[256,896]{1,0:T(8,128)(2,1)} %get-tuple-element.21), channel_id=1, source_target_pairs={{0,32},{16,48},{32,0},{48,16},{64,96},{80,112},{96,64},{112,80},{1... | collective-permute-start | bytes 1376264 | tf_op jit(solution)/shard_map/ppermute | solution.py:224
  112.4 2.2 %collective-permute-start.8 = (bf16[256,896]{1,0:T(8,128)(2,1)}, bf16[256,896]{1,0:T(8,128)(2,1)S(1)}, u32[]{:S(2)}, u32[]{:S(2)}) collective-permute-start(bf16[256,896]{1,0:T(8,128)(2,1)} %get-tuple-element.22), channel_id=1, source_target_pairs={{0,64},{16,80},{32,96},{48,112},{64,0},{80,16},{96,32},{112,48},{1... | collective-permute-start | bytes 1376264 | tf_op jit(solution)/shard_map/ppermute | solution.py:224
  114.6 3.1 %collective-permute-start.9 = (bf16[256,896]{1,0:T(8,128)(2,1)}, bf16[256,896]{1,0:T(8,128)(2,1)S(1)}, u32[]{:S(2)}, u32[]{:S(2)}) collective-permute-start(bf16[256,896]{1,0:T(8,128)(2,1)} %get-tuple-element.23), channel_id=1, source_target_pairs={{0,96},{16,112},{32,64},{48,80},{64,32},{80,48},{96,0},{112,16},{1... | collective-permute-start | bytes 1376264 | tf_op jit(solution)/shard_map/ppermute | solution.py:224
  117.7 0.0 copy-done.6
  117.7 0.6 pad_maximum_fusion.3
  118.4 3.3 %all-to-all-done.4.x = bf16[4,16,32,256]{3,2,1,0:T(8,128)(2,1)S(1)} async-done(((bf16[4,16,32,256]{3,2,1,0:T(8,128)(2,1)}), bf16[4,16,32,256]{3,2,1,0:T(8,128)(2,1)S(1)}, u32[]{:S(2)}, u32[]{:S(2)}) %all-to-all-start.4) | async-done | bytes 1048608 | tf_op jit(solution)/shard_map/all_to_all | solution.py:215
  121.7 0.8 shard_map.79
  122.5 6.5 %all-to-all-start.5 = ((bf16[16,32,256]{2,1,0:T(8,128)(2,1)}), bf16[16,32,256]{2,1,0:T(8,128)(2,1)S(1)}, u32[]{:S(2)}, u32[]{:S(2)}) async-start(bf16[16,32,256]{2,1,0:T(8,128)(2,1)} %shard_map.79), calls=%async_computation.5 | async-start | bytes 524288 | tf_op jit(solution)/shard_map/all_to_all | solution.py:226
  129.0 0.0 collective-permute-done.7
  129.0 8.1 %collective-permute-done.8 = bf16[256,896]{1,0:T(8,128)(2,1)S(1)} collective-permute-done((bf16[256,896]{1,0:T(8,128)(2,1)}, bf16[256,896]{1,0:T(8,128)(2,1)S(1)}, u32[]{:S(2)}, u32[]{:S(2)}) %collective-permute-start.8) | collective-permute-done | bytes 458784 | tf_op jit(solution)/shard_map/ppermute | solution.py:224
  137.2 0.0 collective-permute-done.9
  137.2 0.2 broadcast_select_fusion.7
  137.4 1.4 pad_maximum_fusion
  138.8 1.1 all-to-all-done.5
  139.8 0.6 reduce_sum.38
  (7 shorter events, 0.1 us)
Async XLA Ops:
  2.1 20.6 %all-to-all-start = ((bf16[16,32,256]{2,1,0:T(8,128)(2,1)}), bf16[16,32,256]{2,1,0:T(8,128)(2,1)S(1)}, u32[]{:S(2)}, u32[]{:S(2)}) async-start(bf16[16,32,256]{2,1,0:T(8,128)(2,1)} %broadcast_in_dim.6), calls=%async_computation | async-start | bytes 524288 | tf_op jit(solution)/shard_map/all_to_all | solution.py:168
  14.2 15.2 %collective-permute-start = (bf16[256,896]{1,0:T(8,128)(2,1)}, bf16[256,896]{1,0:T(8,128)(2,1)S(1)}, u32[]{:S(2)}, u32[]{:S(2)}) collective-permute-start(bf16[256,896]{1,0:T(8,128)(2,1)} %get-tuple-element.32), channel_id=1, source_target_pairs={{0,32},{16,48},{32,0},{48,16},{64,96},{80,112},{96,64},{112,80},{1... | collective-permute-start | bytes 1376264 | tf_op jit(solution)/shard_map/ppermute | solution.py:158
  17.5 13.0 %collective-permute-start.1 = (bf16[256,896]{1,0:T(8,128)(2,1)S(1)}, bf16[256,896]{1,0:T(8,128)(2,1)S(1)}, u32[]{:S(2)}, u32[]{:S(2)}) collective-permute-start(bf16[256,896]{1,0:T(8,128)(2,1)S(1)} %get-tuple-element.31), channel_id=1, source_target_pairs={{0,64},{16,80},{32,96},{48,112},{64,0},{80,16},{96,32},{112,48},{1... | collective-permute-start | bytes 1376264 | tf_op jit(solution)/shard_map/ppermute | solution.py:158
  20.6 19.3 %collective-permute-start.2 = (bf16[256,896]{1,0:T(8,128)(2,1)}, bf16[256,896]{1,0:T(8,128)(2,1)S(1)}, u32[]{:S(2)}, u32[]{:S(2)}) collective-permute-start(bf16[256,896]{1,0:T(8,128)(2,1)} %get-tuple-element.30), channel_id=1, source_target_pairs={{0,96},{16,112},{32,64},{48,80},{64,32},{80,48},{96,0},{112,16},{1... | collective-permute-start | bytes 1376264 | tf_op jit(solution)/shard_map/ppermute | solution.py:158
  23.8 17.1 %all-to-all-start.1 = ((bf16[4,16,32,256]{3,2,1,0:T(8,128)(2,1)}), bf16[4,16,32,256]{3,2,1,0:T(8,128)(2,1)S(1)}, u32[]{:S(2)}, u32[]{:S(2)}) async-start(bf16[4,16,32,256]{3,2,1,0:T(8,128)(2,1)} %broadcast_in_dim.7), calls=%async_computation.1 | async-start | bytes 2097152 | tf_op jit(solution)/shard_map/all_to_all | solution.py:174
  27.8 2.6 %copy-start.2 = (bf16[256,1792]{1,0:T(8,128)(2,1)S(1)}, bf16[256,1792]{1,0:T(8,128)(2,1)}, u32[]{:S(2)}) copy-start(bf16[256,1792]{1,0:T(8,128)(2,1)} %param.5) | copy-start | bytes 2752516
  27.8 2.6 %copy-start.3 = (bf16[256,1792]{1,0:T(8,128)(2,1)S(1)}, bf16[256,1792]{1,0:T(8,128)(2,1)}, u32[]{:S(2)}) copy-start(bf16[256,1792]{1,0:T(8,128)(2,1)} %param.6) | copy-start | bytes 2752516
  42.2 6.2 %copy-start = (bf16[512,1024]{1,0:T(8,128)(2,1)}, bf16[512,1024]{1,0:T(8,128)(2,1)S(1)}, u32[]{:S(2)}) copy-start(bf16[512,1024]{1,0:T(8,128)(2,1)S(1)} %get-tuple-element.17.tokens) | copy-start | bytes 3145732
  42.2 7.0 %collective-permute-start.3 = (f32[256,896]{1,0:T(8,128)S(1)}, f32[256,896]{1,0:T(8,128)S(1)}, u32[]{:S(2)}, u32[]{:S(2)}) collective-permute-start(f32[256,896]{1,0:T(8,128)S(1)} %get-tuple-element.18), channel_id=1, source_target_pairs={{0,16},{16,0},{32,48},{48,32},{64,80},{80,64},{96,112},{112,96},{1... | collective-permute-start | bytes 2752520 | tf_op jit(solution)/shard_map/ppermute | solution.py:182
  48.4 11.0 %copy-start.4 = (bf16[16,1792]{1,0:T(8,128)(2,1)S(1)}, bf16[16,1792]{1,0:T(8,128)(2,1)}, u32[]{:S(2)}) copy-start(bf16[16,1792]{1,0:T(8,128)(2,1)} %param.7) | copy-start | bytes 172036
  50.0 25.9 %all-to-all-start.2 = ((bf16[8,32,896]{2,1,0:T(8,128)(2,1)}), bf16[8,32,896]{2,1,0:T(8,128)(2,1)S(1)}, u32[]{:S(2)}, u32[]{:S(2)}) async-start(bf16[8,32,896]{2,1,0:T(8,128)(2,1)} %bitcast.3), calls=%async_computation.2 | async-start | bytes 917504 | tf_op jit(solution)/shard_map/all_to_all | solution.py:185
  59.4 4.9 %collective-permute-start.5 = (bf16[16,896]{1,0:T(8,128)(2,1)S(1)}, bf16[16,896]{1,0:T(8,128)(2,1)S(1)}, u32[]{:S(2)}, u32[]{:S(2)}) collective-permute-start(bf16[16,896]{1,0:T(8,128)(2,1)S(1)} %broadcast_select_fusion.12), channel_id=1, source_target_pairs={{0,32},{16,48},{32,0},{48,16},{64,96},{80,112},{96,64},{112,80},{1... | collective-permute-start | bytes 86024 | tf_op jit(solution)/shard_map/ppermute | solution.py:191
  76.9 20.0 %all-to-all-start.3 = ((bf16[8,32,896]{2,1,0:T(8,128)(2,1)}), bf16[8,32,896]{2,1,0:T(8,128)(2,1)S(1)}, u32[]{:S(2)}, u32[]{:S(2)}) async-start(bf16[8,32,896]{2,1,0:T(8,128)(2,1)} %bitcast.8), calls=%async_computation.3 | async-start | bytes 917504 | tf_op jit(solution)/shard_map/all_to_all | solution.py:198
  80.4 4.9 %collective-permute-start.4 = (bf16[16,896]{1,0:T(8,128)(2,1)S(1)}, bf16[16,896]{1,0:T(8,128)(2,1)S(1)}, u32[]{:S(2)}, u32[]{:S(2)}) collective-permute-start(bf16[16,896]{1,0:T(8,128)(2,1)S(1)} %broadcast_select_fusion.16), channel_id=1, source_target_pairs={{0,32},{16,48},{32,0},{48,16},{64,96},{80,112},{96,64},{112,80},{1... | collective-permute-start | bytes 86024 | tf_op jit(solution)/shard_map/ppermute | solution.py:205
  85.3 17.9 %copy-start.5 = (bf16[16,896]{1,0:T(8,128)(2,1)}, bf16[16,896]{1,0:T(8,128)(2,1)S(1)}, u32[]{:S(2)}) copy-start(bf16[16,896]{1,0:T(8,128)(2,1)S(1)} %collective-permute-done.4) | copy-start | bytes 86020
  96.8 3.8 %collective-permute-start.6 = (bf16[256,896]{1,0:T(8,128)(2,1)S(1)}, bf16[256,896]{1,0:T(8,128)(2,1)S(1)}, u32[]{:S(2)}, u32[]{:S(2)}) collective-permute-start(bf16[256,896]{1,0:T(8,128)(2,1)S(1)} %bitcast.32), channel_id=1, source_target_pairs={{0,16},{16,0},{32,48},{48,32},{64,80},{80,64},{96,112},{112,96},{1... | collective-permute-start | bytes 1376264 | tf_op jit(solution)/shard_map/ppermute | solution.py:208
  103.2 3.7 %copy-start.1 = (bf16[512,1024]{1,0:T(8,128)(2,1)S(1)}, bf16[512,1024]{1,0:T(8,128)(2,1)}, u32[]{:S(2)}) copy-start(bf16[512,1024]{1,0:T(8,128)(2,1)} %copy-done) | copy-start | bytes 3145732
  103.2 18.5 %all-to-all-start.4 = ((bf16[4,16,32,256]{3,2,1,0:T(8,128)(2,1)}), bf16[4,16,32,256]{3,2,1,0:T(8,128)(2,1)S(1)}, u32[]{:S(2)}, u32[]{:S(2)}) async-start(bf16[4,16,32,256]{3,2,1,0:T(8,128)(2,1)} %bitcast.10), calls=%async_computation.4 | async-start | bytes 2097152 | tf_op jit(solution)/shard_map/all_to_all | solution.py:215
  106.9 10.8 %copy-start.6 = (bf16[16,896]{1,0:T(8,128)(2,1)S(1)}, bf16[16,896]{1,0:T(8,128)(2,1)}, u32[]{:S(2)}) copy-start(bf16[16,896]{1,0:T(8,128)(2,1)} %copy-done.5) | copy-start | bytes 86020
  109.3 19.7 %collective-permute-start.7 = (bf16[256,896]{1,0:T(8,128)(2,1)}, bf16[256,896]{1,0:T(8,128)(2,1)S(1)}, u32[]{:S(2)}, u32[]{:S(2)}) collective-permute-start(bf16[256,896]{1,0:T(8,128)(2,1)} %get-tuple-element.21), channel_id=1, source_target_pairs={{0,32},{16,48},{32,0},{48,16},{64,96},{80,112},{96,64},{112,80},{1... | collective-permute-start | bytes 1376264 | tf_op jit(solution)/shard_map/ppermute | solution.py:224
  112.4 24.8 %collective-permute-start.8 = (bf16[256,896]{1,0:T(8,128)(2,1)}, bf16[256,896]{1,0:T(8,128)(2,1)S(1)}, u32[]{:S(2)}, u32[]{:S(2)}) collective-permute-start(bf16[256,896]{1,0:T(8,128)(2,1)} %get-tuple-element.22), channel_id=1, source_target_pairs={{0,64},{16,80},{32,96},{48,112},{64,0},{80,16},{96,32},{112,48},{1... | collective-permute-start | bytes 1376264 | tf_op jit(solution)/shard_map/ppermute | solution.py:224
  114.6 22.5 %collective-permute-start.9 = (bf16[256,896]{1,0:T(8,128)(2,1)}, bf16[256,896]{1,0:T(8,128)(2,1)S(1)}, u32[]{:S(2)}, u32[]{:S(2)}) collective-permute-start(bf16[256,896]{1,0:T(8,128)(2,1)} %get-tuple-element.23), channel_id=1, source_target_pairs={{0,96},{16,112},{32,64},{48,80},{64,32},{80,48},{96,0},{112,16},{1... | collective-permute-start | bytes 1376264 | tf_op jit(solution)/shard_map/ppermute | solution.py:224
  122.5 17.3 %all-to-all-start.5 = ((bf16[16,32,256]{2,1,0:T(8,128)(2,1)}), bf16[16,32,256]{2,1,0:T(8,128)(2,1)S(1)}, u32[]{:S(2)}, u32[]{:S(2)}) async-start(bf16[16,32,256]{2,1,0:T(8,128)(2,1)} %shard_map.79), calls=%async_computation.5 | async-start | bytes 524288 | tf_op jit(solution)/shard_map/all_to_all | solution.py:226
